TPU v7x, 128 devices: a whole 4x4x4 slice. The times are simulated.
128 devices in a mesh: dp: 32 (over z, x_hi, y), mp: 4 (over x_lo, core).
Axes of the slice: x: 4 (x_hi: 2, x_lo: 2; x = x_hi * 2 + x_lo), y: 4, z: 4, core: 2. Of those that a mesh axis runs over, the one named last changes fastest.
Arguments:
- vit_partial: bfloat16 [4, 16384, 6144], P('mp', 'dp'), may hold values from -6 to 6
- vit_residual: bfloat16 [16384, 6144], P(('dp', 'mp')), may hold values from -6 to 6
- ln_gain: float32 [6144], replicated, may hold values from 0.5 to 1.5
- key_weight: bfloat16 [6144, 2048], P(None, 'mp'), may hold values from -0.078125 to 0.078125
- value_weight: bfloat16 [6144, 2048], P(None, 'mp'), may hold values from -0.078125 to 0.078125
- queries: bfloat16 [64, 512, 2048], P('dp', None, 'mp'), may hold values from -16 to 16
- context_grad: bfloat16 [64, 512, 2048], P('dp', None, 'mp'), may hold values from -6 to 6
- text_len: int32 [64], P('dp'), may hold values from 1 to 512
- image_pick: int32 [32, 2], P('dp'), may hold values from 0 to 1, each once within a row
Outputs:
- context: float32 [64, 512, 2048], P('dp', None, 'mp')
- query_grad: float32 [64, 512, 2048], P('dp', None, 'mp')
- key_weight_grad: float32 [6144, 2048], P('dp', 'mp')
- value_weight_grad: float32 [6144, 2048], P('dp', 'mp')
- stream_grad: float32 [16384, 6144], P(('dp', 'mp'))
All inputs are finite; a program needn't handle non-finite values.
Results may differ from a plain program's by a relative error of at most 0.034.
Values may be sent and summed in bfloat16 or wider, within the bound.
No kernel may reach another device: no remote copies, remote signals or barrier semaphores. Data moves between devices by JAX's collectives and lax.ppermute only.
A program may use at most 192 MiB of HBM per device.

v0:
```python
import functools

import jax
import jax.numpy as jnp
from jax import lax
from jax.experimental import pallas as pl
from jax.experimental.pallas import tpu as pltpu
from jax.sharding import Mesh, PartitionSpec as P

HD = 256
RING = 4
BF = jnp.bfloat16
F32 = jnp.float32
SWAP = [(0, 1), (1, 0)]
MIB = 1024 * 1024
LANES = 512
CUTS = 4
ANYWHERE = pl.BlockSpec(memory_space=pl.ANY)


def dot(left, right, dims=((1,), (0,))):
    return lax.dot_general(left, right, (dims, ((), ())), preferred_element_type=F32)


def shape(dims, kind=BF):
    return jax.ShapeDtypeStruct(dims, kind)


def cost(flops, moved, special=0):
    return pl.CostEstimate(flops=flops, bytes_accessed=moved, transcendentals=special)


def call(body, grid, scalars, ins, in_specs, outs, out_specs, scratch=(), after=(), mib=20, **more):
    count, waits = len(scalars) + len(ins), len(after)

    def with_waits(*refs):
        body(*refs[:count], *refs[count + waits :])

    return pl.pallas_call(
        with_waits,
        grid_spec=pltpu.PrefetchScalarGridSpec(
            num_scalar_prefetch=len(scalars),
            grid=grid,
            in_specs=list(in_specs) + [ANYWHERE] * waits,
            out_specs=out_specs,
            scratch_shapes=scratch,
        ),
        out_shape=outs,
        compiler_params=pltpu.CompilerParams(vmem_limit_bytes=mib * MIB),
        **more,
    )(*scalars, *ins, *after)


def part_of_body(image, where_ref, part_in, share_in, out, hold, load_sems, store_sems):
    rows = out.shape[0]
    step = rows // 4
    start = (image * 2 + 1 - where_ref[0]) * rows

    def load(n):
        source = part_in.at[0, pl.ds(pl.multiple_of(start + n * step, step), step)]
        return pltpu.make_async_copy(source, hold.at[pl.ds(n * step, step)], load_sems.at[n])

    def store(n):
        at = pl.ds(n * step, step)
        return pltpu.make_async_copy(hold.at[at], out.at[at], store_sems.at[n])

    for n in range(4):
        load(n).start()
    for n in range(4):
        load(n).wait()
        store(n).start()
    for n in range(4):
        store(n).wait()


def part_of(image, where, vit_partial, vit_residual, after):
    return call(
        functools.partial(part_of_body, image),
        (1,),
        [where],
        [vit_partial, vit_residual],
        [ANYWHERE] * 2,
        shape(vit_residual.shape),
        ANYWHERE,
        scratch=[
            pltpu.VMEM(vit_residual.shape, BF),
            pltpu.SemaphoreType.DMA((4,)),
            pltpu.SemaphoreType.DMA((4,)),
        ],
        after=after,
        mib=60,
    )


def lanes(width):
    return [slice(start, start + LANES) for start in range(0, width, LANES)]


def chip_sum_body(image, where_ref, part_ref, theirs_ref, residual_ref, out_ref):
    scale = jnp.where(where_ref[1] == image, 1.0, 0.0)
    for at in lanes(out_ref.shape[1]):
        total = part_ref[0, :, at].astype(F32) + theirs_ref[:, at].astype(F32)
        out_ref[:, at] = (total + scale * residual_ref[:, at].astype(F32)).astype(BF)


def chip_sum(image, where, vit_partial, theirs, residual):
    rows, width = residual.shape
    step = rows // 4
    plain = pl.BlockSpec((step, width), lambda i, where_ref: (i, 0))
    return call(
        functools.partial(chip_sum_body, image),
        (4,),
        [where],
        [vit_partial, theirs, residual],
        [
            pl.BlockSpec(
                (1, step, width), lambda i, where_ref: (0, (image * 2 + where_ref[0]) * 4 + i, 0)
            ),
            plain,
            plain,
        ],
        shape((rows, width)),
        plain,
        cost_estimate=cost(0, 8 * rows * width),
    )


def centre_rows(first_ref, second_ref, hold_ref, rows):
    width = hold_ref.shape[1]
    total = 0.0
    for at in lanes(width):
        stream = first_ref[rows, at].astype(F32) + second_ref[rows, at].astype(F32)
        hold_ref[rows, at] = stream
        total = total + stream
    row_mean = jnp.sum(total, axis=-1, keepdims=True) * (1.0 / width)
    total = 0.0
    for at in lanes(width):
        centred = hold_ref[rows, at] - row_mean
        hold_ref[rows, at] = centred
        total = total + centred * centred
    return lax.rsqrt(jnp.sum(total, axis=-1, keepdims=True) * (1.0 / width) + 1e-06)


def norm_body(mine_ref, other_ref, gain_ref, out_ref, hold_ref):
    rows = slice(None)
    inv_std = centre_rows(mine_ref, other_ref, hold_ref, rows)
    for at in lanes(out_ref.shape[1]):
        out_ref[:, at] = (hold_ref[:, at] * inv_std * gain_ref[:, at]).astype(BF)


def norm(mine, other, gain, after):
    rows, width = mine.shape
    plain = pl.BlockSpec((rows // 4, width), lambda i: (i, 0))
    return call(
        norm_body,
        (4,),
        [],
        [mine, other, gain],
        [plain, plain, pl.BlockSpec((1, width), lambda i: (0, 0))],
        shape((rows, width)),
        plain,
        scratch=[pltpu.VMEM((rows // 4, width), F32)],
        after=after,
        cost_estimate=cost(0, 6 * rows * width),
    )


def norm_back_body(where_ref, gain_ref, *refs):
    first, second = refs[:4], refs[4:8]
    out, held, hold, result, load_sems, store_sems = refs[8:]
    width = hold.shape[1]
    rows = held.shape[1] // 4

    def loads(n, group):
        at = pl.ds(n * rows, rows)
        return [
            pltpu.make_async_copy(source.at[at], held.at[j, at], load_sems.at[j, n])
            for j, source in enumerate(group)
        ]

    for side, group in enumerate((first, second)):

        @pl.when(where_ref[1] == side)
        def _(group=group):
            for n in range(4):
                for copy in loads(n, group):
                    copy.start()

    stores = []
    for n in range(4):
        for copy in loads(n, first):
            copy.wait()
        part = slice(n * rows, (n + 1) * rows)
        inv_std = centre_rows(held.at[0], held.at[1], hold, part)
        sum_grad = sum_proj = 0.0
        for at in lanes(width):
            scaled = held[2, part, at].astype(F32) + held[3, part, at].astype(F32)
            scaled = scaled * gain_ref[:, at]
            result[part, at] = scaled
            sum_grad = sum_grad + scaled
            sum_proj = sum_proj + scaled * hold[part, at]
        mean_grad = jnp.sum(sum_grad, axis=-1, keepdims=True) * (1.0 / width)
        mean_proj = jnp.sum(sum_proj, axis=-1, keepdims=True) * inv_std * (1.0 / width)
        for at in lanes(width):
            normal_rows = hold[part, at] * inv_std
            result[part, at] = inv_std * (result[part, at] - mean_grad - normal_rows * mean_proj)
        at = pl.ds(n * rows, rows)
        stores.append(pltpu.make_async_copy(result.at[at], out.at[at], store_sems.at[n]))
        stores[n].start()
    for copy in stores:
        copy.wait()


def norm_back(where, gain, first, second):
    rows, width = first[0].shape
    return call(
        norm_back_body,
        (1,),
        [where],
        [gain, *first, *second],
        [pl.BlockSpec((1, width), lambda i, where_ref: (0, 0))] + [ANYWHERE] * 8,
        shape((rows, width), F32),
        ANYWHERE,
        scratch=[
            pltpu.VMEM((4, rows, width), BF),
            pltpu.VMEM((rows, width), F32),
            pltpu.VMEM((rows, width), F32),
            pltpu.SemaphoreType.DMA((4, 4)),
            pltpu.SemaphoreType.DMA((4,)),
        ],
        mib=56,
        cost_estimate=cost(0, 12 * rows * width),
    )


def ring_sum_body(where_ref, *refs):
    *blocks, kept_ref, sent_ref = refs
    rows = kept_ref.shape[0]

    def total(block):
        at = pl.ds(pl.multiple_of(block * rows, rows), rows)
        return sum(ref[at].astype(F32) for ref in blocks)

    sent_ref[...] = total(1 - where_ref[4]).astype(BF)
    kept_ref[...] = total(where_ref[4])


def ring_sum(where, blocks, after):
    rows, width = blocks[0].shape
    whole = pl.BlockSpec((rows, width), lambda i, where_ref: (0, 0))
    half = pl.BlockSpec((rows // 2, width), lambda i, where_ref: (0, 0))
    return call(
        ring_sum_body,
        (1,),
        [where],
        blocks,
        [whole] * len(blocks),
        [shape((rows // 2, width), F32), shape((rows // 2, width))],
        [half, half],
        after=after,
        cost_estimate=cost(0, 12 * rows * width),
    )


def last_sum_body(kept_ref, got_ref, key_ref, value_ref):
    total = kept_ref[...] + got_ref[...].astype(F32)
    width = key_ref.shape[1]
    key_ref[...] = total[:, :width]
    value_ref[...] = total[:, width:]


def last_sum(kept, got, after):
    rows, width = kept.shape
    whole = pl.BlockSpec((rows, width), lambda i: (0, 0))
    half = pl.BlockSpec((rows, width // 2), lambda i: (0, 0))
    return call(
        last_sum_body,
        (1,),
        [],
        [kept, got],
        [whole, whole],
        [shape((rows, width // 2), F32)] * 2,
        [half, half],
        after=after,
        cost_estimate=cost(0, 10 * rows * width),
    )


def strips_body(where_ref, own_in, far_in, *rest):
    outs = rest[:RING]
    own_ref, far_ref, hold, load_sems, store_sems = rest[RING:]
    total_rows, width = own_ref.shape
    step = total_rows // 4
    piece = width // (2 * RING * RING)
    refs = (own_ref, far_ref)

    def load(n, half):
        at = pl.ds(n * step, step)
        source = (own_in, far_in)[half]
        return pltpu.make_async_copy(source.at[at], refs[half].at[at], load_sems.at[half, n])

    def store(n, k):
        at = pl.ds(n * step, step)
        source = hold.at[lax.rem(where_ref[2] + k, RING)]
        return pltpu.make_async_copy(source.at[:, at], outs[k].at[:, at], store_sems.at[k, n])

    def fill(n, along_y):
        at = slice(n * step, (n + 1) * step)
        for half in range(2):
            for a in range(RING):
                for b in range(RING):
                    for x in range(2):
                        z, y = (b, a) if along_y else (a, b)
                        start = ((z * 2 + x) * RING + y) * piece
                        spot = (b * 2 + x) * piece
                        hold[a, half, at, spot : spot + piece] = refs[half][at, start : start + piece]

    for n in range(4):
        for half in range(2):
            load(n, half).start()
    for n in range(4):
        for half in range(2):
            load(n, half).wait()
        pl.when(where_ref[0] == 0)(functools.partial(fill, n, True))
        pl.when(where_ref[0] == 1)(functools.partial(fill, n, False))
        for k in range(RING):
            store(n, k).start()
    for n in range(4):
        for k in range(RING):
            store(n, k).wait()


def strips(where, own, far, after):
    rows, width = own.shape
    part = width // RING
    return call(
        strips_body,
        (1,),
        [where],
        [own, far],
        [ANYWHERE] * 2,
        [shape((2, rows, part))] * RING,
        [ANYWHERE] * RING,
        scratch=[
            pltpu.VMEM((rows, width), BF),
            pltpu.VMEM((rows, width), BF),
            pltpu.VMEM((RING, 2, rows, part), BF),
            pltpu.SemaphoreType.DMA((2, 4)),
            pltpu.SemaphoreType.DMA((RING, 4)),
        ],
        after=after,
        cost_estimate=cost(0, 8 * rows * width),
    )


def image_body(image, pick_ref, len_ref, own_in, far_in, key_in, value_in, q_in, g_in, *rest):
    context_out, query_grad_out, near_out, away_out, grads_ref = rest[-19:-14]
    rows, keys, values, total, q_ref, g_ref, context_ref, query_grad_ref, back = rest[-14:-5]
    row_sems, weight_sems, text_sems, back_sems, done_sems = rest[-5:]
    half = rows.shape[0] // 2
    chunk = keys.shape[0] // CUTS
    width = keys.shape[1]
    example = pick_ref[image]
    limit = len_ref[example]

    def at(n):
        return pl.ds(pl.multiple_of(n * chunk, chunk), chunk)

    def row_loads(n):
        return [
            pltpu.make_async_copy(own_in.at[:, at(n)], rows.at[:half, at(n)], row_sems.at[0, n]),
            pltpu.make_async_copy(far_in.at[:, at(n)], rows.at[half:, at(n)], row_sems.at[1, n]),
        ]

    def weight_loads(n):
        return [
            pltpu.make_async_copy(key_in.at[at(n)], keys.at[at(n)], weight_sems.at[0, n]),
            pltpu.make_async_copy(value_in.at[at(n)], values.at[at(n)], weight_sems.at[1, n]),
        ]

    def back_stores(n):
        return [
            pltpu.make_async_copy(back.at[:half, at(n)], near_out.at[:, at(n)], back_sems.at[0, n]),
            pltpu.make_async_copy(back.at[half:, at(n)], away_out.at[:, at(n)], back_sems.at[1, n]),
        ]

    text_loads = [
        pltpu.make_async_copy(q_in.at[example], q_ref, text_sems.at[0]),
        pltpu.make_async_copy(g_in.at[example], g_ref, text_sems.at[1]),
    ]
    text_stores = [
        pltpu.make_async_copy(context_ref, context_out.at[example], done_sems.at[0]),
        pltpu.make_async_copy(query_grad_ref, query_grad_out.at[example], done_sems.at[1]),
    ]

    @pl.loop(0, CUTS)
    def _(n):
        for copy in row_loads(n) + weight_loads(n):
            copy.start()

    for copy in text_loads:
        copy.start()
    total[...] = jnp.zeros_like(total)

    @pl.loop(0, CUTS)
    def _(n):
        for copy in row_loads(n) + weight_loads(n):
            copy.wait()
        left = rows[:, at(n)]
        total[:, :width] += dot(left, keys[at(n)])
        total[:, width:] += dot(left, values[at(n)])

    for copy in text_loads:
        copy.wait()
    mask = lax.broadcasted_iota(jnp.int32, (q_ref.shape[0], 1), 0) < limit
    for head in range(width // HD):
        key_at = slice(head * HD, (head + 1) * HD)
        value_at = slice(width + head * HD, width + (head + 1) * HD)
        key, value = total[:, key_at].astype(BF), total[:, value_at].astype(BF)
        q = q_ref[:, key_at]
        scores = dot(q, key, ((1,), (1,))) * HD ** (-0.5)
        exp_terms = jnp.exp(scores - jnp.max(scores, axis=-1, keepdims=True))
        softmax_w = exp_terms / jnp.sum(exp_terms, axis=-1, keepdims=True)
        weights_bf = softmax_w.astype(BF)
        context_ref[:, key_at] = jnp.where(mask, dot(weights_bf, value), 0.0)
        upstream = jnp.where(mask, g_ref[:, key_at].astype(F32), 0.0).astype(BF)
        weight_grad = dot(upstream, value, ((1,), (1,)))
        centre = jnp.sum(weight_grad * softmax_w, axis=-1, keepdims=True)
        score_grad = (softmax_w * (weight_grad - centre) * HD ** (-0.5)).astype(BF)
        query_grad_ref[:, key_at] = dot(score_grad, key)
        grads_ref[:, key_at] = dot(score_grad, q, ((0,), (0,))).astype(BF)
        grads_ref[:, value_at] = dot(weights_bf, upstream, ((0,), (0,))).astype(BF)
    for copy in text_stores:
        copy.start()

    @pl.loop(0, CUTS)
    def _(n):
        term = dot(grads_ref[:, :width], keys[at(n)], ((1,), (1,)))
        term = term + dot(grads_ref[:, width:], values[at(n)], ((1,), (1,)))
        back[:, at(n)] = term.astype(BF)
        for copy in back_stores(n):
            copy.start()

    @pl.loop(0, CUTS)
    def _(n):
        for copy in back_stores(n):
            copy.wait()

    for copy in text_stores:
        copy.wait()


def image_step(
    image, pick, text_len, own, far, key_weight, value_weight, queries, context_grad, partly, after
):
    text_rows, width = queries.shape[1:]
    half, depth = own.shape
    flat = (2 * half, 2 * width)
    sems = pltpu.SemaphoreType.DMA
    return call(
        functools.partial(image_body, image),
        (1,),
        [pick, text_len],
        [own, far, key_weight, value_weight, queries, context_grad, *partly],
        [ANYWHERE] * (6 + len(partly)),
        [shape(queries.shape, F32)] * 2 + [shape(own.shape)] * 2 + [shape(flat)],
        [ANYWHERE] * 4 + [pl.BlockSpec(flat, lambda i, *scalars: (0, 0))],
        scratch=[
            pltpu.VMEM((2 * half, depth), BF),
            pltpu.VMEM(key_weight.shape, BF),
            pltpu.VMEM(key_weight.shape, BF),
            pltpu.VMEM(flat, F32),
            pltpu.VMEM((text_rows, width), BF),
            pltpu.VMEM((text_rows, width), BF),
            pltpu.VMEM((text_rows, width), F32),
            pltpu.VMEM((text_rows, width), F32),
            pltpu.VMEM((2 * half, depth), BF),
            sems((2, CUTS)),
            sems((2, CUTS)),
            sems((2,)),
            sems((2, CUTS)),
            sems((2,)),
        ],
        after=after,
        input_output_aliases={8: 0, 9: 1} if partly else {},
        mib=44,
        cost_estimate=cost(
            16 * half * depth * width + 24 * text_rows * half * width,
            4 * depth * (2 * half + width) + 12 * text_rows * width,
            2 * text_rows * half * width // HD,
        ),
    )


def weight_grad_body(first, pieces, where_ref, *refs):
    lefts_in, rights_in, rest = refs[:RING], refs[RING : RING + pieces], refs[RING + pieces :]
    left, right, result, left_sems, right_sems, store_sems = rest[-6:]
    outs = rest[:1] if first else rest[1:-6]
    rows = right.shape[0] // RING
    chunk, width = result.shape[1:]
    half = rows // 2
    wide = width // 2

    def right_loads():
        start = 0
        for k, source in enumerate(rights_in):
            target = right.at[pl.ds(start, source.shape[0])]
            start += source.shape[0]
            yield pltpu.make_async_copy(source, target, right_sems.at[k])

    def left_load(n, k, h):
        columns = pl.ds(pl.multiple_of(lax.rem(where_ref[3] + n, RING) * chunk, chunk), chunk)
        at = pl.ds(k * rows + h * half, half)
        source = lefts_in[k].at[h, :, columns]
        return pltpu.make_async_copy(source, left.at[n, at], left_sems.at[n, k, h])

    def stores(n):
        if first:
            return [pltpu.make_async_copy(result.at[n], outs[0].at[n], store_sems.at[n])]
        if n != 2:
            target = outs[(0, 1, None, 4)[n]]
            return [pltpu.make_async_copy(result.at[n], target, store_sems.at[n])]
        cut = chunk // 2
        top, bottom = pl.ds(0, cut), pl.ds(cut, cut)
        return [
            pltpu.make_async_copy(result.at[n, top], outs[2], store_sems.at[n]),
            pltpu.make_async_copy(result.at[n, bottom], outs[3], store_sems.at[RING]),
        ]

    each = [(k, h) for k in range(RING) for h in range(2)]
    order = (2, 1, 3, 0)
    for copy in right_loads():
        copy.start()
    for n in order:
        for k, h in each:
            left_load(n, k, h).start()
    for copy in right_loads():
        copy.wait()
    for n in order:
        for k, h in each:
            left_load(n, k, h).wait()
        for columns in (slice(0, wide), slice(wide, width)):
            total = dot(left[n], right[:, columns], ((0,), (0,)))
            if not first:
                total = total + rest[0][n, :, columns].astype(F32)
            result[n, :, columns] = total.astype(BF)
        for copy in stores(n):
            copy.start()
    for n in order:
        for copy in stores(n):
            copy.wait()


def weight_grad(where, lefts, rights, so_far=None, after=()):
    halves, rows, part = lefts[0].shape
    width = rights[0].shape[1]
    chunk, pieces = part // RING, len(rights)
    first = so_far is None
    whole = (RING, chunk, width)
    heights = [chunk, chunk, chunk // 2, chunk // 2, chunk]
    outs = [shape(whole)] if first else [shape((height, width)) for height in heights]
    return call(
        functools.partial(weight_grad_body, first, pieces),
        (1,),
        [where],
        [*lefts, *rights] + ([] if first else [so_far]),
        [ANYWHERE] * (RING + pieces)
        + ([] if first else [pl.BlockSpec(whole, lambda i, where_ref: (0, 0, 0))]),
        outs,
        [ANYWHERE] * len(outs),
        scratch=[
            pltpu.VMEM((RING, RING * halves * rows, chunk), BF),
            pltpu.VMEM((RING * halves * rows, width), BF),
            pltpu.VMEM(whole, BF),
            pltpu.SemaphoreType.DMA((RING, RING, 2)),
            pltpu.SemaphoreType.DMA((pieces,)),
            pltpu.SemaphoreType.DMA((RING + 1,)),
        ],
        after=after,
        cost_estimate=cost(0, 0),
        mib=56 if first else 20,
    )


def relay_body(up_ref, got_up_ref, down_ref, got_down_ref, up_out, down_out):
    cut = got_up_ref.shape[0]
    up_out[:cut] = (up_ref[:cut].astype(F32) + got_up_ref[...].astype(F32)).astype(BF)
    up_out[cut:] = up_ref[cut:]
    down_out[:cut] = down_ref[:cut]
    down_out[cut:] = (down_ref[cut:].astype(F32) + got_down_ref[...].astype(F32)).astype(BF)


def relay(up, got_up, down, got_down):
    whole = pl.BlockSpec(up.shape, lambda i: (0, 0))
    half = pl.BlockSpec(got_up.shape, lambda i: (0, 0))
    return call(
        relay_body,
        (1,),
        [],
        [up, got_up, down, got_down],
        [whole, half, whole, half],
        [shape(up.shape)] * 2,
        [whole, whole],
        cost_estimate=cost(0, 0),
    )


def later(array, after):
    return call(
        lambda *refs: None,
        (1,),
        [],
        [array],
        [ANYWHERE],
        shape(array.shape, array.dtype),
        ANYWHERE,
        after=after,
        input_output_aliases={0: 0},
    )


def hop(first, distance):
    pairs = []
    for z in range(RING):
        for y in range(RING):
            for core in range(2):
                along_y = (core == 0) == first
                to = (z, (y + distance) % RING) if along_y else ((z + distance) % RING, y)
                pairs.append(((z * RING + y) * 2 + core, (to[0] * RING + to[1]) * 2 + core))
    return pairs


def rotate(array, first, distance):
    return lax.ppermute(array, ("z", "y", "c"), hop(first, distance))


def local(
    vit_partial,
    vit_residual,
    ln_gain,
    key_weight,
    value_weight,
    queries,
    context_grad,
    text_len,
    image_pick,
):
    share, model_width = vit_residual.shape
    width = key_weight.shape[1]
    core, side, cross = lax.axis_index("c"), lax.axis_index("xl"), lax.axis_index("xh")
    y, z = lax.axis_index("y"), lax.axis_index("z")
    where = jnp.stack([core, side, jnp.where(core == 0, y, z), jnp.where(core == 0, z, y), cross])
    pick = image_pick[0]
    gain = ln_gain[None, :]

    mine, other, after = [], [], []
    for image in range(2):
        sent = part_of(image, where, vit_partial, vit_residual, after)
        after = [sent]
        theirs = lax.ppermute(sent, "c", SWAP)
        mine.append(chip_sum(image, where, vit_partial, theirs, vit_residual))
        other.append(lax.ppermute(mine[image], "xl", SWAP))

    def spread(array, firsts):
        return [array] + [rotate(firsts[k], True, k) for k in range(1, RING)]

    def gather(array):
        half = array.shape[0] // 2
        below, above = rotate(array, True, 1), rotate(array, True, RING - 1)
        top = rotate(below[:half], True, 1)
        bottom = rotate(above[half:], True, RING - 1)
        return [array, below, top, bottom, above]

    def core_sum(near_rows, away_rows):
        theirs = lax.ppermute(away_rows, "c", SWAP)
        return (near_rows.astype(F32) + theirs.astype(F32)).astype(BF)

    def step(image, own, far, texts, after):
        given = (key_weight, value_weight, queries, context_grad)
        return image_step(image, pick, text_len, own, far, *given, texts, after)

    own = norm(mine[0], other[0], gain, [mine[1]])
    far = lax.ppermute(own, "c", SWAP)
    pieces = strips(where, own, far, [])
    lefts = spread(pieces[0], pieces)
    *texts, near_rows, away_rows, grads = step(0, own, far, [], [pieces[0]])
    grads = later(grads, lefts[1:])
    rights = spread(grads, [grads] * RING)

    own = norm(mine[1], other[1], gain, [near_rows, *rights[1:]])
    far = lax.ppermute(own, "c", SWAP)
    pieces = strips(where, own, far, [])
    last_lefts = spread(pieces[0], pieces)
    near_0, away_0 = near_rows, away_rows
    *texts, near_rows, away_rows, grads = step(1, own, far, texts, [pieces[0]])
    share_0 = core_sum(near_0, later(away_0, [pieces[0]]))
    (so_far,) = weight_grad(where, lefts, rights, after=[near_rows, share_0])
    grads = later(grads, last_lefts[1:] + [so_far])
    last_rights = gather(grads)
    share_1 = core_sum(near_rows, later(away_rows, [grads]))

    from_second = lax.ppermute(share_0, "xl", [(1, 0)])
    from_first = lax.ppermute(share_1, "xl", [(0, 1)])
    blocks = weight_grad(where, last_lefts, last_rights, so_far, [share_0, share_1])
    kept, up, across_up, across_down, down = blocks
    got_up = rotate(across_up, False, 1)
    got_down = rotate(across_down, False, RING - 1)
    up, down = relay(up, got_up, down, got_down)
    got = [rotate(up, False, 1), rotate(down, False, RING - 1)]
    stream_grad = norm_back(
        where,
        gain,
        [mine[0], other[0], share_0, from_second],
        [mine[1], other[1], share_1, from_first],
    )
    kept, sent = ring_sum(where, [kept, *got], [from_first, from_second])
    got = lax.ppermute(sent, "xh", SWAP)
    key_weight_grad, value_weight_grad = last_sum(kept, got, [stream_grad])
    return texts[0], texts[1], key_weight_grad, value_weight_grad, stream_grad


def solution(mesh):
    fine = Mesh(mesh.devices.reshape(4, 2, 4, 2, 2), ("z", "xh", "y", "xl", "c"))
    dp, mp = ("z", "xh", "y"), ("xl", "c")
    placed = (
        P(mp, dp, None),
        P(dp + mp, None),
        P(),
        P(None, mp),
        P(None, mp),
        P(dp, None, mp),
        P(dp, None, mp),
        P(dp),
        P(dp, None),
    )
    return jax.shard_map(
        local,
        mesh=fine,
        in_specs=placed,
        out_specs=(P(dp, None, mp), P(dp, None, mp), P(dp, mp), P(dp, mp), P(dp + mp, None)),
        check_vma=False,
    )
```

profile of v0, /device:TPU:0, one launch (start us, length us, event | category | flops | bytes accessed | tf_op | source)
XLA Modules:
  0.0 205.5 jit_solution(9175407819253266055)
XLA Ops:
  1.3 2.9 %shard_map.128.refs_3_ = bf16[128,6144]{1,0:T(8,128)(2,1)} custom-call(s32[5]{0:T(128)} %stack.23.refs_0_, bf16[1,512,6144]{2,1,0:T(8,128)(2,1)} %refs_1_.9, bf16[128,6144]{1,0:T(8,128)(2,1)} %refs_3_.3), custom_call_target="tpu_custom_call" | custom-call | tf_op jit(solution)/shard_map/pallas_call | solution.py:39
  4.3 3.0 %shard_map.129 = bf16[128,6144]{1,0:T(8,128)(2,1)} custom-call(s32[5]{0:T(128)} %stack.23.refs_0_, bf16[1,512,6144]{2,1,0:T(8,128)(2,1)} %refs_1_.9, bf16[128,6144]{1,0:T(8,128)(2,1)} %refs_3_.3, bf16[128,6144]{1,0:T(8,128)(2,1)} %shard_map.128.refs_3_), custom_call_target="tpu_custom_call" | custom-call | tf_op jit(solution)/shard_map/pallas_call | solution.py:39
  7.9 2.8 %copy-done = bf16[1,512,6144]{2,1,0:T(8,128)(2,1)S(1)} copy-done((bf16[1,512,6144]{2,1,0:T(8,128)(2,1)S(1)}, bf16[1,512,6144]{2,1,0:T(8,128)(2,1)}, u32[]{:S(2)}) %copy-start) | copy-done | bytes 6291480
  10.7 1.3 shard_map.131.refs_0_.refs_2_
  12.0 1.7 collective-permute-start.3
  13.7 1.3 shard_map.130.refs_3_.refs_0_.refs_6_
  15.0 33.5 %collective-permute-done.3.refs_1_.refs_3_ = bf16[128,6144]{1,0:T(8,128)(2,1)S(1)} collective-permute-done((bf16[128,6144]{1,0:T(8,128)(2,1)S(1)}, bf16[128,6144]{1,0:T(8,128)(2,1)S(1)}, u32[]{:S(2)}, u32[]{:S(2)}) %collective-permute-start.3) | collective-permute-done | bytes 1572896 | tf_op jit(solution)/shard_map/ppermute | solution.py:662
  48.5 1.4 shard_map.132.refs_1_.refs_2_
  50.1 1.7 collective-permute-start.1
  51.7 1.7 collective-permute-done.4.refs_2_.refs_3_
  53.5 5.3 %shard_map.133 = (bf16[2,128,1536]{2,1,0:T(8,128)(2,1)S(1)}, bf16[2,128,1536]{2,1,0:T(8,128)(2,1)S(1)}, bf16[2,128,1536]{2,1,0:T(8,128)(2,1)S(1)}, bf16[2,128,1536]{2,1,0:T(8,128)(2,1)S(1)}) custom-call(s32[5]{0:T(128)S(1)} %copy-done.30, bf16[128,6144]{1,0:T(8,128)(2,1)S(1)} %shard_map.132.refs_1_.refs_2_, ...), custom_call_target="tpu_custom_call" | custom-call | bytes 6291456 | tf_op jit(solution)/shard_map/pallas_call | solution.py:39
  58.8 1.7 collective-permute-start.5
  60.5 2.9 %collective-permute-start.6 = (bf16[2,128,1536]{2,1,0:T(8,128)(2,1)S(1)}, bf16[2,128,1536]{2,1,0:T(8,128)(2,1)S(1)}, u32[]{:S(2)}, u32[]{:S(2)}) collective-permute-start(bf16[2,128,1536]{2,1,0:T(8,128)(2,1)S(1)} %get-tuple-element.38), channel_id=1, source_target_pairs={{0,8},{1,65},{4,12},{5,69},{8,0},{9,73},{12,4},{13,77},{32,40},{33... | collective-permute-start | bytes 2359304 | tf_op jit(solution)/shard_map/ppermute | solution.py:634
  63.4 1.3 collective-permute-start.7
  64.7 13.1 %shard_map.134 = (f32[2,512,512]{2,1,0:T(8,128)}, f32[2,512,512]{2,1,0:T(8,128)}, bf16[128,6144]{1,0:T(8,128)(2,1)S(1)}, bf16[128,6144]{1,0:T(8,128)(2,1)S(1)}, bf16[256,1024]{1,0:T(8,128)(2,1)S(1)}) custom-call(s32[2]{0:T(128)S(1)} %bitcast.10, s32[2]{0:T(128)S(1)} %copy-done.36, bf16[128,6144]{1,0:T(8,128)(2,1)S(1)} %shard_map.132.refs_1_.refs_2_, ...), custom_call_target="tpu_custom_call" | custom-call | flops 7247757312 | bytes 22020096 | tf_op jit(solution)/shard_map/pallas_call | solution.py:39
  77.9 3.9 %collective-permute-done.6.refs_2_.refs_3_ = bf16[2,128,1536]{2,1,0:T(8,128)(2,1)S(1)} collective-permute-done((bf16[2,128,1536]{2,1,0:T(8,128)(2,1)S(1)}, bf16[2,128,1536]{2,1,0:T(8,128)(2,1)S(1)}, u32[]{:S(2)}, u32[]{:S(2)}) %collective-permute-start.6) | collective-permute-done | bytes 786464 | tf_op jit(solution)/shard_map/ppermute | solution.py:634
  82.9 2.0 collective-permute-start.10
  85.0 2.6 %collective-permute-start.9 = (bf16[256,1024]{1,0:T(8,128)(2,1)S(1)}, bf16[256,1024]{1,0:T(8,128)(2,1)S(1)}, u32[]{:S(2)}, u32[]{:S(2)}) collective-permute-start(bf16[256,1024]{1,0:T(8,128)(2,1)S(1)} %shard_map.135.refs_5_), channel_id=1, source_target_pairs={{0,8},{1,65},{4,12},{5,69},{8,0},{9,73},{12,4},{13,77},{32,40},{33... | collective-permute-start | bytes 1572872 | tf_op jit(solution)/shard_map/ppermute | solution.py:634
  87.6 9.7 %collective-permute-done.10.refs_6_.refs_8_ = bf16[256,1024]{1,0:T(8,128)(2,1)S(1)} collective-permute-done((bf16[256,1024]{1,0:T(8,128)(2,1)S(1)}, bf16[256,1024]{1,0:T(8,128)(2,1)S(1)}, u32[]{:S(2)}, u32[]{:S(2)}) %collective-permute-start.10) | collective-permute-done | bytes 524320 | tf_op jit(solution)/shard_map/ppermute | solution.py:634
  97.2 3.7 %collective-permute-done.8.refs_4_.refs_6_ = bf16[256,1024]{1,0:T(8,128)(2,1)S(1)} collective-permute-done((bf16[256,1024]{1,0:T(8,128)(2,1)S(1)}, bf16[256,1024]{1,0:T(8,128)(2,1)S(1)}, u32[]{:S(2)}, u32[]{:S(2)}) %collective-permute-start.8) | collective-permute-done | bytes 524320 | tf_op jit(solution)/shard_map/ppermute | solution.py:634
  100.9 1.4 shard_map.136.refs_1_.refs_2_
  102.4 3.4 %collective-permute-done.11.refs_2_.refs_3_ = bf16[128,6144]{1,0:T(8,128)(2,1)S(1)} collective-permute-done((bf16[128,6144]{1,0:T(8,128)(2,1)S(1)}, bf16[128,6144]{1,0:T(8,128)(2,1)S(1)}, u32[]{:S(2)}, u32[]{:S(2)}) %collective-permute-start.11) | collective-permute-done | bytes 1572896 | tf_op jit(solution)/shard_map/ppermute | solution.py:691
  105.8 4.7 %shard_map.137 = (bf16[2,128,1536]{2,1,0:T(8,128)(2,1)S(1)}, bf16[2,128,1536]{2,1,0:T(8,128)(2,1)}, bf16[2,128,1536]{2,1,0:T(8,128)(2,1)}, bf16[2,128,1536]{2,1,0:T(8,128)(2,1)}) custom-call(s32[5]{0:T(128)S(1)} %copy-done.30, bf16[128,6144]{1,0:T(8,128)(2,1)S(1)} %shard_map.136.refs_1_.refs_2_, bf16[128,6144]{1,0:T(8,128)(2,1)S(1)} %collective-permute-done.11.refs_2_.refs_3_), custom_call_target="tpu_custom_call" | custom-call | bytes 6291456 | tf_op jit(solution)/shard_map/pallas_call | solution.py:39
  110.8 3.2 %collective-permute-start.13 = (bf16[2,128,1536]{2,1,0:T(8,128)(2,1)}, bf16[2,128,1536]{2,1,0:T(8,128)(2,1)S(1)}, u32[]{:S(2)}, u32[]{:S(2)}) collective-permute-start(bf16[2,128,1536]{2,1,0:T(8,128)(2,1)} %get-tuple-element.46), channel_id=1, source_target_pairs={{0,8},{1,65},{4,12},{5,69},{8,0},{9,73},{12,4},{13,77},{32,40},{33... | collective-permute-start | bytes 2359304 | tf_op jit(solution)/shard_map/ppermute | solution.py:634
  114.0 1.1 collective-permute-start.14
  115.0 13.1 %shard_map.138 = (f32[2,512,512]{2,1,0:T(8,128)}, f32[2,512,512]{2,1,0:T(8,128)}, bf16[128,6144]{1,0:T(8,128)(2,1)S(1)}, bf16[128,6144]{1,0:T(8,128)(2,1)S(1)}, bf16[256,1024]{1,0:T(8,128)(2,1)S(1)}) custom-call(s32[2]{0:T(128)S(1)} %bitcast.11, s32[2]{0:T(128)S(1)} %copy-done.36, ...), custom_call_target="tpu_custom_call", output_to_operand_aliasing={{0}: (8, {}), {1}: (9, {})} | custom-call | flops 7247757312 | bytes 22020096 | tf_op jit(solution)/shard_map/pallas_call | solution.py:39
  128.1 1.7 add_convert_fusion.1.refs_10_.refs_11_.refs_4_
  129.8 8.6 %shard_map.140.refs_4_.refs_10_ = bf16[4,384,1024]{2,1,0:T(8,128)(2,1)} custom-call(s32[5]{0:T(128)} %stack.23.refs_0_, bf16[2,128,1536]{2,1,0:T(8,128)(2,1)} %copy-done.28, bf16[2,128,1536]{2,1,0:T(8,128)(2,1)} %copy-done.21, bf16[2,128,1536]{2,1,0:T(8,128)(2,1)} %copy-done.22, bf16[2,128,1536]{2,1,0:T(8,128)(2,1)} %copy-done.23, ...), custom_call_target="tpu_custom_call" | custom-call | tf_op jit(solution)/shard_map/pallas_call | solution.py:39
  138.5 2.4 %copy-done.1 = bf16[4,384,1024]{2,1,0:T(8,128)(2,1)S(1)} copy-done((bf16[4,384,1024]{2,1,0:T(8,128)(2,1)S(1)}, bf16[4,384,1024]{2,1,0:T(8,128)(2,1)}, u32[]{:S(2)}) %copy-start.1) | copy-done | bytes 3145752
  140.9 2.0 collective-permute-start.20
  142.9 1.3 collective-permute-start.26
  144.7 2.9 %collective-permute-start.18 = (bf16[256,1024]{1,0:T(8,128)(2,1)S(1)}, bf16[256,1024]{1,0:T(8,128)(2,1)S(1)}, u32[]{:S(2)}, u32[]{:S(2)}) collective-permute-start(bf16[256,1024]{1,0:T(8,128)(2,1)S(1)} %shard_map.141.refs_1_.refs_5_), channel_id=1, source_target_pairs={{0,12},{1,97},{4,0},{5,101},{8,4},{9,105},{12,8},{13,109},{32,44},... | collective-permute-start | bytes 1572872 | tf_op jit(solution)/shard_map/ppermute | solution.py:634
  148.0 5.0 %collective-permute-start.25 = (bf16[128,6144]{1,0:T(8,128)(2,1)S(1)}, bf16[128,6144]{1,0:T(8,128)(2,1)S(1)}, u32[]{:S(2)}, u32[]{:S(2)}) collective-permute-start(bf16[128,6144]{1,0:T(8,128)(2,1)S(1)} %add_convert_fusion.refs_12_.refs_8_), channel_id=1, source_target_pairs={{0,2},{1,3},{4,6},{5,7},{8,10},{9,11},{12,14},{13,15},{16,18},{17,... | collective-permute-start | bytes 4718600 | tf_op jit(solution)/shard_map/ppermute | solution.py:703
  153.0 1.7 collective-permute-done.16.refs_6_
  154.8 3.5 %collective-permute-start.19 = (bf16[128,1024]{1,0:T(8,128)(2,1)S(1)}, bf16[128,1024]{1,0:T(8,128)(2,1)S(1)}, u32[]{:S(2)}, u32[]{:S(2)}) collective-permute-start(bf16[128,1024]{1,0:T(8,128)(2,1)S(1)} %slice.9), channel_id=1, source_target_pairs={{0,12},{1,97},{4,0},{5,101},{8,4},{9,105},{12,8},{13,109},{32,44},... | collective-permute-start | bytes 786440 | tf_op jit(solution)/shard_map/ppermute | solution.py:634
  158.3 4.0 %collective-permute-done.17.refs_7_ = bf16[128,1024]{1,0:T(8,128)(2,1)S(1)} collective-permute-done((bf16[128,1024]{1,0:T(8,128)(2,1)S(1)}, bf16[128,1024]{1,0:T(8,128)(2,1)S(1)}, u32[]{:S(2)}, u32[]{:S(2)}) %collective-permute-start.17) | collective-permute-done | bytes 262176 | tf_op jit(solution)/shard_map/ppermute | solution.py:634
  162.4 6.3 %shard_map.143 = (bf16[384,1024]{1,0:T(8,128)(2,1)S(1)}, bf16[384,1024]{1,0:T(8,128)(2,1)S(1)}, bf16[192,1024]{1,0:T(8,128)(2,1)S(1)}, bf16[192,1024]{1,0:T(8,128)(2,1)S(1)}, bf16[384,1024]{1,0:T(8,128)(2,1)S(1)}) custom-call(s32[5]{0:T(128)S(1)} %copy-done.31, bf16[2,128,1536]{2,1,0:T(8,128)(2,1)S(1)} %copy-done.20, ...), custom_call_target="tpu_custom_call" | custom-call | tf_op jit(solution)/shard_map/pallas_call | solution.py:39
  168.8 1.1 collective-permute-start.21
  169.8 2.2 %collective-permute-start.22 = (bf16[192,1024]{1,0:T(8,128)(2,1)S(1)}, bf16[192,1024]{1,0:T(8,128)(2,1)S(1)}, u32[]{:S(2)}, u32[]{:S(2)}) collective-permute-start(bf16[192,1024]{1,0:T(8,128)(2,1)S(1)} %get-tuple-element.56), channel_id=1, source_target_pairs={{0,96},{1,13},{4,100},{5,1},{8,104},{9,5},{12,108},{13,9},{32,0},{... | collective-permute-start | bytes 1179656 | tf_op jit(solution)/shard_map/ppermute | solution.py:634
  172.1 5.8 %collective-permute-done.21.refs_1_ = bf16[192,1024]{1,0:T(8,128)(2,1)S(1)} collective-permute-done((bf16[192,1024]{1,0:T(8,128)(2,1)S(1)}, bf16[192,1024]{1,0:T(8,128)(2,1)S(1)}, u32[]{:S(2)}, u32[]{:S(2)}) %collective-permute-start.21) | collective-permute-done | bytes 393248 | tf_op jit(solution)/shard_map/ppermute | solution.py:634
  178.1 1.2 collective-permute-start.23
  179.2 2.2 %collective-permute-start.24 = (bf16[384,1024]{1,0:T(8,128)(2,1)S(1)}, bf16[384,1024]{1,0:T(8,128)(2,1)S(1)}, u32[]{:S(2)}, u32[]{:S(2)}) collective-permute-start(bf16[384,1024]{1,0:T(8,128)(2,1)S(1)} %get-tuple-element.58), channel_id=1, source_target_pairs={{0,96},{1,13},{4,100},{5,1},{8,104},{9,5},{12,108},{13,9},{32,0},{... | collective-permute-start | bytes 2359304 | tf_op jit(solution)/shard_map/ppermute | solution.py:634
  181.8 9.6 %collective-permute-done.23.refs_2_ = bf16[384,1024]{1,0:T(8,128)(2,1)S(1)} collective-permute-done((bf16[384,1024]{1,0:T(8,128)(2,1)S(1)}, bf16[384,1024]{1,0:T(8,128)(2,1)S(1)}, u32[]{:S(2)}, u32[]{:S(2)}) %collective-permute-start.23) | collective-permute-done | bytes 786464 | tf_op jit(solution)/shard_map/ppermute | solution.py:634
  192.5 3.0 %collective-permute-start.27 = (bf16[192,1024]{1,0:T(8,128)(2,1)S(1)}, bf16[192,1024]{1,0:T(8,128)(2,1)S(1)}, u32[]{:S(2)}, u32[]{:S(2)}) collective-permute-start(bf16[192,1024]{1,0:T(8,128)(2,1)S(1)} %get-tuple-element.60), channel_id=1, source_target_pairs={{0,16},{16,0},{1,17},{17,1},{2,18},{18,2},{3,19},{19,3},{4,20},{20... | collective-permute-start | bytes 1179656 | tf_op jit(solution)/shard_map/ppermute | solution.py:717
  195.6 6.1 %shard_map.146.refs_2_ = f32[128,6144]{1,0:T(8,128)} custom-call(s32[5]{0:T(128)} %stack.23.refs_0_, f32[1,6144]{1,0:T(1,128)} %bitcast.7, bf16[128,6144]{1,0:T(8,128)(2,1)} %copy-done.6, bf16[128,6144]{1,0:T(8,128)(2,1)} %copy-done.9, bf16[128,6144]{1,0:T(8,128)(2,1)} %add_convert_fusion.1.refs_10_.refs_11_.refs_4_, bf16[128,6144]{1,0:T(8,128)(2,1)} %copy-done.11, ...), custom_call_target="tpu_custom_call" | custom-call | bytes 9437184 | tf_op jit(solution)/shard_map/pallas_call | solution.py:39
  201.7 0.9 collective-permute-done.27.refs_1_
  202.6 1.9 copy-done.8
  204.5 0.9 shard_map.147
  (107 shorter events, 5.8 us)
Async XLA Ops:
  4.2 3.7 %collective-permute-start.2 = (bf16[128,6144]{1,0:T(8,128)(2,1)}, bf16[128,6144]{1,0:T(8,128)(2,1)S(1)}, u32[]{:S(2)}, u32[]{:S(2)}) collective-permute-start(bf16[128,6144]{1,0:T(8,128)(2,1)} %shard_map.128.refs_3_), channel_id=1, source_target_pairs={{0,1},{1,0},{2,3},{3,2},{4,5},{5,4},{6,7},{7,6},{8,9},{9,8},{10,11... | collective-permute-start | bytes 4718600 | tf_op jit(solution)/shard_map/ppermute | solution.py:660
  7.3 6.4 %collective-permute-start = (bf16[128,6144]{1,0:T(8,128)(2,1)}, bf16[128,6144]{1,0:T(8,128)(2,1)S(1)}, u32[]{:S(2)}, u32[]{:S(2)}) collective-permute-start(bf16[128,6144]{1,0:T(8,128)(2,1)} %shard_map.129), channel_id=1, source_target_pairs={{0,1},{1,0},{2,3},{3,2},{4,5},{5,4},{6,7},{7,6},{8,9},{9,8},{10,11... | collective-permute-start | bytes 4718600 | tf_op jit(solution)/shard_map/ppermute | solution.py:660
  12.0 36.5 %copy-start.6 = (bf16[128,6144]{1,0:T(8,128)(2,1)}, bf16[128,6144]{1,0:T(8,128)(2,1)S(1)}, u32[]{:S(2)}) copy-start(bf16[128,6144]{1,0:T(8,128)(2,1)S(1)} %shard_map.131.refs_0_.refs_2_) | copy-start | bytes 4718596
  12.0 36.5 %copy-start.29 = (f32[6144]{0:T(1024)S(1)}, f32[6144]{0:T(1024)}, u32[]{:S(2)}) copy-start(f32[6144]{0:T(1024)} %param.11) | copy-start | bytes 73732
  12.0 36.5 %collective-permute-start.3 = (bf16[128,6144]{1,0:T(8,128)(2,1)S(1)}, bf16[128,6144]{1,0:T(8,128)(2,1)S(1)}, u32[]{:S(2)}, u32[]{:S(2)}) collective-permute-start(bf16[128,6144]{1,0:T(8,128)(2,1)S(1)} %shard_map.131.refs_0_.refs_2_), channel_id=1, source_target_pairs={{0,2},{2,0},{1,3},{3,1},{4,6},{6,4},{5,7},{7,5},{8,10},{10,8},{9,1... | collective-permute-start | bytes 4718600 | tf_op jit(solution)/shard_map/ppermute | solution.py:662
  15.0 85.9 %copy-start.3 = (bf16[128,6144]{1,0:T(8,128)(2,1)}, bf16[128,6144]{1,0:T(8,128)(2,1)S(1)}, u32[]{:S(2)}) copy-start(bf16[128,6144]{1,0:T(8,128)(2,1)S(1)} %shard_map.130.refs_3_.refs_0_.refs_6_) | copy-start | bytes 4718596
  49.9 14.8 %copy-start.32 = (bf16[2,512,512]{2,1,0:T(8,128)(2,1)S(1)}, bf16[2,512,512]{2,1,0:T(8,128)(2,1)}, u32[]{:S(2)}) copy-start(bf16[2,512,512]{2,1,0:T(8,128)(2,1)} %refs_6_.3) | copy-start | bytes 3145732
  49.9 14.8 %copy-start.33 = (bf16[2,512,512]{2,1,0:T(8,128)(2,1)S(1)}, bf16[2,512,512]{2,1,0:T(8,128)(2,1)}, u32[]{:S(2)}) copy-start(bf16[2,512,512]{2,1,0:T(8,128)(2,1)} %refs_7_.3) | copy-start | bytes 3145732
  50.0 14.8 %copy-start.35 = (s32[1,2]{1,0:T(1,128)S(1)}, s32[1,2]{1,0:T(1,128)}, u32[]{:S(2)}) copy-start(s32[1,2]{1,0:T(1,128)} %param.17) | copy-start | bytes 28
  50.0 14.8 %copy-start.36 = (s32[2]{0:T(128)S(1)}, s32[2]{0:T(128)}, u32[]{:S(2)}) copy-start(s32[2]{0:T(128)} %refs_1_.11) | copy-start | bytes 28
  50.0 3.5 %collective-permute-start.4 = (bf16[128,6144]{1,0:T(8,128)(2,1)S(1)}, bf16[128,6144]{1,0:T(8,128)(2,1)S(1)}, u32[]{:S(2)}, u32[]{:S(2)}) collective-permute-start(bf16[128,6144]{1,0:T(8,128)(2,1)S(1)} %shard_map.132.refs_1_.refs_2_), channel_id=1, source_target_pairs={{0,1},{1,0},{2,3},{3,2},{4,5},{5,4},{6,7},{7,6},{8,9},{9,8},{10,11... | collective-permute-start | bytes 4718600 | tf_op jit(solution)/shard_map/ppermute | solution.py:683
  50.1 37.5 %collective-permute-start.1 = (bf16[128,6144]{1,0:T(8,128)(2,1)S(1)}, bf16[128,6144]{1,0:T(8,128)(2,1)S(1)}, u32[]{:S(2)}, u32[]{:S(2)}) collective-permute-start(bf16[128,6144]{1,0:T(8,128)(2,1)S(1)} %shard_map.130.refs_3_.refs_0_.refs_6_), channel_id=1, source_target_pairs={{0,2},{2,0},{1,3},{3,1},{4,6},{6,4},{5,7},{7,5},{8,10},{10,8},{9,1... | collective-permute-start | bytes 4718600 | tf_op jit(solution)/shard_map/ppermute | solution.py:662
  58.7 19.1 %copy-start.28 = (bf16[2,128,1536]{2,1,0:T(8,128)(2,1)}, bf16[2,128,1536]{2,1,0:T(8,128)(2,1)S(1)}, u32[]{:S(2)}) copy-start(bf16[2,128,1536]{2,1,0:T(8,128)(2,1)S(1)} %get-tuple-element.34.refs_8_.refs_1_) | copy-start | bytes 2359300
  58.8 19.1 %collective-permute-start.5 = (bf16[2,128,1536]{2,1,0:T(8,128)(2,1)S(1)}, bf16[2,128,1536]{2,1,0:T(8,128)(2,1)S(1)}, u32[]{:S(2)}, u32[]{:S(2)}) collective-permute-start(bf16[2,128,1536]{2,1,0:T(8,128)(2,1)S(1)} %get-tuple-element.37), channel_id=1, source_target_pairs={{0,4},{1,33},{4,8},{5,37},{8,12},{9,41},{12,0},{13,45},{32,36},{33... | collective-permute-start | bytes 2359304 | tf_op jit(solution)/shard_map/ppermute | solution.py:634
  60.5 21.3 %collective-permute-start.6 = (bf16[2,128,1536]{2,1,0:T(8,128)(2,1)S(1)}, bf16[2,128,1536]{2,1,0:T(8,128)(2,1)S(1)}, u32[]{:S(2)}, u32[]{:S(2)}) collective-permute-start(bf16[2,128,1536]{2,1,0:T(8,128)(2,1)S(1)} %get-tuple-element.38), channel_id=1, source_target_pairs={{0,8},{1,65},{4,12},{5,69},{8,0},{9,73},{12,4},{13,77},{32,40},{33... | collective-permute-start | bytes 2359304 | tf_op jit(solution)/shard_map/ppermute | solution.py:634
  63.4 18.4 %collective-permute-start.7 = (bf16[2,128,1536]{2,1,0:T(8,128)(2,1)S(1)}, bf16[2,128,1536]{2,1,0:T(8,128)(2,1)S(1)}, u32[]{:S(2)}, u32[]{:S(2)}) collective-permute-start(bf16[2,128,1536]{2,1,0:T(8,128)(2,1)S(1)} %get-tuple-element.39), channel_id=1, source_target_pairs={{0,12},{1,97},{4,0},{5,101},{8,4},{9,105},{12,8},{13,109},{32,44},... | collective-permute-start | bytes 2359304 | tf_op jit(solution)/shard_map/ppermute | solution.py:634
  82.9 19.4 %copy-start.27 = (bf16[256,1024]{1,0:T(8,128)(2,1)}, bf16[256,1024]{1,0:T(8,128)(2,1)S(1)}, u32[]{:S(2)}) copy-start(bf16[256,1024]{1,0:T(8,128)(2,1)S(1)} %shard_map.135.refs_5_) | copy-start | bytes 1572868
  82.9 14.3 %collective-permute-start.10 = (bf16[256,1024]{1,0:T(8,128)(2,1)S(1)}, bf16[256,1024]{1,0:T(8,128)(2,1)S(1)}, u32[]{:S(2)}, u32[]{:S(2)}) collective-permute-start(bf16[256,1024]{1,0:T(8,128)(2,1)S(1)} %shard_map.135.refs_5_), channel_id=1, source_target_pairs={{0,12},{1,97},{4,0},{5,101},{8,4},{9,105},{12,8},{13,109},{32,44},... | collective-permute-start | bytes 1572872 | tf_op jit(solution)/shard_map/ppermute | solution.py:634
  84.9 16.0 %collective-permute-start.8 = (bf16[256,1024]{1,0:T(8,128)(2,1)S(1)}, bf16[256,1024]{1,0:T(8,128)(2,1)S(1)}, u32[]{:S(2)}, u32[]{:S(2)}) collective-permute-start(bf16[256,1024]{1,0:T(8,128)(2,1)S(1)} %shard_map.135.refs_5_), channel_id=1, source_target_pairs={{0,4},{1,33},{4,8},{5,37},{8,12},{9,41},{12,0},{13,45},{32,36},{33... | collective-permute-start | bytes 1572872 | tf_op jit(solution)/shard_map/ppermute | solution.py:634
  85.0 15.9 %collective-permute-start.9 = (bf16[256,1024]{1,0:T(8,128)(2,1)S(1)}, bf16[256,1024]{1,0:T(8,128)(2,1)S(1)}, u32[]{:S(2)}, u32[]{:S(2)}) collective-permute-start(bf16[256,1024]{1,0:T(8,128)(2,1)S(1)} %shard_map.135.refs_5_), channel_id=1, source_target_pairs={{0,8},{1,65},{4,12},{5,69},{8,0},{9,73},{12,4},{13,77},{32,40},{33... | collective-permute-start | bytes 1572872 | tf_op jit(solution)/shard_map/ppermute | solution.py:634
  87.6 14.7 %copy-start.10 = (bf16[128,6144]{1,0:T(8,128)(2,1)}, bf16[128,6144]{1,0:T(8,128)(2,1)S(1)}, u32[]{:S(2)}) copy-start(bf16[128,6144]{1,0:T(8,128)(2,1)S(1)} %collective-permute-done.1.refs_1_.refs_7_) | copy-start | bytes 4718596
  97.2 5.1 %copy-start.24 = (bf16[256,1024]{1,0:T(8,128)(2,1)}, bf16[256,1024]{1,0:T(8,128)(2,1)S(1)}, u32[]{:S(2)}) copy-start(bf16[256,1024]{1,0:T(8,128)(2,1)S(1)} %collective-permute-done.10.refs_6_.refs_8_) | copy-start | bytes 1572868
  102.3 3.5 %collective-permute-start.11 = (bf16[128,6144]{1,0:T(8,128)(2,1)S(1)}, bf16[128,6144]{1,0:T(8,128)(2,1)S(1)}, u32[]{:S(2)}, u32[]{:S(2)}) collective-permute-start(bf16[128,6144]{1,0:T(8,128)(2,1)S(1)} %shard_map.136.refs_1_.refs_2_), channel_id=1, source_target_pairs={{0,1},{1,0},{2,3},{3,2},{4,5},{5,4},{6,7},{7,6},{8,9},{9,8},{10,11... | collective-permute-start | bytes 4718600 | tf_op jit(solution)/shard_map/ppermute | solution.py:691
  110.5 4.5 %copy-start.19 = (bf16[2,128,1536]{2,1,0:T(8,128)(2,1)}, bf16[2,128,1536]{2,1,0:T(8,128)(2,1)S(1)}, u32[]{:S(2)}) copy-start(bf16[2,128,1536]{2,1,0:T(8,128)(2,1)S(1)} %get-tuple-element.42.refs_10_.refs_1_) | copy-start | bytes 2359300
  110.6 17.5 %collective-permute-start.15 = (bf16[128,6144]{1,0:T(8,128)(2,1)S(1)}, bf16[128,6144]{1,0:T(8,128)(2,1)S(1)}, u32[]{:S(2)}, u32[]{:S(2)}) collective-permute-start(bf16[128,6144]{1,0:T(8,128)(2,1)S(1)} %shard_map.139), channel_id=1, source_target_pairs={{0,1},{1,0},{2,3},{3,2},{4,5},{5,4},{6,7},{7,6},{8,9},{9,8},{10,11... | collective-permute-start | bytes 4718600 | tf_op jit(solution)/shard_map/ppermute | solution.py:675
  110.8 27.6 %collective-permute-start.12 = (bf16[2,128,1536]{2,1,0:T(8,128)(2,1)}, bf16[2,128,1536]{2,1,0:T(8,128)(2,1)S(1)}, u32[]{:S(2)}, u32[]{:S(2)}) collective-permute-start(bf16[2,128,1536]{2,1,0:T(8,128)(2,1)} %get-tuple-element.45), channel_id=1, source_target_pairs={{0,4},{1,33},{4,8},{5,37},{8,12},{9,41},{12,0},{13,45},{32,36},{33... | collective-permute-start | bytes 2359304 | tf_op jit(solution)/shard_map/ppermute | solution.py:634
  110.8 27.6 %collective-permute-start.13 = (bf16[2,128,1536]{2,1,0:T(8,128)(2,1)}, bf16[2,128,1536]{2,1,0:T(8,128)(2,1)S(1)}, u32[]{:S(2)}, u32[]{:S(2)}) collective-permute-start(bf16[2,128,1536]{2,1,0:T(8,128)(2,1)} %get-tuple-element.46), channel_id=1, source_target_pairs={{0,8},{1,65},{4,12},{5,69},{8,0},{9,73},{12,4},{13,77},{32,40},{33... | collective-permute-start | bytes 2359304 | tf_op jit(solution)/shard_map/ppermute | solution.py:634
  114.0 24.5 %collective-permute-start.14 = (bf16[2,128,1536]{2,1,0:T(8,128)(2,1)}, bf16[2,128,1536]{2,1,0:T(8,128)(2,1)S(1)}, u32[]{:S(2)}, u32[]{:S(2)}) collective-permute-start(bf16[2,128,1536]{2,1,0:T(8,128)(2,1)} %get-tuple-element.47), channel_id=1, source_target_pairs={{0,12},{1,97},{4,0},{5,101},{8,4},{9,105},{12,8},{13,109},{32,44},... | collective-permute-start | bytes 2359304 | tf_op jit(solution)/shard_map/ppermute | solution.py:634
  140.9 6.6 %copy-start.14 = (bf16[128,6144]{1,0:T(8,128)(2,1)S(1)}, bf16[128,6144]{1,0:T(8,128)(2,1)}, u32[]{:S(2)}) copy-start(bf16[128,6144]{1,0:T(8,128)(2,1)} %copy-done.13) | copy-start | bytes 4718596
  140.9 21.4 %copy-start.31 = (s32[5]{0:T(128)S(1)}, s32[5]{0:T(128)}, u32[]{:S(2)}) copy-start(s32[5]{0:T(128)} %stack.23.refs_0_) | copy-start | bytes 64
  140.9 6.6 %collective-permute-start.20 = (bf16[128,6144]{1,0:T(8,128)(2,1)S(1)}, bf16[128,6144]{1,0:T(8,128)(2,1)S(1)}, u32[]{:S(2)}, u32[]{:S(2)}) collective-permute-start(bf16[128,6144]{1,0:T(8,128)(2,1)S(1)} %shard_map.142), channel_id=1, source_target_pairs={{0,1},{1,0},{2,3},{3,2},{4,5},{5,4},{6,7},{7,6},{8,9},{9,8},{10,11... | collective-permute-start | bytes 4718600 | tf_op jit(solution)/shard_map/ppermute | solution.py:675
  142.9 38.8 %collective-permute-start.26 = (bf16[128,6144]{1,0:T(8,128)(2,1)S(1)}, bf16[128,6144]{1,0:T(8,128)(2,1)S(1)}, u32[]{:S(2)}, u32[]{:S(2)}) collective-permute-start(bf16[128,6144]{1,0:T(8,128)(2,1)S(1)} %copy-done.4), channel_id=1, source_target_pairs={{2,0},{3,1},{6,4},{7,5},{10,8},{11,9},{14,12},{15,13},{18,16},{19,... | collective-permute-start | bytes 4718600 | tf_op jit(solution)/shard_map/ppermute | solution.py:702
  144.2 10.5 %collective-permute-start.16 = (bf16[256,1024]{1,0:T(8,128)(2,1)S(1)}, bf16[256,1024]{1,0:T(8,128)(2,1)S(1)}, u32[]{:S(2)}, u32[]{:S(2)}) collective-permute-start(bf16[256,1024]{1,0:T(8,128)(2,1)S(1)} %shard_map.141.refs_1_.refs_5_), channel_id=1, source_target_pairs={{0,4},{1,33},{4,8},{5,37},{8,12},{9,41},{12,0},{13,45},{32,36},{33... | collective-permute-start | bytes 1572872 | tf_op jit(solution)/shard_map/ppermute | solution.py:634
  144.7 10.1 %collective-permute-start.18 = (bf16[256,1024]{1,0:T(8,128)(2,1)S(1)}, bf16[256,1024]{1,0:T(8,128)(2,1)S(1)}, u32[]{:S(2)}, u32[]{:S(2)}) collective-permute-start(bf16[256,1024]{1,0:T(8,128)(2,1)S(1)} %shard_map.141.refs_1_.refs_5_), channel_id=1, source_target_pairs={{0,12},{1,97},{4,0},{5,101},{8,4},{9,105},{12,8},{13,109},{32,44},... | collective-permute-start | bytes 1572872 | tf_op jit(solution)/shard_map/ppermute | solution.py:634
  147.5 14.8 %copy-start.2 = (bf16[4,384,1024]{2,1,0:T(8,128)(2,1)S(1)}, bf16[4,384,1024]{2,1,0:T(8,128)(2,1)}, u32[]{:S(2)}) copy-start(bf16[4,384,1024]{2,1,0:T(8,128)(2,1)} %shard_map.140.refs_4_.refs_10_) | copy-start | bytes 9437188
  147.5 14.8 %copy-start.18 = (bf16[2,128,1536]{2,1,0:T(8,128)(2,1)S(1)}, bf16[2,128,1536]{2,1,0:T(8,128)(2,1)}, u32[]{:S(2)}) copy-start(bf16[2,128,1536]{2,1,0:T(8,128)(2,1)} %copy-done.17) | copy-start | bytes 2359300
  147.5 14.8 %copy-start.20 = (bf16[2,128,1536]{2,1,0:T(8,128)(2,1)S(1)}, bf16[2,128,1536]{2,1,0:T(8,128)(2,1)}, u32[]{:S(2)}) copy-start(bf16[2,128,1536]{2,1,0:T(8,128)(2,1)} %copy-done.19) | copy-start | bytes 2359300
  147.9 20.8 %copy-start.7 = (bf16[128,6144]{1,0:T(8,128)(2,1)}, bf16[128,6144]{1,0:T(8,128)(2,1)S(1)}, u32[]{:S(2)}) copy-start(bf16[128,6144]{1,0:T(8,128)(2,1)S(1)} %add_convert_fusion.refs_12_.refs_8_) | copy-start | bytes 4718596
  147.9 14.4 %copy-start.16 = (bf16[2,128,1536]{2,1,0:T(8,128)(2,1)S(1)}, bf16[2,128,1536]{2,1,0:T(8,128)(2,1)}, u32[]{:S(2)}) copy-start(bf16[2,128,1536]{2,1,0:T(8,128)(2,1)} %copy-done.15) | copy-start | bytes 2359300
  148.0 43.4 %collective-permute-start.25 = (bf16[128,6144]{1,0:T(8,128)(2,1)S(1)}, bf16[128,6144]{1,0:T(8,128)(2,1)S(1)}, u32[]{:S(2)}, u32[]{:S(2)}) collective-permute-start(bf16[128,6144]{1,0:T(8,128)(2,1)S(1)} %add_convert_fusion.refs_12_.refs_8_), channel_id=1, source_target_pairs={{0,2},{1,3},{4,6},{5,7},{8,10},{9,11},{12,14},{13,15},{16,18},{17,... | collective-permute-start | bytes 4718600 | tf_op jit(solution)/shard_map/ppermute | solution.py:703
  154.7 7.7 %collective-permute-start.17 = (bf16[128,1024]{1,0:T(8,128)(2,1)S(1)}, bf16[128,1024]{1,0:T(8,128)(2,1)S(1)}, u32[]{:S(2)}, u32[]{:S(2)}) collective-permute-start(bf16[128,1024]{1,0:T(8,128)(2,1)S(1)} %slice.8), channel_id=1, source_target_pairs={{0,4},{1,33},{4,8},{5,37},{8,12},{9,41},{12,0},{13,45},{32,36},{33... | collective-permute-start | bytes 786440 | tf_op jit(solution)/shard_map/ppermute | solution.py:634
  154.8 7.5 %collective-permute-start.19 = (bf16[128,1024]{1,0:T(8,128)(2,1)S(1)}, bf16[128,1024]{1,0:T(8,128)(2,1)S(1)}, u32[]{:S(2)}, u32[]{:S(2)}) collective-permute-start(bf16[128,1024]{1,0:T(8,128)(2,1)S(1)} %slice.9), channel_id=1, source_target_pairs={{0,12},{1,97},{4,0},{5,101},{8,4},{9,105},{12,8},{13,109},{32,44},... | collective-permute-start | bytes 786440 | tf_op jit(solution)/shard_map/ppermute | solution.py:634
  168.8 9.1 %collective-permute-start.21 = (bf16[192,1024]{1,0:T(8,128)(2,1)S(1)}, bf16[192,1024]{1,0:T(8,128)(2,1)S(1)}, u32[]{:S(2)}, u32[]{:S(2)}) collective-permute-start(bf16[192,1024]{1,0:T(8,128)(2,1)S(1)} %get-tuple-element.54), channel_id=1, source_target_pairs={{0,32},{1,5},{4,36},{5,9},{8,40},{9,13},{12,44},{13,1},{32,64},{33... | collective-permute-start | bytes 1179656 | tf_op jit(solution)/shard_map/ppermute | solution.py:634
  169.8 8.0 %collective-permute-start.22 = (bf16[192,1024]{1,0:T(8,128)(2,1)S(1)}, bf16[192,1024]{1,0:T(8,128)(2,1)S(1)}, u32[]{:S(2)}, u32[]{:S(2)}) collective-permute-start(bf16[192,1024]{1,0:T(8,128)(2,1)S(1)} %get-tuple-element.56), channel_id=1, source_target_pairs={{0,96},{1,13},{4,100},{5,1},{8,104},{9,5},{12,108},{13,9},{32,0},{... | collective-permute-start | bytes 1179656 | tf_op jit(solution)/shard_map/ppermute | solution.py:634
  178.1 13.3 %collective-permute-start.23 = (bf16[384,1024]{1,0:T(8,128)(2,1)S(1)}, bf16[384,1024]{1,0:T(8,128)(2,1)S(1)}, u32[]{:S(2)}, u32[]{:S(2)}) collective-permute-start(bf16[384,1024]{1,0:T(8,128)(2,1)S(1)} %get-tuple-element.57), channel_id=1, source_target_pairs={{0,32},{1,5},{4,36},{5,9},{8,40},{9,13},{12,44},{13,1},{32,64},{33... | collective-permute-start | bytes 2359304 | tf_op jit(solution)/shard_map/ppermute | solution.py:634
  179.2 12.1 %collective-permute-start.24 = (bf16[384,1024]{1,0:T(8,128)(2,1)S(1)}, bf16[384,1024]{1,0:T(8,128)(2,1)S(1)}, u32[]{:S(2)}, u32[]{:S(2)}) collective-permute-start(bf16[384,1024]{1,0:T(8,128)(2,1)S(1)} %get-tuple-element.58), channel_id=1, source_target_pairs={{0,96},{1,13},{4,100},{5,1},{8,104},{9,5},{12,108},{13,9},{32,0},{... | collective-permute-start | bytes 2359304 | tf_op jit(solution)/shard_map/ppermute | solution.py:634
  181.8 10.4 %copy-start.11 = (bf16[128,6144]{1,0:T(8,128)(2,1)}, bf16[128,6144]{1,0:T(8,128)(2,1)S(1)}, u32[]{:S(2)}) copy-start(bf16[128,6144]{1,0:T(8,128)(2,1)S(1)} %collective-permute-done.26.refs_5_) | copy-start | bytes 4718596
  192.5 10.1 %collective-permute-start.27 = (bf16[192,1024]{1,0:T(8,128)(2,1)S(1)}, bf16[192,1024]{1,0:T(8,128)(2,1)S(1)}, u32[]{:S(2)}, u32[]{:S(2)}) collective-permute-start(bf16[192,1024]{1,0:T(8,128)(2,1)S(1)} %get-tuple-element.60), channel_id=1, source_target_pairs={{0,16},{16,0},{1,17},{17,1},{2,18},{18,2},{3,19},{19,3},{4,20},{20... | collective-permute-start | bytes 1179656 | tf_op jit(solution)/shard_map/ppermute | solution.py:717
  (17 other events, 39.1 us)
where the time goes:
time: 207 us; the launch traced here: 205 us
  waiting for transfers between devices  78.4 us (38%)
  Pallas kernels  70.4 us (34%)
  starting transfers between devices  43.9 us (21%)
  local copies, waits for them, and re-layouts  9.43 us (5%)
  other arithmetic  2.07 us (1%)
    pallas_call x20, Pallas kernels, call(): pl.pallas_call(with_waits, grid_spec=pltpu.PrefetchScalarGridSpec(num_sca...  70.4 us
    ppermute x17, waiting for transfers between devices, rotate(): return lax.ppermute(array, ('z', 'y', 'c'), hop(first, distance))  38.3 us
    ppermute x2, waiting for transfers between devices, local(): other.append(lax.ppermute(mine[image], 'xl', SWAP))  33.5 us
    ppermute x17, starting transfers between devices, rotate(): return lax.ppermute(array, ('z', 'y', 'c'), hop(first, distance))  28.4 us
    unnamed x74, local copies, waits for them, and re-layouts  8.77 us
    ppermute x2, waiting for transfers between devices, local(): far = lax.ppermute(own, 'c', SWAP)  5.14 us
    ppermute x1, starting transfers between devices, local(): from_first = lax.ppermute(share_1, 'xl', [(0, 1)])  5 us
  transfers between devices with their start and end apart: 28, of which 13 were waited for; matrix products, arithmetic and copies ran while one was open for 1% of the time, Pallas kernels for 28%

commit v1 on v0

--- a/solution.py
+++ b/solution.py
@@ -578,7 +578,6 @@
         ],
         after=after,
         cost_estimate=cost(0, 0),
-        mib=56 if first else 20,
     )
 
 
@@ -664,13 +663,6 @@
     def spread(array, firsts):
         return [array] + [rotate(firsts[k], True, k) for k in range(1, RING)]
 
-    def gather(array):
-        half = array.shape[0] // 2
-        below, above = rotate(array, True, 1), rotate(array, True, RING - 1)
-        top = rotate(below[:half], True, 1)
-        bottom = rotate(above[half:], True, RING - 1)
-        return [array, below, top, bottom, above]
-
     def core_sum(near_rows, away_rows):
         theirs = lax.ppermute(away_rows, "c", SWAP)
         return (near_rows.astype(F32) + theirs.astype(F32)).astype(BF)
@@ -694,9 +686,9 @@
     near_0, away_0 = near_rows, away_rows
     *texts, near_rows, away_rows, grads = step(1, own, far, texts, [pieces[0]])
     share_0 = core_sum(near_0, later(away_0, [pieces[0]]))
-    (so_far,) = weight_grad(where, lefts, rights, after=[near_rows, share_0])
-    grads = later(grads, last_lefts[1:] + [so_far])
-    last_rights = gather(grads)
+    grads = later(grads, last_lefts[1:])
+    last_rights = spread(grads, [grads] * RING)
+    (so_far,) = weight_grad(where, lefts, rights, after=[grads, share_0])
     share_1 = core_sum(near_rows, later(away_rows, [grads]))
 
     from_second = lax.ppermute(share_0, "xl", [(1, 0)])

time: 207 us -> 198 us (0.957)
  starting transfers between devices: 43.9 us -> 39.6 us
  local copies, waits for them, and re-layouts: 9.43 us -> 6.72 us
    ppermute x1, waiting for transfers between devices: 0.33 us -> 4.16 us  [local(): from_second = lax.ppermute(share_0, 'xl', [(1, 0)])]
    ppermute x17 -> x16, starting transfers between devices: 28.4 us -> 25 us  [rotate(): return lax.ppermute(array, ('z', 'y', 'c'), hop(first, distance))]
    unnamed x74 -> x60, local copies, waits for them, and re-layouts: 8.77 us -> 6.05 us
    ppermute x17 -> x16, waiting for transfers between devices: 38.3 us -> 36.8 us  [rotate(): return lax.ppermute(array, ('z', 'y', 'c'), hop(first, distance))]
  transfers between devices with their start and end apart: 28 -> 27, of which waited for: 13 -> 15; matrix products, arithmetic and copies ran while one was open for 1% -> 0% of each run, Pallas kernels for 28% -> 28%
where the time goes in v1:
time: 198 us; the launch traced here: 197 us
  waiting for transfers between devices  80.3 us (41%)
  Pallas kernels  68.6 us (35%)
  starting transfers between devices  39.6 us (20%)
  local copies, waits for them, and re-layouts  6.72 us (3%)
    pallas_call x20, Pallas kernels, call(): pl.pallas_call(with_waits, grid_spec=pltpu.PrefetchScalarGridSpec(num_sca...  68.6 us
    ppermute x16, waiting for transfers between devices, rotate(): return lax.ppermute(array, ('z', 'y', 'c'), hop(first, distance))  36.8 us
    ppermute x2, waiting for transfers between devices, local(): other.append(lax.ppermute(mine[image], 'xl', SWAP))  33.6 us
    ppermute x16, starting transfers between devices, rotate(): return lax.ppermute(array, ('z', 'y', 'c'), hop(first, distance))  25 us
    unnamed x60, local copies, waits for them, and re-layouts  6.05 us
    ppermute x1, starting transfers between devices, local(): from_first = lax.ppermute(share_1, 'xl', [(0, 1)])  5.23 us
    ppermute x2, waiting for transfers between devices, local(): far = lax.ppermute(own, 'c', SWAP)  5.14 us
    ppermute x1, waiting for transfers between devices, local(): from_second = lax.ppermute(share_0, 'xl', [(1, 0)])  4.16 us
  transfers between devices with their start and end apart: 27, of which 15 were waited for; matrix products, arithmetic and copies ran while one was open for 0% of the time, Pallas kernels for 28%

profile of v1, /device:TPU:0, one launch (start us, length us, event | category | flops | bytes accessed | tf_op | source)
XLA Modules:
  0.0 197.1 jit_solution(6750474276639839584)
XLA Ops:
  1.3 2.9 %shard_map.128.refs_3_ = bf16[128,6144]{1,0:T(8,128)(2,1)} custom-call(s32[5]{0:T(128)} %stack.23.refs_0_, bf16[1,512,6144]{2,1,0:T(8,128)(2,1)} %refs_1_.9, bf16[128,6144]{1,0:T(8,128)(2,1)} %refs_3_.3), custom_call_target="tpu_custom_call" | custom-call | tf_op jit(solution)/shard_map/pallas_call | solution.py:39
  4.3 3.0 %shard_map.129 = bf16[128,6144]{1,0:T(8,128)(2,1)} custom-call(s32[5]{0:T(128)} %stack.23.refs_0_, bf16[1,512,6144]{2,1,0:T(8,128)(2,1)} %refs_1_.9, bf16[128,6144]{1,0:T(8,128)(2,1)} %refs_3_.3, bf16[128,6144]{1,0:T(8,128)(2,1)} %shard_map.128.refs_3_), custom_call_target="tpu_custom_call" | custom-call | tf_op jit(solution)/shard_map/pallas_call | solution.py:39
  7.9 2.8 %copy-done = bf16[1,512,6144]{2,1,0:T(8,128)(2,1)S(1)} copy-done((bf16[1,512,6144]{2,1,0:T(8,128)(2,1)S(1)}, bf16[1,512,6144]{2,1,0:T(8,128)(2,1)}, u32[]{:S(2)}) %copy-start) | copy-done | bytes 6291480
  10.7 1.3 shard_map.131.refs_0_.refs_2_
  12.0 1.7 collective-permute-start.3
  13.7 1.3 shard_map.130.refs_3_.refs_0_.refs_6_
  15.0 33.6 %collective-permute-done.3.refs_1_.refs_3_ = bf16[128,6144]{1,0:T(8,128)(2,1)S(1)} collective-permute-done((bf16[128,6144]{1,0:T(8,128)(2,1)S(1)}, bf16[128,6144]{1,0:T(8,128)(2,1)S(1)}, u32[]{:S(2)}, u32[]{:S(2)}) %collective-permute-start.3) | collective-permute-done | bytes 1572896 | tf_op jit(solution)/shard_map/ppermute | solution.py:661
  48.5 1.4 shard_map.132.refs_1_.refs_2_
  50.1 1.7 collective-permute-start.1
  51.7 1.7 collective-permute-done.4.refs_2_.refs_3_
  53.5 5.3 %shard_map.133 = (bf16[2,128,1536]{2,1,0:T(8,128)(2,1)S(1)}, bf16[2,128,1536]{2,1,0:T(8,128)(2,1)S(1)}, bf16[2,128,1536]{2,1,0:T(8,128)(2,1)S(1)}, bf16[2,128,1536]{2,1,0:T(8,128)(2,1)S(1)}) custom-call(s32[5]{0:T(128)S(1)} %copy-done.24, bf16[128,6144]{1,0:T(8,128)(2,1)S(1)} %shard_map.132.refs_1_.refs_2_, ...), custom_call_target="tpu_custom_call" | custom-call | bytes 6291456 | tf_op jit(solution)/shard_map/pallas_call | solution.py:39
  58.7 1.7 collective-permute-start.5
  60.5 2.9 %collective-permute-start.6 = (bf16[2,128,1536]{2,1,0:T(8,128)(2,1)S(1)}, bf16[2,128,1536]{2,1,0:T(8,128)(2,1)S(1)}, u32[]{:S(2)}, u32[]{:S(2)}) collective-permute-start(bf16[2,128,1536]{2,1,0:T(8,128)(2,1)S(1)} %get-tuple-element.38), channel_id=1, source_target_pairs={{0,8},{1,65},{4,12},{5,69},{8,0},{9,73},{12,4},{13,77},{32,40},{33... | collective-permute-start | bytes 2359304 | tf_op jit(solution)/shard_map/ppermute | solution.py:633
  63.4 1.3 collective-permute-start.7
  64.7 13.2 %shard_map.134 = (f32[2,512,512]{2,1,0:T(8,128)}, f32[2,512,512]{2,1,0:T(8,128)}, bf16[128,6144]{1,0:T(8,128)(2,1)S(1)}, bf16[128,6144]{1,0:T(8,128)(2,1)S(1)}, bf16[256,1024]{1,0:T(8,128)(2,1)S(1)}) custom-call(s32[2]{0:T(128)S(1)} %bitcast.10, s32[2]{0:T(128)S(1)} %copy-done.29, bf16[128,6144]{1,0:T(8,128)(2,1)S(1)} %shard_map.132.refs_1_.refs_2_, ...), custom_call_target="tpu_custom_call" | custom-call | flops 7247757312 | bytes 22020096 | tf_op jit(solution)/shard_map/pallas_call | solution.py:39
  78.0 3.8 %collective-permute-done.6.refs_2_.refs_3_ = bf16[2,128,1536]{2,1,0:T(8,128)(2,1)S(1)} collective-permute-done((bf16[2,128,1536]{2,1,0:T(8,128)(2,1)S(1)}, bf16[2,128,1536]{2,1,0:T(8,128)(2,1)S(1)}, u32[]{:S(2)}, u32[]{:S(2)}) %collective-permute-start.6) | collective-permute-done | bytes 786464 | tf_op jit(solution)/shard_map/ppermute | solution.py:633
  81.8 0.9 copy-done.11
  82.6 2.2 %collective-permute-start.10 = (bf16[256,1024]{1,0:T(8,128)(2,1)S(1)}, bf16[256,1024]{1,0:T(8,128)(2,1)S(1)}, u32[]{:S(2)}, u32[]{:S(2)}) collective-permute-start(bf16[256,1024]{1,0:T(8,128)(2,1)S(1)} %shard_map.135.refs_5_), channel_id=1, source_target_pairs={{0,12},{1,97},{4,0},{5,101},{8,4},{9,105},{12,8},{13,109},{32,44},... | collective-permute-start | bytes 1572872 | tf_op jit(solution)/shard_map/ppermute | solution.py:633
  84.8 1.4 collective-permute-start.9
  86.9 10.3 %collective-permute-done.10.refs_6_.refs_8_ = bf16[256,1024]{1,0:T(8,128)(2,1)S(1)} collective-permute-done((bf16[256,1024]{1,0:T(8,128)(2,1)S(1)}, bf16[256,1024]{1,0:T(8,128)(2,1)S(1)}, u32[]{:S(2)}, u32[]{:S(2)}) %collective-permute-start.10) | collective-permute-done | bytes 524320 | tf_op jit(solution)/shard_map/ppermute | solution.py:633
  97.2 3.9 %collective-permute-done.8.refs_4_.refs_6_ = bf16[256,1024]{1,0:T(8,128)(2,1)S(1)} collective-permute-done((bf16[256,1024]{1,0:T(8,128)(2,1)S(1)}, bf16[256,1024]{1,0:T(8,128)(2,1)S(1)}, u32[]{:S(2)}, u32[]{:S(2)}) %collective-permute-start.8) | collective-permute-done | bytes 524320 | tf_op jit(solution)/shard_map/ppermute | solution.py:633
  101.1 1.3 shard_map.136.refs_1_.refs_2_
  102.6 3.4 %collective-permute-done.11.refs_2_.refs_3_ = bf16[128,6144]{1,0:T(8,128)(2,1)S(1)} collective-permute-done((bf16[128,6144]{1,0:T(8,128)(2,1)S(1)}, bf16[128,6144]{1,0:T(8,128)(2,1)S(1)}, u32[]{:S(2)}, u32[]{:S(2)}) %collective-permute-start.11) | collective-permute-done | bytes 1572896 | tf_op jit(solution)/shard_map/ppermute | solution.py:683
  106.0 5.3 %shard_map.137 = (bf16[2,128,1536]{2,1,0:T(8,128)(2,1)S(1)}, bf16[2,128,1536]{2,1,0:T(8,128)(2,1)}, bf16[2,128,1536]{2,1,0:T(8,128)(2,1)S(1)}, bf16[2,128,1536]{2,1,0:T(8,128)(2,1)S(1)}) custom-call(s32[5]{0:T(128)S(1)} %copy-done.24, bf16[128,6144]{1,0:T(8,128)(2,1)S(1)} %shard_map.136.refs_1_.refs_2_, ...), custom_call_target="tpu_custom_call" | custom-call | bytes 6291456 | tf_op jit(solution)/shard_map/pallas_call | solution.py:39
  111.6 3.2 %collective-permute-start.13 = (bf16[2,128,1536]{2,1,0:T(8,128)(2,1)S(1)}, bf16[2,128,1536]{2,1,0:T(8,128)(2,1)S(1)}, u32[]{:S(2)}, u32[]{:S(2)}) collective-permute-start(bf16[2,128,1536]{2,1,0:T(8,128)(2,1)S(1)} %get-tuple-element.46), channel_id=1, source_target_pairs={{0,8},{1,65},{4,12},{5,69},{8,0},{9,73},{12,4},{13,77},{32,40},{33... | collective-permute-start | bytes 2359304 | tf_op jit(solution)/shard_map/ppermute | solution.py:633
  114.8 1.1 collective-permute-start.14
  115.8 13.2 %shard_map.138 = (f32[2,512,512]{2,1,0:T(8,128)}, f32[2,512,512]{2,1,0:T(8,128)}, bf16[128,6144]{1,0:T(8,128)(2,1)S(1)}, bf16[128,6144]{1,0:T(8,128)(2,1)S(1)}, bf16[256,1024]{1,0:T(8,128)(2,1)S(1)}) custom-call(s32[2]{0:T(128)S(1)} %bitcast.11, s32[2]{0:T(128)S(1)} %copy-done.29, ...), custom_call_target="tpu_custom_call", output_to_operand_aliasing={{0}: (8, {}), {1}: (9, {})} | custom-call | flops 7247757312 | bytes 22020096 | tf_op jit(solution)/shard_map/pallas_call | solution.py:39
  129.0 4.4 %collective-permute-done.13.refs_2_.refs_3_ = bf16[2,128,1536]{2,1,0:T(8,128)(2,1)S(1)} collective-permute-done((bf16[2,128,1536]{2,1,0:T(8,128)(2,1)S(1)}, bf16[2,128,1536]{2,1,0:T(8,128)(2,1)S(1)}, u32[]{:S(2)}, u32[]{:S(2)}) %collective-permute-start.13) | collective-permute-done | bytes 786464 | tf_op jit(solution)/shard_map/ppermute | solution.py:633
  134.1 0.9 collective-permute-start.19
  135.0 1.7 collective-permute-start.17
  137.1 0.7 collective-permute-start.15
  138.2 1.3 collective-permute-start.25
  140.0 5.2 %collective-permute-start.24 = (bf16[128,6144]{1,0:T(8,128)(2,1)S(1)}, bf16[128,6144]{1,0:T(8,128)(2,1)S(1)}, u32[]{:S(2)}, u32[]{:S(2)}) collective-permute-start(bf16[128,6144]{1,0:T(8,128)(2,1)S(1)} %add_convert_fusion.refs_11_.refs_8_), channel_id=1, source_target_pairs={{0,2},{1,3},{4,6},{5,7},{8,10},{9,11},{12,14},{13,15},{16,18},{17,... | collective-permute-start | bytes 4718600 | tf_op jit(solution)/shard_map/ppermute | solution.py:695
  145.3 6.0 %shard_map.141.refs_9_ = bf16[4,384,1024]{2,1,0:T(8,128)(2,1)S(1)} custom-call(s32[5]{0:T(128)S(1)} %copy-done.24, bf16[2,128,1536]{2,1,0:T(8,128)(2,1)S(1)} %copy-done.22, bf16[2,128,1536]{2,1,0:T(8,128)(2,1)S(1)} %collective-permute-done.5.refs_1_.refs_2_, bf16[2,128,1536]{2,1,0:T(8,128)(2,1)S(1)} %collective-permute-done.6.refs_2_.refs_3_, ...), custom_call_target="tpu_custom_call" | custom-call | tf_op jit(solution)/shard_map/pallas_call | solution.py:39
  151.3 1.7 collective-permute-done.15.refs_6_
  153.1 6.3 %shard_map.143 = (bf16[384,1024]{1,0:T(8,128)(2,1)S(1)}, bf16[384,1024]{1,0:T(8,128)(2,1)S(1)}, bf16[192,1024]{1,0:T(8,128)(2,1)S(1)}, bf16[192,1024]{1,0:T(8,128)(2,1)S(1)}, bf16[384,1024]{1,0:T(8,128)(2,1)S(1)}) custom-call(s32[5]{0:T(128)S(1)} %copy-done.24, bf16[2,128,1536]{2,1,0:T(8,128)(2,1)S(1)} %get-tuple-element.42.refs_10_.refs_1_, ...), custom_call_target="tpu_custom_call" | custom-call | tf_op jit(solution)/shard_map/pallas_call | solution.py:39
  159.4 2.0 %collective-permute-start.20 = (bf16[192,1024]{1,0:T(8,128)(2,1)S(1)}, bf16[192,1024]{1,0:T(8,128)(2,1)S(1)}, u32[]{:S(2)}, u32[]{:S(2)}) collective-permute-start(bf16[192,1024]{1,0:T(8,128)(2,1)S(1)} %get-tuple-element.54), channel_id=1, source_target_pairs={{0,32},{1,5},{4,36},{5,9},{8,40},{9,13},{12,44},{13,1},{32,64},{33... | collective-permute-start | bytes 1179656 | tf_op jit(solution)/shard_map/ppermute | solution.py:633
  161.4 2.2 %collective-permute-start.21 = (bf16[192,1024]{1,0:T(8,128)(2,1)S(1)}, bf16[192,1024]{1,0:T(8,128)(2,1)S(1)}, u32[]{:S(2)}, u32[]{:S(2)}) collective-permute-start(bf16[192,1024]{1,0:T(8,128)(2,1)S(1)} %get-tuple-element.56), channel_id=1, source_target_pairs={{0,96},{1,13},{4,100},{5,1},{8,104},{9,5},{12,108},{13,9},{32,0},{... | collective-permute-start | bytes 1179656 | tf_op jit(solution)/shard_map/ppermute | solution.py:633
  163.6 5.7 %collective-permute-done.20.refs_1_ = bf16[192,1024]{1,0:T(8,128)(2,1)S(1)} collective-permute-done((bf16[192,1024]{1,0:T(8,128)(2,1)S(1)}, bf16[192,1024]{1,0:T(8,128)(2,1)S(1)}, u32[]{:S(2)}, u32[]{:S(2)}) %collective-permute-start.20) | collective-permute-done | bytes 393248 | tf_op jit(solution)/shard_map/ppermute | solution.py:633
  169.5 1.9 collective-permute-start.22
  171.4 1.6 collective-permute-start.23
  173.0 4.2 %collective-permute-done.25.refs_5_ = bf16[128,6144]{1,0:T(8,128)(2,1)S(1)} collective-permute-done((bf16[128,6144]{1,0:T(8,128)(2,1)S(1)}, bf16[128,6144]{1,0:T(8,128)(2,1)S(1)}, u32[]{:S(2)}, u32[]{:S(2)}) %collective-permute-start.25) | collective-permute-done | bytes 1572896 | tf_op jit(solution)/shard_map/ppermute | solution.py:694
  177.1 5.7 %collective-permute-done.22.refs_2_ = bf16[384,1024]{1,0:T(8,128)(2,1)S(1)} collective-permute-done((bf16[384,1024]{1,0:T(8,128)(2,1)S(1)}, bf16[384,1024]{1,0:T(8,128)(2,1)S(1)}, u32[]{:S(2)}, u32[]{:S(2)}) %collective-permute-start.22) | collective-permute-done | bytes 786464 | tf_op jit(solution)/shard_map/ppermute | solution.py:633
  183.4 0.8 shard_map.145
  184.6 3.0 %collective-permute-start.26 = (bf16[192,1024]{1,0:T(8,128)(2,1)S(1)}, bf16[192,1024]{1,0:T(8,128)(2,1)S(1)}, u32[]{:S(2)}, u32[]{:S(2)}) collective-permute-start(bf16[192,1024]{1,0:T(8,128)(2,1)S(1)} %get-tuple-element.60), channel_id=1, source_target_pairs={{0,16},{16,0},{1,17},{17,1},{2,18},{18,2},{3,19},{19,3},{4,20},{20... | collective-permute-start | bytes 1179656 | tf_op jit(solution)/shard_map/ppermute | solution.py:709
  187.6 6.1 %shard_map.146.refs_2_ = f32[128,6144]{1,0:T(8,128)} custom-call(s32[5]{0:T(128)} %stack.23.refs_0_, f32[1,6144]{1,0:T(1,128)} %bitcast.7, bf16[128,6144]{1,0:T(8,128)(2,1)} %copy-done.4, bf16[128,6144]{1,0:T(8,128)(2,1)} %copy-done.7, bf16[128,6144]{1,0:T(8,128)(2,1)} %copy-done.2, bf16[128,6144]{1,0:T(8,128)(2,1)} %copy-done.9, ...), custom_call_target="tpu_custom_call" | custom-call | bytes 9437184 | tf_op jit(solution)/shard_map/pallas_call | solution.py:39
  194.3 1.9 copy-done.6
  196.2 0.9 shard_map.147
  (89 shorter events, 6.0 us)
Async XLA Ops:
  4.2 3.7 %collective-permute-start.2 = (bf16[128,6144]{1,0:T(8,128)(2,1)}, bf16[128,6144]{1,0:T(8,128)(2,1)S(1)}, u32[]{:S(2)}, u32[]{:S(2)}) collective-permute-start(bf16[128,6144]{1,0:T(8,128)(2,1)} %shard_map.128.refs_3_), channel_id=1, source_target_pairs={{0,1},{1,0},{2,3},{3,2},{4,5},{5,4},{6,7},{7,6},{8,9},{9,8},{10,11... | collective-permute-start | bytes 4718600 | tf_op jit(solution)/shard_map/ppermute | solution.py:659
  7.3 6.4 %collective-permute-start = (bf16[128,6144]{1,0:T(8,128)(2,1)}, bf16[128,6144]{1,0:T(8,128)(2,1)S(1)}, u32[]{:S(2)}, u32[]{:S(2)}) collective-permute-start(bf16[128,6144]{1,0:T(8,128)(2,1)} %shard_map.129), channel_id=1, source_target_pairs={{0,1},{1,0},{2,3},{3,2},{4,5},{5,4},{6,7},{7,6},{8,9},{9,8},{10,11... | collective-permute-start | bytes 4718600 | tf_op jit(solution)/shard_map/ppermute | solution.py:659
  12.0 36.5 %copy-start.4 = (bf16[128,6144]{1,0:T(8,128)(2,1)}, bf16[128,6144]{1,0:T(8,128)(2,1)S(1)}, u32[]{:S(2)}) copy-start(bf16[128,6144]{1,0:T(8,128)(2,1)S(1)} %shard_map.131.refs_0_.refs_2_) | copy-start | bytes 4718596
  12.0 36.5 %copy-start.23 = (f32[6144]{0:T(1024)S(1)}, f32[6144]{0:T(1024)}, u32[]{:S(2)}) copy-start(f32[6144]{0:T(1024)} %param.11) | copy-start | bytes 73732
  12.0 36.5 %collective-permute-start.3 = (bf16[128,6144]{1,0:T(8,128)(2,1)S(1)}, bf16[128,6144]{1,0:T(8,128)(2,1)S(1)}, u32[]{:S(2)}, u32[]{:S(2)}) collective-permute-start(bf16[128,6144]{1,0:T(8,128)(2,1)S(1)} %shard_map.131.refs_0_.refs_2_), channel_id=1, source_target_pairs={{0,2},{2,0},{1,3},{3,1},{4,6},{6,4},{5,7},{7,5},{8,10},{10,8},{9,1... | collective-permute-start | bytes 4718600 | tf_op jit(solution)/shard_map/ppermute | solution.py:661
  15.0 86.2 %copy-start.1 = (bf16[128,6144]{1,0:T(8,128)(2,1)}, bf16[128,6144]{1,0:T(8,128)(2,1)S(1)}, u32[]{:S(2)}) copy-start(bf16[128,6144]{1,0:T(8,128)(2,1)S(1)} %shard_map.130.refs_3_.refs_0_.refs_6_) | copy-start | bytes 4718596
  49.9 14.8 %copy-start.25 = (bf16[2,512,512]{2,1,0:T(8,128)(2,1)S(1)}, bf16[2,512,512]{2,1,0:T(8,128)(2,1)}, u32[]{:S(2)}) copy-start(bf16[2,512,512]{2,1,0:T(8,128)(2,1)} %refs_6_.3) | copy-start | bytes 3145732
  49.9 14.8 %copy-start.26 = (bf16[2,512,512]{2,1,0:T(8,128)(2,1)S(1)}, bf16[2,512,512]{2,1,0:T(8,128)(2,1)}, u32[]{:S(2)}) copy-start(bf16[2,512,512]{2,1,0:T(8,128)(2,1)} %refs_7_.3) | copy-start | bytes 3145732
  49.9 14.8 %copy-start.28 = (s32[1,2]{1,0:T(1,128)S(1)}, s32[1,2]{1,0:T(1,128)}, u32[]{:S(2)}) copy-start(s32[1,2]{1,0:T(1,128)} %param.17) | copy-start | bytes 28
  49.9 14.8 %copy-start.29 = (s32[2]{0:T(128)S(1)}, s32[2]{0:T(128)}, u32[]{:S(2)}) copy-start(s32[2]{0:T(128)} %refs_1_.11) | copy-start | bytes 28
  50.0 3.5 %collective-permute-start.4 = (bf16[128,6144]{1,0:T(8,128)(2,1)S(1)}, bf16[128,6144]{1,0:T(8,128)(2,1)S(1)}, u32[]{:S(2)}, u32[]{:S(2)}) collective-permute-start(bf16[128,6144]{1,0:T(8,128)(2,1)S(1)} %shard_map.132.refs_1_.refs_2_), channel_id=1, source_target_pairs={{0,1},{1,0},{2,3},{3,2},{4,5},{5,4},{6,7},{7,6},{8,9},{9,8},{10,11... | collective-permute-start | bytes 4718600 | tf_op jit(solution)/shard_map/ppermute | solution.py:675
  50.1 36.9 %collective-permute-start.1 = (bf16[128,6144]{1,0:T(8,128)(2,1)S(1)}, bf16[128,6144]{1,0:T(8,128)(2,1)S(1)}, u32[]{:S(2)}, u32[]{:S(2)}) collective-permute-start(bf16[128,6144]{1,0:T(8,128)(2,1)S(1)} %shard_map.130.refs_3_.refs_0_.refs_6_), channel_id=1, source_target_pairs={{0,2},{2,0},{1,3},{3,1},{4,6},{6,4},{5,7},{7,5},{8,10},{10,8},{9,1... | collective-permute-start | bytes 4718600 | tf_op jit(solution)/shard_map/ppermute | solution.py:661
  58.7 19.2 %copy-start.21 = (bf16[2,128,1536]{2,1,0:T(8,128)(2,1)}, bf16[2,128,1536]{2,1,0:T(8,128)(2,1)S(1)}, u32[]{:S(2)}) copy-start(bf16[2,128,1536]{2,1,0:T(8,128)(2,1)S(1)} %get-tuple-element.34.refs_8_.refs_1_) | copy-start | bytes 2359300
  58.7 19.2 %collective-permute-start.5 = (bf16[2,128,1536]{2,1,0:T(8,128)(2,1)S(1)}, bf16[2,128,1536]{2,1,0:T(8,128)(2,1)S(1)}, u32[]{:S(2)}, u32[]{:S(2)}) collective-permute-start(bf16[2,128,1536]{2,1,0:T(8,128)(2,1)S(1)} %get-tuple-element.37), channel_id=1, source_target_pairs={{0,4},{1,33},{4,8},{5,37},{8,12},{9,41},{12,0},{13,45},{32,36},{33... | collective-permute-start | bytes 2359304 | tf_op jit(solution)/shard_map/ppermute | solution.py:633
  60.5 21.3 %collective-permute-start.6 = (bf16[2,128,1536]{2,1,0:T(8,128)(2,1)S(1)}, bf16[2,128,1536]{2,1,0:T(8,128)(2,1)S(1)}, u32[]{:S(2)}, u32[]{:S(2)}) collective-permute-start(bf16[2,128,1536]{2,1,0:T(8,128)(2,1)S(1)} %get-tuple-element.38), channel_id=1, source_target_pairs={{0,8},{1,65},{4,12},{5,69},{8,0},{9,73},{12,4},{13,77},{32,40},{33... | collective-permute-start | bytes 2359304 | tf_op jit(solution)/shard_map/ppermute | solution.py:633
  63.4 18.4 %collective-permute-start.7 = (bf16[2,128,1536]{2,1,0:T(8,128)(2,1)S(1)}, bf16[2,128,1536]{2,1,0:T(8,128)(2,1)S(1)}, u32[]{:S(2)}, u32[]{:S(2)}) collective-permute-start(bf16[2,128,1536]{2,1,0:T(8,128)(2,1)S(1)} %get-tuple-element.39), channel_id=1, source_target_pairs={{0,12},{1,97},{4,0},{5,101},{8,4},{9,105},{12,8},{13,109},{32,44},... | collective-permute-start | bytes 2359304 | tf_op jit(solution)/shard_map/ppermute | solution.py:633
  82.6 19.9 %copy-start.19 = (bf16[256,1024]{1,0:T(8,128)(2,1)}, bf16[256,1024]{1,0:T(8,128)(2,1)S(1)}, u32[]{:S(2)}) copy-start(bf16[256,1024]{1,0:T(8,128)(2,1)S(1)} %shard_map.135.refs_5_) | copy-start | bytes 1572868
  82.6 14.6 %collective-permute-start.10 = (bf16[256,1024]{1,0:T(8,128)(2,1)S(1)}, bf16[256,1024]{1,0:T(8,128)(2,1)S(1)}, u32[]{:S(2)}, u32[]{:S(2)}) collective-permute-start(bf16[256,1024]{1,0:T(8,128)(2,1)S(1)} %shard_map.135.refs_5_), channel_id=1, source_target_pairs={{0,12},{1,97},{4,0},{5,101},{8,4},{9,105},{12,8},{13,109},{32,44},... | collective-permute-start | bytes 1572872 | tf_op jit(solution)/shard_map/ppermute | solution.py:633
  84.8 12.4 %collective-permute-start.9 = (bf16[256,1024]{1,0:T(8,128)(2,1)S(1)}, bf16[256,1024]{1,0:T(8,128)(2,1)S(1)}, u32[]{:S(2)}, u32[]{:S(2)}) collective-permute-start(bf16[256,1024]{1,0:T(8,128)(2,1)S(1)} %shard_map.135.refs_5_), channel_id=1, source_target_pairs={{0,8},{1,65},{4,12},{5,69},{8,0},{9,73},{12,4},{13,77},{32,40},{33... | collective-permute-start | bytes 1572872 | tf_op jit(solution)/shard_map/ppermute | solution.py:633
  86.3 14.9 %collective-permute-start.8 = (bf16[256,1024]{1,0:T(8,128)(2,1)S(1)}, bf16[256,1024]{1,0:T(8,128)(2,1)S(1)}, u32[]{:S(2)}, u32[]{:S(2)}) collective-permute-start(bf16[256,1024]{1,0:T(8,128)(2,1)S(1)} %shard_map.135.refs_5_), channel_id=1, source_target_pairs={{0,4},{1,33},{4,8},{5,37},{8,12},{9,41},{12,0},{13,45},{32,36},{33... | collective-permute-start | bytes 1572872 | tf_op jit(solution)/shard_map/ppermute | solution.py:633
  86.9 15.6 %copy-start.8 = (bf16[128,6144]{1,0:T(8,128)(2,1)}, bf16[128,6144]{1,0:T(8,128)(2,1)S(1)}, u32[]{:S(2)}) copy-start(bf16[128,6144]{1,0:T(8,128)(2,1)S(1)} %collective-permute-done.1.refs_1_.refs_7_) | copy-start | bytes 4718596
  97.2 5.3 %copy-start.13 = (bf16[256,1024]{1,0:T(8,128)(2,1)}, bf16[256,1024]{1,0:T(8,128)(2,1)S(1)}, u32[]{:S(2)}) copy-start(bf16[256,1024]{1,0:T(8,128)(2,1)S(1)} %collective-permute-done.10.refs_6_.refs_8_) | copy-start | bytes 1572868
  97.2 5.3 %copy-start.15 = (bf16[256,1024]{1,0:T(8,128)(2,1)}, bf16[256,1024]{1,0:T(8,128)(2,1)S(1)}, u32[]{:S(2)}) copy-start(bf16[256,1024]{1,0:T(8,128)(2,1)S(1)} %collective-permute-done.9.refs_5_.refs_7_) | copy-start | bytes 1572868
  102.5 3.5 %collective-permute-start.11 = (bf16[128,6144]{1,0:T(8,128)(2,1)S(1)}, bf16[128,6144]{1,0:T(8,128)(2,1)S(1)}, u32[]{:S(2)}, u32[]{:S(2)}) collective-permute-start(bf16[128,6144]{1,0:T(8,128)(2,1)S(1)} %shard_map.136.refs_1_.refs_2_), channel_id=1, source_target_pairs={{0,1},{1,0},{2,3},{3,2},{4,5},{5,4},{6,7},{7,6},{8,9},{9,8},{10,11... | collective-permute-start | bytes 4718600 | tf_op jit(solution)/shard_map/ppermute | solution.py:683
  111.4 26.5 %collective-permute-start.18 = (bf16[128,6144]{1,0:T(8,128)(2,1)S(1)}, bf16[128,6144]{1,0:T(8,128)(2,1)S(1)}, u32[]{:S(2)}, u32[]{:S(2)}) collective-permute-start(bf16[128,6144]{1,0:T(8,128)(2,1)S(1)} %shard_map.140), channel_id=1, source_target_pairs={{0,1},{1,0},{2,3},{3,2},{4,5},{5,4},{6,7},{7,6},{8,9},{9,8},{10,11... | collective-permute-start | bytes 4718600 | tf_op jit(solution)/shard_map/ppermute | solution.py:667
  111.6 17.4 %collective-permute-start.12 = (bf16[2,128,1536]{2,1,0:T(8,128)(2,1)}, bf16[2,128,1536]{2,1,0:T(8,128)(2,1)S(1)}, u32[]{:S(2)}, u32[]{:S(2)}) collective-permute-start(bf16[2,128,1536]{2,1,0:T(8,128)(2,1)} %get-tuple-element.45), channel_id=1, source_target_pairs={{0,4},{1,33},{4,8},{5,37},{8,12},{9,41},{12,0},{13,45},{32,36},{33... | collective-permute-start | bytes 2359304 | tf_op jit(solution)/shard_map/ppermute | solution.py:633
  111.6 21.8 %collective-permute-start.13 = (bf16[2,128,1536]{2,1,0:T(8,128)(2,1)S(1)}, bf16[2,128,1536]{2,1,0:T(8,128)(2,1)S(1)}, u32[]{:S(2)}, u32[]{:S(2)}) collective-permute-start(bf16[2,128,1536]{2,1,0:T(8,128)(2,1)S(1)} %get-tuple-element.46), channel_id=1, source_target_pairs={{0,8},{1,65},{4,12},{5,69},{8,0},{9,73},{12,4},{13,77},{32,40},{33... | collective-permute-start | bytes 2359304 | tf_op jit(solution)/shard_map/ppermute | solution.py:633
  114.8 19.4 %collective-permute-start.14 = (bf16[2,128,1536]{2,1,0:T(8,128)(2,1)S(1)}, bf16[2,128,1536]{2,1,0:T(8,128)(2,1)S(1)}, u32[]{:S(2)}, u32[]{:S(2)}) collective-permute-start(bf16[2,128,1536]{2,1,0:T(8,128)(2,1)S(1)} %get-tuple-element.47), channel_id=1, source_target_pairs={{0,12},{1,97},{4,0},{5,101},{8,4},{9,105},{12,8},{13,109},{32,44},... | collective-permute-start | bytes 2359304 | tf_op jit(solution)/shard_map/ppermute | solution.py:633
  134.1 5.4 %collective-permute-start.19 = (bf16[128,6144]{1,0:T(8,128)(2,1)S(1)}, bf16[128,6144]{1,0:T(8,128)(2,1)S(1)}, u32[]{:S(2)}, u32[]{:S(2)}) collective-permute-start(bf16[128,6144]{1,0:T(8,128)(2,1)S(1)} %shard_map.142), channel_id=1, source_target_pairs={{0,1},{1,0},{2,3},{3,2},{4,5},{5,4},{6,7},{7,6},{8,9},{9,8},{10,11... | collective-permute-start | bytes 4718600 | tf_op jit(solution)/shard_map/ppermute | solution.py:667
  135.0 16.3 %collective-permute-start.17 = (bf16[256,1024]{1,0:T(8,128)(2,1)S(1)}, bf16[256,1024]{1,0:T(8,128)(2,1)S(1)}, u32[]{:S(2)}, u32[]{:S(2)}) collective-permute-start(bf16[256,1024]{1,0:T(8,128)(2,1)S(1)} %shard_map.139.refs_9_.refs_1_.refs_5_), channel_id=1, source_target_pairs={{0,12},{1,97},{4,0},{5,101},{8,4},{9,105},{12,8},{13,109},{32,44},... | collective-permute-start | bytes 1572872 | tf_op jit(solution)/shard_map/ppermute | solution.py:633
  136.8 14.5 %collective-permute-start.16 = (bf16[256,1024]{1,0:T(8,128)(2,1)S(1)}, bf16[256,1024]{1,0:T(8,128)(2,1)S(1)}, u32[]{:S(2)}, u32[]{:S(2)}) collective-permute-start(bf16[256,1024]{1,0:T(8,128)(2,1)S(1)} %shard_map.139.refs_9_.refs_1_.refs_5_), channel_id=1, source_target_pairs={{0,8},{1,65},{4,12},{5,69},{8,0},{9,73},{12,4},{13,77},{32,40},{33... | collective-permute-start | bytes 1572872 | tf_op jit(solution)/shard_map/ppermute | solution.py:633
  137.1 15.9 %collective-permute-start.15 = (bf16[256,1024]{1,0:T(8,128)(2,1)S(1)}, bf16[256,1024]{1,0:T(8,128)(2,1)S(1)}, u32[]{:S(2)}, u32[]{:S(2)}) collective-permute-start(bf16[256,1024]{1,0:T(8,128)(2,1)S(1)} %shard_map.139.refs_9_.refs_1_.refs_5_), channel_id=1, source_target_pairs={{0,4},{1,33},{4,8},{5,37},{8,12},{9,41},{12,0},{13,45},{32,36},{33... | collective-permute-start | bytes 1572872 | tf_op jit(solution)/shard_map/ppermute | solution.py:633
  138.2 14.8 %copy-start.2 = (bf16[128,6144]{1,0:T(8,128)(2,1)}, bf16[128,6144]{1,0:T(8,128)(2,1)S(1)}, u32[]{:S(2)}) copy-start(bf16[128,6144]{1,0:T(8,128)(2,1)S(1)} %add_convert_fusion.1.refs_10_.refs_4_) | copy-start | bytes 4718596
  138.2 38.9 %collective-permute-start.25 = (bf16[128,6144]{1,0:T(8,128)(2,1)S(1)}, bf16[128,6144]{1,0:T(8,128)(2,1)S(1)}, u32[]{:S(2)}, u32[]{:S(2)}) collective-permute-start(bf16[128,6144]{1,0:T(8,128)(2,1)S(1)} %add_convert_fusion.1.refs_10_.refs_4_), channel_id=1, source_target_pairs={{2,0},{3,1},{6,4},{7,5},{10,8},{11,9},{14,12},{15,13},{18,16},{19,... | collective-permute-start | bytes 4718600 | tf_op jit(solution)/shard_map/ppermute | solution.py:694
  139.6 5.7 %copy-start.12 = (bf16[2,128,1536]{2,1,0:T(8,128)(2,1)S(1)}, bf16[2,128,1536]{2,1,0:T(8,128)(2,1)}, u32[]{:S(2)}) copy-start(bf16[2,128,1536]{2,1,0:T(8,128)(2,1)} %copy-done.11) | copy-start | bytes 2359300
  139.6 5.7 %copy-start.14 = (bf16[256,1024]{1,0:T(8,128)(2,1)S(1)}, bf16[256,1024]{1,0:T(8,128)(2,1)}, u32[]{:S(2)}) copy-start(bf16[256,1024]{1,0:T(8,128)(2,1)} %copy-done.13) | copy-start | bytes 1572868
  139.6 5.7 %copy-start.16 = (bf16[256,1024]{1,0:T(8,128)(2,1)S(1)}, bf16[256,1024]{1,0:T(8,128)(2,1)}, u32[]{:S(2)}) copy-start(bf16[256,1024]{1,0:T(8,128)(2,1)} %copy-done.15) | copy-start | bytes 1572868
  139.6 5.7 %copy-start.18 = (bf16[256,1024]{1,0:T(8,128)(2,1)S(1)}, bf16[256,1024]{1,0:T(8,128)(2,1)}, u32[]{:S(2)}) copy-start(bf16[256,1024]{1,0:T(8,128)(2,1)} %copy-done.17) | copy-start | bytes 1572868
  139.6 5.7 %copy-start.20 = (bf16[256,1024]{1,0:T(8,128)(2,1)S(1)}, bf16[256,1024]{1,0:T(8,128)(2,1)}, u32[]{:S(2)}) copy-start(bf16[256,1024]{1,0:T(8,128)(2,1)} %copy-done.19) | copy-start | bytes 1572868
  139.6 5.7 %copy-start.22 = (bf16[2,128,1536]{2,1,0:T(8,128)(2,1)S(1)}, bf16[2,128,1536]{2,1,0:T(8,128)(2,1)}, u32[]{:S(2)}) copy-start(bf16[2,128,1536]{2,1,0:T(8,128)(2,1)} %copy-done.21) | copy-start | bytes 2359300
  140.0 13.1 %copy-start.5 = (bf16[128,6144]{1,0:T(8,128)(2,1)}, bf16[128,6144]{1,0:T(8,128)(2,1)S(1)}, u32[]{:S(2)}) copy-start(bf16[128,6144]{1,0:T(8,128)(2,1)S(1)} %add_convert_fusion.refs_11_.refs_8_) | copy-start | bytes 4718596
  140.0 43.4 %collective-permute-start.24 = (bf16[128,6144]{1,0:T(8,128)(2,1)S(1)}, bf16[128,6144]{1,0:T(8,128)(2,1)S(1)}, u32[]{:S(2)}, u32[]{:S(2)}) collective-permute-start(bf16[128,6144]{1,0:T(8,128)(2,1)S(1)} %add_convert_fusion.refs_11_.refs_8_), channel_id=1, source_target_pairs={{0,2},{1,3},{4,6},{5,7},{8,10},{9,11},{12,14},{13,15},{16,18},{17,... | collective-permute-start | bytes 4718600 | tf_op jit(solution)/shard_map/ppermute | solution.py:695
  159.4 9.9 %collective-permute-start.20 = (bf16[192,1024]{1,0:T(8,128)(2,1)S(1)}, bf16[192,1024]{1,0:T(8,128)(2,1)S(1)}, u32[]{:S(2)}, u32[]{:S(2)}) collective-permute-start(bf16[192,1024]{1,0:T(8,128)(2,1)S(1)} %get-tuple-element.54), channel_id=1, source_target_pairs={{0,32},{1,5},{4,36},{5,9},{8,40},{9,13},{12,44},{13,1},{32,64},{33... | collective-permute-start | bytes 1179656 | tf_op jit(solution)/shard_map/ppermute | solution.py:633
  161.4 7.9 %collective-permute-start.21 = (bf16[192,1024]{1,0:T(8,128)(2,1)S(1)}, bf16[192,1024]{1,0:T(8,128)(2,1)S(1)}, u32[]{:S(2)}, u32[]{:S(2)}) collective-permute-start(bf16[192,1024]{1,0:T(8,128)(2,1)S(1)} %get-tuple-element.56), channel_id=1, source_target_pairs={{0,96},{1,13},{4,100},{5,1},{8,104},{9,5},{12,108},{13,9},{32,0},{... | collective-permute-start | bytes 1179656 | tf_op jit(solution)/shard_map/ppermute | solution.py:633
  169.5 13.3 %collective-permute-start.22 = (bf16[384,1024]{1,0:T(8,128)(2,1)S(1)}, bf16[384,1024]{1,0:T(8,128)(2,1)S(1)}, u32[]{:S(2)}, u32[]{:S(2)}) collective-permute-start(bf16[384,1024]{1,0:T(8,128)(2,1)S(1)} %get-tuple-element.57), channel_id=1, source_target_pairs={{0,32},{1,5},{4,36},{5,9},{8,40},{9,13},{12,44},{13,1},{32,64},{33... | collective-permute-start | bytes 2359304 | tf_op jit(solution)/shard_map/ppermute | solution.py:633
  171.4 12.0 %collective-permute-start.23 = (bf16[384,1024]{1,0:T(8,128)(2,1)S(1)}, bf16[384,1024]{1,0:T(8,128)(2,1)S(1)}, u32[]{:S(2)}, u32[]{:S(2)}) collective-permute-start(bf16[384,1024]{1,0:T(8,128)(2,1)S(1)} %get-tuple-element.58), channel_id=1, source_target_pairs={{0,96},{1,13},{4,100},{5,1},{8,104},{9,5},{12,108},{13,9},{32,0},{... | collective-permute-start | bytes 2359304 | tf_op jit(solution)/shard_map/ppermute | solution.py:633
  177.1 7.1 %copy-start.9 = (bf16[128,6144]{1,0:T(8,128)(2,1)}, bf16[128,6144]{1,0:T(8,128)(2,1)S(1)}, u32[]{:S(2)}) copy-start(bf16[128,6144]{1,0:T(8,128)(2,1)S(1)} %collective-permute-done.25.refs_5_) | copy-start | bytes 4718596
  184.6 9.7 %collective-permute-start.26 = (bf16[192,1024]{1,0:T(8,128)(2,1)S(1)}, bf16[192,1024]{1,0:T(8,128)(2,1)S(1)}, u32[]{:S(2)}, u32[]{:S(2)}) collective-permute-start(bf16[192,1024]{1,0:T(8,128)(2,1)S(1)} %get-tuple-element.60), channel_id=1, source_target_pairs={{0,16},{16,0},{1,17},{17,1},{2,18},{18,2},{3,19},{19,3},{4,20},{20... | collective-permute-start | bytes 1179656 | tf_op jit(solution)/shard_map/ppermute | solution.py:709
  (9 other events, 21.5 us)

commit v2 on v1

--- a/solution.py
+++ b/solution.py
@@ -282,6 +282,7 @@
         [shape((rows, width // 2), F32)] * 2,
         [half, half],
         after=after,
+        mib=60,
         cost_estimate=cost(0, 10 * rows * width),
     )
 
@@ -676,10 +677,10 @@
     pieces = strips(where, own, far, [])
     lefts = spread(pieces[0], pieces)
     *texts, near_rows, away_rows, grads = step(0, own, far, [], [pieces[0]])
-    grads = later(grads, lefts[1:])
+    grads = later(grads, [lefts[1], lefts[3]])
     rights = spread(grads, [grads] * RING)
 
-    own = norm(mine[1], other[1], gain, [near_rows, *rights[1:]])
+    own = norm(mine[1], other[1], gain, [near_rows, lefts[2], *rights[1:]])
     far = lax.ppermute(own, "c", SWAP)
     pieces = strips(where, own, far, [])
     last_lefts = spread(pieces[0], pieces)

time: 198 us -> 197 us (level)
  waiting for transfers between devices: 80.3 us -> 78 us
    ppermute x16, waiting for transfers between devices: 36.8 us -> 31.6 us  [rotate(): return lax.ppermute(array, ('z', 'y', 'c'), hop(first, distance))]
    ppermute x2, waiting for transfers between devices: 33.6 us -> 35.8 us  [local(): other.append(lax.ppermute(mine[image], 'xl', SWAP))]
    unnamed x60 -> x62, local copies, waits for them, and re-layouts: 6.05 us -> 4.94 us
where the time goes in v2:
time: 197 us
  waiting for transfers between devices  78 us (40%)
  Pallas kernels  69.8 us (35%)
  starting transfers between devices  41.3 us (21%)
  local copies, waits for them, and re-layouts  5.59 us (3%)
    pallas_call x20, Pallas kernels, call(): pl.pallas_call(with_waits, grid_spec=pltpu.PrefetchScalarGridSpec(num_sca...  69.8 us
    ppermute x2, waiting for transfers between devices, local(): other.append(lax.ppermute(mine[image], 'xl', SWAP))  35.8 us
    ppermute x16, waiting for transfers between devices, rotate(): return lax.ppermute(array, ('z', 'y', 'c'), hop(first, distance))  31.6 us
    ppermute x16, starting transfers between devices, rotate(): return lax.ppermute(array, ('z', 'y', 'c'), hop(first, distance))  26.6 us
    ppermute x1, starting transfers between devices, local(): from_first = lax.ppermute(share_1, 'xl', [(0, 1)])  5.23 us
    ppermute x2, waiting for transfers between devices, local(): far = lax.ppermute(own, 'c', SWAP)  5.14 us
    unnamed x62, local copies, waits for them, and re-layouts  4.94 us
    ppermute x1, waiting for transfers between devices, local(): from_second = lax.ppermute(share_0, 'xl', [(1, 0)])  4.35 us
  transfers between devices with their start and end apart: 27, of which 15 were waited for; matrix products, arithmetic and copies ran while one was open for 0% of the time, Pallas kernels for 28%

profile of v2, /device:TPU:0, one launch (start us, length us, event | category | flops | bytes accessed | tf_op | source)
XLA Modules:
  0.0 196.6 jit_solution(9859301289911567161)
XLA Ops:
  1.3 2.9 %shard_map.128.refs_3_ = bf16[128,6144]{1,0:T(8,128)(2,1)} custom-call(s32[5]{0:T(128)} %stack.23.refs_0_, bf16[1,512,6144]{2,1,0:T(8,128)(2,1)} %refs_1_.9, bf16[128,6144]{1,0:T(8,128)(2,1)} %refs_3_.3), custom_call_target="tpu_custom_call" | custom-call | tf_op jit(solution)/shard_map/pallas_call | solution.py:39
  4.3 3.0 %shard_map.129 = bf16[128,6144]{1,0:T(8,128)(2,1)} custom-call(s32[5]{0:T(128)} %stack.23.refs_0_, bf16[1,512,6144]{2,1,0:T(8,128)(2,1)} %refs_1_.9, bf16[128,6144]{1,0:T(8,128)(2,1)} %refs_3_.3, bf16[128,6144]{1,0:T(8,128)(2,1)} %shard_map.128.refs_3_), custom_call_target="tpu_custom_call" | custom-call | tf_op jit(solution)/shard_map/pallas_call | solution.py:39
  7.9 2.8 %copy-done = bf16[1,512,6144]{2,1,0:T(8,128)(2,1)S(1)} copy-done((bf16[1,512,6144]{2,1,0:T(8,128)(2,1)S(1)}, bf16[1,512,6144]{2,1,0:T(8,128)(2,1)}, u32[]{:S(2)}) %copy-start) | copy-done | bytes 6291480
  10.7 1.3 shard_map.131.refs_0_.refs_2_
  12.0 1.7 collective-permute-start.3
  13.7 1.3 shard_map.130.refs_3_.refs_0_.refs_6_
  15.0 33.6 %collective-permute-done.3.refs_1_.refs_3_ = bf16[128,6144]{1,0:T(8,128)(2,1)S(1)} collective-permute-done((bf16[128,6144]{1,0:T(8,128)(2,1)S(1)}, bf16[128,6144]{1,0:T(8,128)(2,1)S(1)}, u32[]{:S(2)}, u32[]{:S(2)}) %collective-permute-start.3) | collective-permute-done | bytes 1572896 | tf_op jit(solution)/shard_map/ppermute | solution.py:662
  48.5 1.4 shard_map.132.refs_1_.refs_2_
  50.0 1.7 collective-permute-start.1
  51.7 1.7 collective-permute-done.4.refs_2_.refs_3_
  53.4 5.3 %shard_map.133 = (bf16[2,128,1536]{2,1,0:T(8,128)(2,1)S(1)}, bf16[2,128,1536]{2,1,0:T(8,128)(2,1)S(1)}, bf16[2,128,1536]{2,1,0:T(8,128)(2,1)S(1)}, bf16[2,128,1536]{2,1,0:T(8,128)(2,1)S(1)}) custom-call(s32[5]{0:T(128)S(1)} %copy-done.24, bf16[128,6144]{1,0:T(8,128)(2,1)S(1)} %shard_map.132.refs_1_.refs_2_, ...), custom_call_target="tpu_custom_call" | custom-call | bytes 6291456 | tf_op jit(solution)/shard_map/pallas_call | solution.py:39
  58.7 1.7 collective-permute-start.6
  60.5 1.6 collective-permute-start.7
  62.0 2.1 %collective-permute-start.5 = (bf16[2,128,1536]{2,1,0:T(8,128)(2,1)S(1)}, bf16[2,128,1536]{2,1,0:T(8,128)(2,1)S(1)}, u32[]{:S(2)}, u32[]{:S(2)}) collective-permute-start(bf16[2,128,1536]{2,1,0:T(8,128)(2,1)S(1)} %get-tuple-element.36), channel_id=1, source_target_pairs={{0,8},{1,65},{4,12},{5,69},{8,0},{9,73},{12,4},{13,77},{32,40},{33... | collective-permute-start | bytes 2359304 | tf_op jit(solution)/shard_map/ppermute | solution.py:634
  64.1 13.2 %shard_map.134 = (f32[2,512,512]{2,1,0:T(8,128)}, f32[2,512,512]{2,1,0:T(8,128)}, bf16[128,6144]{1,0:T(8,128)(2,1)S(1)}, bf16[128,6144]{1,0:T(8,128)(2,1)S(1)}, bf16[256,1024]{1,0:T(8,128)(2,1)S(1)}) custom-call(s32[2]{0:T(128)S(1)} %bitcast.10, s32[2]{0:T(128)S(1)} %copy-done.29, bf16[128,6144]{1,0:T(8,128)(2,1)S(1)} %shard_map.132.refs_1_.refs_2_, ...), custom_call_target="tpu_custom_call" | custom-call | flops 7247757312 | bytes 22020096 | tf_op jit(solution)/shard_map/pallas_call | solution.py:39
  77.4 6.2 %collective-permute-start.10 = (bf16[256,1024]{1,0:T(8,128)(2,1)S(1)}, bf16[256,1024]{1,0:T(8,128)(2,1)S(1)}, u32[]{:S(2)}, u32[]{:S(2)}) collective-permute-start(bf16[256,1024]{1,0:T(8,128)(2,1)S(1)} %shard_map.135.refs_5_), channel_id=1, source_target_pairs={{0,12},{1,97},{4,0},{5,101},{8,4},{9,105},{12,8},{13,109},{32,44},... | collective-permute-start | bytes 1572872 | tf_op jit(solution)/shard_map/ppermute | solution.py:634
  83.7 0.9 collective-permute-start.8
  84.6 2.2 %collective-permute-done.1.refs_1_.refs_7_ = bf16[128,6144]{1,0:T(8,128)(2,1)S(1)} collective-permute-done((bf16[128,6144]{1,0:T(8,128)(2,1)S(1)}, bf16[128,6144]{1,0:T(8,128)(2,1)S(1)}, u32[]{:S(2)}, u32[]{:S(2)}) %collective-permute-start.1) | collective-permute-done | bytes 1572896 | tf_op jit(solution)/shard_map/ppermute | solution.py:662
  86.9 9.1 %collective-permute-done.10.refs_7_.refs_8_ = bf16[256,1024]{1,0:T(8,128)(2,1)S(1)} collective-permute-done((bf16[256,1024]{1,0:T(8,128)(2,1)S(1)}, bf16[256,1024]{1,0:T(8,128)(2,1)S(1)}, u32[]{:S(2)}, u32[]{:S(2)}) %collective-permute-start.10) | collective-permute-done | bytes 524320 | tf_op jit(solution)/shard_map/ppermute | solution.py:634
  96.0 3.7 %collective-permute-done.8.refs_5_.refs_6_ = bf16[256,1024]{1,0:T(8,128)(2,1)S(1)} collective-permute-done((bf16[256,1024]{1,0:T(8,128)(2,1)S(1)}, bf16[256,1024]{1,0:T(8,128)(2,1)S(1)}, u32[]{:S(2)}, u32[]{:S(2)}) %collective-permute-start.8) | collective-permute-done | bytes 524320 | tf_op jit(solution)/shard_map/ppermute | solution.py:634
  99.7 1.3 shard_map.136.refs_1_.refs_2_
  101.2 3.4 %collective-permute-done.11.refs_2_.refs_3_ = bf16[128,6144]{1,0:T(8,128)(2,1)S(1)} collective-permute-done((bf16[128,6144]{1,0:T(8,128)(2,1)S(1)}, bf16[128,6144]{1,0:T(8,128)(2,1)S(1)}, u32[]{:S(2)}, u32[]{:S(2)}) %collective-permute-start.11) | collective-permute-done | bytes 1572896 | tf_op jit(solution)/shard_map/ppermute | solution.py:684
  104.6 5.3 %shard_map.137 = (bf16[2,128,1536]{2,1,0:T(8,128)(2,1)S(1)}, bf16[2,128,1536]{2,1,0:T(8,128)(2,1)}, bf16[2,128,1536]{2,1,0:T(8,128)(2,1)S(1)}, bf16[2,128,1536]{2,1,0:T(8,128)(2,1)S(1)}) custom-call(s32[5]{0:T(128)S(1)} %copy-done.24, bf16[128,6144]{1,0:T(8,128)(2,1)S(1)} %shard_map.136.refs_1_.refs_2_, ...), custom_call_target="tpu_custom_call" | custom-call | bytes 6291456 | tf_op jit(solution)/shard_map/pallas_call | solution.py:39
  110.2 3.1 %collective-permute-start.13 = (bf16[2,128,1536]{2,1,0:T(8,128)(2,1)S(1)}, bf16[2,128,1536]{2,1,0:T(8,128)(2,1)S(1)}, u32[]{:S(2)}, u32[]{:S(2)}) collective-permute-start(bf16[2,128,1536]{2,1,0:T(8,128)(2,1)S(1)} %get-tuple-element.46), channel_id=1, source_target_pairs={{0,8},{1,65},{4,12},{5,69},{8,0},{9,73},{12,4},{13,77},{32,40},{33... | collective-permute-start | bytes 2359304 | tf_op jit(solution)/shard_map/ppermute | solution.py:634
  113.3 1.1 collective-permute-start.14
  114.4 13.2 %shard_map.138 = (f32[2,512,512]{2,1,0:T(8,128)}, f32[2,512,512]{2,1,0:T(8,128)}, bf16[128,6144]{1,0:T(8,128)(2,1)S(1)}, bf16[128,6144]{1,0:T(8,128)(2,1)S(1)}, bf16[256,1024]{1,0:T(8,128)(2,1)S(1)}) custom-call(s32[2]{0:T(128)S(1)} %bitcast.11, s32[2]{0:T(128)S(1)} %copy-done.29, ...), custom_call_target="tpu_custom_call", output_to_operand_aliasing={{0}: (8, {}), {1}: (9, {})} | custom-call | flops 7247757312 | bytes 22020096 | tf_op jit(solution)/shard_map/pallas_call | solution.py:39
  127.6 4.4 %collective-permute-done.13.refs_2_.refs_3_ = bf16[2,128,1536]{2,1,0:T(8,128)(2,1)S(1)} collective-permute-done((bf16[2,128,1536]{2,1,0:T(8,128)(2,1)S(1)}, bf16[2,128,1536]{2,1,0:T(8,128)(2,1)S(1)}, u32[]{:S(2)}, u32[]{:S(2)}) %collective-permute-start.13) | collective-permute-done | bytes 786464 | tf_op jit(solution)/shard_map/ppermute | solution.py:634
  132.7 0.9 collective-permute-start.19
  133.6 1.7 collective-permute-start.17
  136.6 1.3 collective-permute-start.25
  138.4 5.2 %collective-permute-start.24 = (bf16[128,6144]{1,0:T(8,128)(2,1)S(1)}, bf16[128,6144]{1,0:T(8,128)(2,1)S(1)}, u32[]{:S(2)}, u32[]{:S(2)}) collective-permute-start(bf16[128,6144]{1,0:T(8,128)(2,1)S(1)} %add_convert_fusion.refs_11_.refs_8_), channel_id=1, source_target_pairs={{0,2},{1,3},{4,6},{5,7},{8,10},{9,11},{12,14},{13,15},{16,18},{17,... | collective-permute-start | bytes 4718600 | tf_op jit(solution)/shard_map/ppermute | solution.py:696
  143.7 6.0 %shard_map.141.refs_9_ = bf16[4,384,1024]{2,1,0:T(8,128)(2,1)S(1)} custom-call(s32[5]{0:T(128)S(1)} %copy-done.24, bf16[2,128,1536]{2,1,0:T(8,128)(2,1)S(1)} %copy-done.22, bf16[2,128,1536]{2,1,0:T(8,128)(2,1)S(1)} %collective-permute-done.6.refs_1_.refs_2_, bf16[2,128,1536]{2,1,0:T(8,128)(2,1)S(1)} %collective-permute-done.5.refs_4_.refs_3_, ...), custom_call_target="tpu_custom_call" | custom-call | tf_op jit(solution)/shard_map/pallas_call | solution.py:39
  149.7 1.9 collective-permute-done.15.refs_6_
  151.6 6.3 %shard_map.143 = (bf16[384,1024]{1,0:T(8,128)(2,1)S(1)}, bf16[384,1024]{1,0:T(8,128)(2,1)S(1)}, bf16[192,1024]{1,0:T(8,128)(2,1)S(1)}, bf16[192,1024]{1,0:T(8,128)(2,1)S(1)}, bf16[384,1024]{1,0:T(8,128)(2,1)S(1)}) custom-call(s32[5]{0:T(128)S(1)} %copy-done.24, bf16[2,128,1536]{2,1,0:T(8,128)(2,1)S(1)} %get-tuple-element.42.refs_10_.refs_1_, ...), custom_call_target="tpu_custom_call" | custom-call | tf_op jit(solution)/shard_map/pallas_call | solution.py:39
  158.0 1.5 collective-permute-start.20
  159.4 2.2 %collective-permute-start.21 = (bf16[192,1024]{1,0:T(8,128)(2,1)S(1)}, bf16[192,1024]{1,0:T(8,128)(2,1)S(1)}, u32[]{:S(2)}, u32[]{:S(2)}) collective-permute-start(bf16[192,1024]{1,0:T(8,128)(2,1)S(1)} %get-tuple-element.56), channel_id=1, source_target_pairs={{0,96},{1,13},{4,100},{5,1},{8,104},{9,5},{12,108},{13,9},{32,0},{... | collective-permute-start | bytes 1179656 | tf_op jit(solution)/shard_map/ppermute | solution.py:634
  161.7 5.7 %collective-permute-done.20.refs_1_ = bf16[192,1024]{1,0:T(8,128)(2,1)S(1)} collective-permute-done((bf16[192,1024]{1,0:T(8,128)(2,1)S(1)}, bf16[192,1024]{1,0:T(8,128)(2,1)S(1)}, u32[]{:S(2)}, u32[]{:S(2)}) %collective-permute-start.20) | collective-permute-done | bytes 393248 | tf_op jit(solution)/shard_map/ppermute | solution.py:634
  167.5 1.9 collective-permute-start.22
  169.4 1.6 collective-permute-start.23
  171.0 4.4 %collective-permute-done.25.refs_5_ = bf16[128,6144]{1,0:T(8,128)(2,1)S(1)} collective-permute-done((bf16[128,6144]{1,0:T(8,128)(2,1)S(1)}, bf16[128,6144]{1,0:T(8,128)(2,1)S(1)}, u32[]{:S(2)}, u32[]{:S(2)}) %collective-permute-start.25) | collective-permute-done | bytes 1572896 | tf_op jit(solution)/shard_map/ppermute | solution.py:695
  175.4 5.5 %collective-permute-done.22.refs_2_ = bf16[384,1024]{1,0:T(8,128)(2,1)S(1)} collective-permute-done((bf16[384,1024]{1,0:T(8,128)(2,1)S(1)}, bf16[384,1024]{1,0:T(8,128)(2,1)S(1)}, u32[]{:S(2)}, u32[]{:S(2)}) %collective-permute-start.22) | collective-permute-done | bytes 786464 | tf_op jit(solution)/shard_map/ppermute | solution.py:634
  181.4 0.8 shard_map.145
  182.7 0.9 copy-done.20
  183.5 3.0 %collective-permute-start.26 = (bf16[192,1024]{1,0:T(8,128)(2,1)S(1)}, bf16[192,1024]{1,0:T(8,128)(2,1)S(1)}, u32[]{:S(2)}, u32[]{:S(2)}) collective-permute-start(bf16[192,1024]{1,0:T(8,128)(2,1)S(1)} %get-tuple-element.60), channel_id=1, source_target_pairs={{0,16},{16,0},{1,17},{17,1},{2,18},{18,2},{3,19},{19,3},{4,20},{20... | collective-permute-start | bytes 1179656 | tf_op jit(solution)/shard_map/ppermute | solution.py:710
  186.6 6.1 %shard_map.146.refs_2_ = f32[128,6144]{1,0:T(8,128)} custom-call(s32[5]{0:T(128)} %stack.23.refs_0_, f32[1,6144]{1,0:T(1,128)} %bitcast.7, bf16[128,6144]{1,0:T(8,128)(2,1)} %copy-done.4, bf16[128,6144]{1,0:T(8,128)(2,1)} %copy-done.7, bf16[128,6144]{1,0:T(8,128)(2,1)} %copy-done.2, bf16[128,6144]{1,0:T(8,128)(2,1)} %copy-done.8, ...), custom_call_target="tpu_custom_call" | custom-call | bytes 9437184 | tf_op jit(solution)/shard_map/pallas_call | solution.py:39
  192.7 1.0 collective-permute-done.26.refs_1_
  193.7 0.8 copy-done.30
  194.5 2.1 %shard_map.147 = (f32[192,512]{1,0:T(8,128)}, f32[192,512]{1,0:T(8,128)}) custom-call(f32[192,1024]{1,0:T(8,128)} %copy-done.20, bf16[192,1024]{1,0:T(8,128)(2,1)} %copy-done.30, f32[128,6144]{1,0:T(8,128)} %shard_map.146.refs_2_), custom_call_target="tpu_custom_call" | custom-call | bytes 1966080 | tf_op jit(solution)/shard_map/pallas_call | solution.py:39
  (91 shorter events, 5.5 us)
Async XLA Ops:
  4.2 3.7 %collective-permute-start.2 = (bf16[128,6144]{1,0:T(8,128)(2,1)}, bf16[128,6144]{1,0:T(8,128)(2,1)S(1)}, u32[]{:S(2)}, u32[]{:S(2)}) collective-permute-start(bf16[128,6144]{1,0:T(8,128)(2,1)} %shard_map.128.refs_3_), channel_id=1, source_target_pairs={{0,1},{1,0},{2,3},{3,2},{4,5},{5,4},{6,7},{7,6},{8,9},{9,8},{10,11... | collective-permute-start | bytes 4718600 | tf_op jit(solution)/shard_map/ppermute | solution.py:660
  7.3 6.4 %collective-permute-start = (bf16[128,6144]{1,0:T(8,128)(2,1)}, bf16[128,6144]{1,0:T(8,128)(2,1)S(1)}, u32[]{:S(2)}, u32[]{:S(2)}) collective-permute-start(bf16[128,6144]{1,0:T(8,128)(2,1)} %shard_map.129), channel_id=1, source_target_pairs={{0,1},{1,0},{2,3},{3,2},{4,5},{5,4},{6,7},{7,6},{8,9},{9,8},{10,11... | collective-permute-start | bytes 4718600 | tf_op jit(solution)/shard_map/ppermute | solution.py:660
  12.0 36.5 %copy-start.4 = (bf16[128,6144]{1,0:T(8,128)(2,1)}, bf16[128,6144]{1,0:T(8,128)(2,1)S(1)}, u32[]{:S(2)}) copy-start(bf16[128,6144]{1,0:T(8,128)(2,1)S(1)} %shard_map.131.refs_0_.refs_2_) | copy-start | bytes 4718596
  12.0 36.5 %copy-start.23 = (f32[6144]{0:T(1024)S(1)}, f32[6144]{0:T(1024)}, u32[]{:S(2)}) copy-start(f32[6144]{0:T(1024)} %param.11) | copy-start | bytes 73732
  12.0 36.5 %collective-permute-start.3 = (bf16[128,6144]{1,0:T(8,128)(2,1)S(1)}, bf16[128,6144]{1,0:T(8,128)(2,1)S(1)}, u32[]{:S(2)}, u32[]{:S(2)}) collective-permute-start(bf16[128,6144]{1,0:T(8,128)(2,1)S(1)} %shard_map.131.refs_0_.refs_2_), channel_id=1, source_target_pairs={{0,2},{2,0},{1,3},{3,1},{4,6},{6,4},{5,7},{7,5},{8,10},{10,8},{9,1... | collective-permute-start | bytes 4718600 | tf_op jit(solution)/shard_map/ppermute | solution.py:662
  15.0 84.7 %copy-start.1 = (bf16[128,6144]{1,0:T(8,128)(2,1)}, bf16[128,6144]{1,0:T(8,128)(2,1)S(1)}, u32[]{:S(2)}) copy-start(bf16[128,6144]{1,0:T(8,128)(2,1)S(1)} %shard_map.130.refs_3_.refs_0_.refs_6_) | copy-start | bytes 4718596
  49.9 14.2 %copy-start.25 = (bf16[2,512,512]{2,1,0:T(8,128)(2,1)S(1)}, bf16[2,512,512]{2,1,0:T(8,128)(2,1)}, u32[]{:S(2)}) copy-start(bf16[2,512,512]{2,1,0:T(8,128)(2,1)} %refs_6_.3) | copy-start | bytes 3145732
  49.9 14.2 %copy-start.26 = (bf16[2,512,512]{2,1,0:T(8,128)(2,1)S(1)}, bf16[2,512,512]{2,1,0:T(8,128)(2,1)}, u32[]{:S(2)}) copy-start(bf16[2,512,512]{2,1,0:T(8,128)(2,1)} %refs_7_.3) | copy-start | bytes 3145732
  49.9 14.2 %copy-start.28 = (s32[1,2]{1,0:T(1,128)S(1)}, s32[1,2]{1,0:T(1,128)}, u32[]{:S(2)}) copy-start(s32[1,2]{1,0:T(1,128)} %param.17) | copy-start | bytes 28
  49.9 14.2 %copy-start.29 = (s32[2]{0:T(128)S(1)}, s32[2]{0:T(128)}, u32[]{:S(2)}) copy-start(s32[2]{0:T(128)} %refs_1_.11) | copy-start | bytes 28
  50.0 3.5 %collective-permute-start.4 = (bf16[128,6144]{1,0:T(8,128)(2,1)S(1)}, bf16[128,6144]{1,0:T(8,128)(2,1)S(1)}, u32[]{:S(2)}, u32[]{:S(2)}) collective-permute-start(bf16[128,6144]{1,0:T(8,128)(2,1)S(1)} %shard_map.132.refs_1_.refs_2_), channel_id=1, source_target_pairs={{0,1},{1,0},{2,3},{3,2},{4,5},{5,4},{6,7},{7,6},{8,9},{9,8},{10,11... | collective-permute-start | bytes 4718600 | tf_op jit(solution)/shard_map/ppermute | solution.py:676
  50.0 36.8 %collective-permute-start.1 = (bf16[128,6144]{1,0:T(8,128)(2,1)S(1)}, bf16[128,6144]{1,0:T(8,128)(2,1)S(1)}, u32[]{:S(2)}, u32[]{:S(2)}) collective-permute-start(bf16[128,6144]{1,0:T(8,128)(2,1)S(1)} %shard_map.130.refs_3_.refs_0_.refs_6_), channel_id=1, source_target_pairs={{0,2},{2,0},{1,3},{3,1},{4,6},{6,4},{5,7},{7,5},{8,10},{10,8},{9,1... | collective-permute-start | bytes 4718600 | tf_op jit(solution)/shard_map/ppermute | solution.py:662
  58.7 18.6 %copy-start.21 = (bf16[2,128,1536]{2,1,0:T(8,128)(2,1)}, bf16[2,128,1536]{2,1,0:T(8,128)(2,1)S(1)}, u32[]{:S(2)}) copy-start(bf16[2,128,1536]{2,1,0:T(8,128)(2,1)S(1)} %get-tuple-element.34.refs_8_.refs_1_) | copy-start | bytes 2359300
  58.7 18.6 %collective-permute-start.6 = (bf16[2,128,1536]{2,1,0:T(8,128)(2,1)S(1)}, bf16[2,128,1536]{2,1,0:T(8,128)(2,1)S(1)}, u32[]{:S(2)}, u32[]{:S(2)}) collective-permute-start(bf16[2,128,1536]{2,1,0:T(8,128)(2,1)S(1)} %get-tuple-element.38), channel_id=1, source_target_pairs={{0,4},{1,33},{4,8},{5,37},{8,12},{9,41},{12,0},{13,45},{32,36},{33... | collective-permute-start | bytes 2359304 | tf_op jit(solution)/shard_map/ppermute | solution.py:634
  60.5 16.9 %collective-permute-start.7 = (bf16[2,128,1536]{2,1,0:T(8,128)(2,1)S(1)}, bf16[2,128,1536]{2,1,0:T(8,128)(2,1)S(1)}, u32[]{:S(2)}, u32[]{:S(2)}) collective-permute-start(bf16[2,128,1536]{2,1,0:T(8,128)(2,1)S(1)} %get-tuple-element.39), channel_id=1, source_target_pairs={{0,12},{1,97},{4,0},{5,101},{8,4},{9,105},{12,8},{13,109},{32,44},... | collective-permute-start | bytes 2359304 | tf_op jit(solution)/shard_map/ppermute | solution.py:634
  62.0 24.8 %collective-permute-start.5 = (bf16[2,128,1536]{2,1,0:T(8,128)(2,1)S(1)}, bf16[2,128,1536]{2,1,0:T(8,128)(2,1)S(1)}, u32[]{:S(2)}, u32[]{:S(2)}) collective-permute-start(bf16[2,128,1536]{2,1,0:T(8,128)(2,1)S(1)} %get-tuple-element.36), channel_id=1, source_target_pairs={{0,8},{1,65},{4,12},{5,69},{8,0},{9,73},{12,4},{13,77},{32,40},{33... | collective-permute-start | bytes 2359304 | tf_op jit(solution)/shard_map/ppermute | solution.py:634
  77.4 23.7 %copy-start.10 = (bf16[2,128,1536]{2,1,0:T(8,128)(2,1)}, bf16[2,128,1536]{2,1,0:T(8,128)(2,1)S(1)}, u32[]{:S(2)}) copy-start(bf16[2,128,1536]{2,1,0:T(8,128)(2,1)S(1)} %collective-permute-done.7.refs_2_.refs_4_) | copy-start | bytes 2359300
  77.4 23.6 %copy-start.18 = (bf16[256,1024]{1,0:T(8,128)(2,1)}, bf16[256,1024]{1,0:T(8,128)(2,1)S(1)}, u32[]{:S(2)}) copy-start(bf16[256,1024]{1,0:T(8,128)(2,1)S(1)} %shard_map.135.refs_5_) | copy-start | bytes 1572868
  77.4 18.6 %collective-permute-start.10 = (bf16[256,1024]{1,0:T(8,128)(2,1)S(1)}, bf16[256,1024]{1,0:T(8,128)(2,1)S(1)}, u32[]{:S(2)}, u32[]{:S(2)}) collective-permute-start(bf16[256,1024]{1,0:T(8,128)(2,1)S(1)} %shard_map.135.refs_5_), channel_id=1, source_target_pairs={{0,12},{1,97},{4,0},{5,101},{8,4},{9,105},{12,8},{13,109},{32,44},... | collective-permute-start | bytes 1572872 | tf_op jit(solution)/shard_map/ppermute | solution.py:634
  83.7 12.3 %collective-permute-start.9 = (bf16[256,1024]{1,0:T(8,128)(2,1)S(1)}, bf16[256,1024]{1,0:T(8,128)(2,1)S(1)}, u32[]{:S(2)}, u32[]{:S(2)}) collective-permute-start(bf16[256,1024]{1,0:T(8,128)(2,1)S(1)} %shard_map.135.refs_5_), channel_id=1, source_target_pairs={{0,8},{1,65},{4,12},{5,69},{8,0},{9,73},{12,4},{13,77},{32,40},{33... | collective-permute-start | bytes 1572872 | tf_op jit(solution)/shard_map/ppermute | solution.py:634
  83.7 16.0 %collective-permute-start.8 = (bf16[256,1024]{1,0:T(8,128)(2,1)S(1)}, bf16[256,1024]{1,0:T(8,128)(2,1)S(1)}, u32[]{:S(2)}, u32[]{:S(2)}) collective-permute-start(bf16[256,1024]{1,0:T(8,128)(2,1)S(1)} %shard_map.135.refs_5_), channel_id=1, source_target_pairs={{0,4},{1,33},{4,8},{5,37},{8,12},{9,41},{12,0},{13,45},{32,36},{33... | collective-permute-start | bytes 1572872 | tf_op jit(solution)/shard_map/ppermute | solution.py:634
  86.9 14.2 %copy-start.6 = (bf16[128,6144]{1,0:T(8,128)(2,1)}, bf16[128,6144]{1,0:T(8,128)(2,1)S(1)}, u32[]{:S(2)}) copy-start(bf16[128,6144]{1,0:T(8,128)(2,1)S(1)} %collective-permute-done.1.refs_1_.refs_7_) | copy-start | bytes 4718596
  96.0 5.1 %copy-start.14 = (bf16[256,1024]{1,0:T(8,128)(2,1)}, bf16[256,1024]{1,0:T(8,128)(2,1)S(1)}, u32[]{:S(2)}) copy-start(bf16[256,1024]{1,0:T(8,128)(2,1)S(1)} %collective-permute-done.9.refs_6_.refs_7_) | copy-start | bytes 1572868
  101.1 3.5 %collective-permute-start.11 = (bf16[128,6144]{1,0:T(8,128)(2,1)S(1)}, bf16[128,6144]{1,0:T(8,128)(2,1)S(1)}, u32[]{:S(2)}, u32[]{:S(2)}) collective-permute-start(bf16[128,6144]{1,0:T(8,128)(2,1)S(1)} %shard_map.136.refs_1_.refs_2_), channel_id=1, source_target_pairs={{0,1},{1,0},{2,3},{3,2},{4,5},{5,4},{6,7},{7,6},{8,9},{9,8},{10,11... | collective-permute-start | bytes 4718600 | tf_op jit(solution)/shard_map/ppermute | solution.py:684
  109.9 26.3 %collective-permute-start.18 = (bf16[128,6144]{1,0:T(8,128)(2,1)S(1)}, bf16[128,6144]{1,0:T(8,128)(2,1)S(1)}, u32[]{:S(2)}, u32[]{:S(2)}) collective-permute-start(bf16[128,6144]{1,0:T(8,128)(2,1)S(1)} %shard_map.140), channel_id=1, source_target_pairs={{0,1},{1,0},{2,3},{3,2},{4,5},{5,4},{6,7},{7,6},{8,9},{9,8},{10,11... | collective-permute-start | bytes 4718600 | tf_op jit(solution)/shard_map/ppermute | solution.py:668
  110.1 17.4 %collective-permute-start.12 = (bf16[2,128,1536]{2,1,0:T(8,128)(2,1)}, bf16[2,128,1536]{2,1,0:T(8,128)(2,1)S(1)}, u32[]{:S(2)}, u32[]{:S(2)}) collective-permute-start(bf16[2,128,1536]{2,1,0:T(8,128)(2,1)} %get-tuple-element.45), channel_id=1, source_target_pairs={{0,4},{1,33},{4,8},{5,37},{8,12},{9,41},{12,0},{13,45},{32,36},{33... | collective-permute-start | bytes 2359304 | tf_op jit(solution)/shard_map/ppermute | solution.py:634
  110.2 21.7 %collective-permute-start.13 = (bf16[2,128,1536]{2,1,0:T(8,128)(2,1)S(1)}, bf16[2,128,1536]{2,1,0:T(8,128)(2,1)S(1)}, u32[]{:S(2)}, u32[]{:S(2)}) collective-permute-start(bf16[2,128,1536]{2,1,0:T(8,128)(2,1)S(1)} %get-tuple-element.46), channel_id=1, source_target_pairs={{0,8},{1,65},{4,12},{5,69},{8,0},{9,73},{12,4},{13,77},{32,40},{33... | collective-permute-start | bytes 2359304 | tf_op jit(solution)/shard_map/ppermute | solution.py:634
  113.3 19.4 %collective-permute-start.14 = (bf16[2,128,1536]{2,1,0:T(8,128)(2,1)S(1)}, bf16[2,128,1536]{2,1,0:T(8,128)(2,1)S(1)}, u32[]{:S(2)}, u32[]{:S(2)}) collective-permute-start(bf16[2,128,1536]{2,1,0:T(8,128)(2,1)S(1)} %get-tuple-element.47), channel_id=1, source_target_pairs={{0,12},{1,97},{4,0},{5,101},{8,4},{9,105},{12,8},{13,109},{32,44},... | collective-permute-start | bytes 2359304 | tf_op jit(solution)/shard_map/ppermute | solution.py:634
  132.7 5.3 %collective-permute-start.19 = (bf16[128,6144]{1,0:T(8,128)(2,1)S(1)}, bf16[128,6144]{1,0:T(8,128)(2,1)S(1)}, u32[]{:S(2)}, u32[]{:S(2)}) collective-permute-start(bf16[128,6144]{1,0:T(8,128)(2,1)S(1)} %shard_map.142), channel_id=1, source_target_pairs={{0,1},{1,0},{2,3},{3,2},{4,5},{5,4},{6,7},{7,6},{8,9},{9,8},{10,11... | collective-permute-start | bytes 4718600 | tf_op jit(solution)/shard_map/ppermute | solution.py:668
  133.6 16.1 %collective-permute-start.17 = (bf16[256,1024]{1,0:T(8,128)(2,1)S(1)}, bf16[256,1024]{1,0:T(8,128)(2,1)S(1)}, u32[]{:S(2)}, u32[]{:S(2)}) collective-permute-start(bf16[256,1024]{1,0:T(8,128)(2,1)S(1)} %shard_map.139.refs_9_.refs_1_.refs_5_), channel_id=1, source_target_pairs={{0,12},{1,97},{4,0},{5,101},{8,4},{9,105},{12,8},{13,109},{32,44},... | collective-permute-start | bytes 1572872 | tf_op jit(solution)/shard_map/ppermute | solution.py:634
  135.3 14.4 %collective-permute-start.16 = (bf16[256,1024]{1,0:T(8,128)(2,1)S(1)}, bf16[256,1024]{1,0:T(8,128)(2,1)S(1)}, u32[]{:S(2)}, u32[]{:S(2)}) collective-permute-start(bf16[256,1024]{1,0:T(8,128)(2,1)S(1)} %shard_map.139.refs_9_.refs_1_.refs_5_), channel_id=1, source_target_pairs={{0,8},{1,65},{4,12},{5,69},{8,0},{9,73},{12,4},{13,77},{32,40},{33... | collective-permute-start | bytes 1572872 | tf_op jit(solution)/shard_map/ppermute | solution.py:634
  135.7 15.9 %collective-permute-start.15 = (bf16[256,1024]{1,0:T(8,128)(2,1)S(1)}, bf16[256,1024]{1,0:T(8,128)(2,1)S(1)}, u32[]{:S(2)}, u32[]{:S(2)}) collective-permute-start(bf16[256,1024]{1,0:T(8,128)(2,1)S(1)} %shard_map.139.refs_9_.refs_1_.refs_5_), channel_id=1, source_target_pairs={{0,4},{1,33},{4,8},{5,37},{8,12},{9,41},{12,0},{13,45},{32,36},{33... | collective-permute-start | bytes 1572872 | tf_op jit(solution)/shard_map/ppermute | solution.py:634
  136.6 15.0 %copy-start.2 = (bf16[128,6144]{1,0:T(8,128)(2,1)}, bf16[128,6144]{1,0:T(8,128)(2,1)S(1)}, u32[]{:S(2)}) copy-start(bf16[128,6144]{1,0:T(8,128)(2,1)S(1)} %add_convert_fusion.1.refs_10_.refs_4_) | copy-start | bytes 4718596
  136.6 38.7 %collective-permute-start.25 = (bf16[128,6144]{1,0:T(8,128)(2,1)S(1)}, bf16[128,6144]{1,0:T(8,128)(2,1)S(1)}, u32[]{:S(2)}, u32[]{:S(2)}) collective-permute-start(bf16[128,6144]{1,0:T(8,128)(2,1)S(1)} %add_convert_fusion.1.refs_10_.refs_4_), channel_id=1, source_target_pairs={{2,0},{3,1},{6,4},{7,5},{10,8},{11,9},{14,12},{15,13},{18,16},{19,... | collective-permute-start | bytes 4718600 | tf_op jit(solution)/shard_map/ppermute | solution.py:695
  137.9 5.7 %copy-start.11 = (bf16[2,128,1536]{2,1,0:T(8,128)(2,1)S(1)}, bf16[2,128,1536]{2,1,0:T(8,128)(2,1)}, u32[]{:S(2)}) copy-start(bf16[2,128,1536]{2,1,0:T(8,128)(2,1)} %copy-done.10) | copy-start | bytes 2359300
  138.0 5.7 %copy-start.13 = (bf16[256,1024]{1,0:T(8,128)(2,1)S(1)}, bf16[256,1024]{1,0:T(8,128)(2,1)}, u32[]{:S(2)}) copy-start(bf16[256,1024]{1,0:T(8,128)(2,1)} %copy-done.12) | copy-start | bytes 1572868
  138.0 5.7 %copy-start.15 = (bf16[256,1024]{1,0:T(8,128)(2,1)S(1)}, bf16[256,1024]{1,0:T(8,128)(2,1)}, u32[]{:S(2)}) copy-start(bf16[256,1024]{1,0:T(8,128)(2,1)} %copy-done.14) | copy-start | bytes 1572868
  138.0 5.7 %copy-start.17 = (bf16[256,1024]{1,0:T(8,128)(2,1)S(1)}, bf16[256,1024]{1,0:T(8,128)(2,1)}, u32[]{:S(2)}) copy-start(bf16[256,1024]{1,0:T(8,128)(2,1)} %copy-done.16) | copy-start | bytes 1572868
  138.0 5.7 %copy-start.19 = (bf16[256,1024]{1,0:T(8,128)(2,1)S(1)}, bf16[256,1024]{1,0:T(8,128)(2,1)}, u32[]{:S(2)}) copy-start(bf16[256,1024]{1,0:T(8,128)(2,1)} %copy-done.18) | copy-start | bytes 1572868
  138.0 5.7 %copy-start.22 = (bf16[2,128,1536]{2,1,0:T(8,128)(2,1)S(1)}, bf16[2,128,1536]{2,1,0:T(8,128)(2,1)}, u32[]{:S(2)}) copy-start(bf16[2,128,1536]{2,1,0:T(8,128)(2,1)} %copy-done.21) | copy-start | bytes 2359300
  138.4 13.2 %copy-start.5 = (bf16[128,6144]{1,0:T(8,128)(2,1)}, bf16[128,6144]{1,0:T(8,128)(2,1)S(1)}, u32[]{:S(2)}) copy-start(bf16[128,6144]{1,0:T(8,128)(2,1)S(1)} %add_convert_fusion.refs_11_.refs_8_) | copy-start | bytes 4718596
  138.4 43.0 %collective-permute-start.24 = (bf16[128,6144]{1,0:T(8,128)(2,1)S(1)}, bf16[128,6144]{1,0:T(8,128)(2,1)S(1)}, u32[]{:S(2)}, u32[]{:S(2)}) collective-permute-start(bf16[128,6144]{1,0:T(8,128)(2,1)S(1)} %add_convert_fusion.refs_11_.refs_8_), channel_id=1, source_target_pairs={{0,2},{1,3},{4,6},{5,7},{8,10},{9,11},{12,14},{13,15},{16,18},{17,... | collective-permute-start | bytes 4718600 | tf_op jit(solution)/shard_map/ppermute | solution.py:696
  158.0 9.4 %collective-permute-start.20 = (bf16[192,1024]{1,0:T(8,128)(2,1)S(1)}, bf16[192,1024]{1,0:T(8,128)(2,1)S(1)}, u32[]{:S(2)}, u32[]{:S(2)}) collective-permute-start(bf16[192,1024]{1,0:T(8,128)(2,1)S(1)} %get-tuple-element.54), channel_id=1, source_target_pairs={{0,32},{1,5},{4,36},{5,9},{8,40},{9,13},{12,44},{13,1},{32,64},{33... | collective-permute-start | bytes 1179656 | tf_op jit(solution)/shard_map/ppermute | solution.py:634
  159.4 7.9 %collective-permute-start.21 = (bf16[192,1024]{1,0:T(8,128)(2,1)S(1)}, bf16[192,1024]{1,0:T(8,128)(2,1)S(1)}, u32[]{:S(2)}, u32[]{:S(2)}) collective-permute-start(bf16[192,1024]{1,0:T(8,128)(2,1)S(1)} %get-tuple-element.56), channel_id=1, source_target_pairs={{0,96},{1,13},{4,100},{5,1},{8,104},{9,5},{12,108},{13,9},{32,0},{... | collective-permute-start | bytes 1179656 | tf_op jit(solution)/shard_map/ppermute | solution.py:634
  167.5 13.3 %collective-permute-start.22 = (bf16[384,1024]{1,0:T(8,128)(2,1)S(1)}, bf16[384,1024]{1,0:T(8,128)(2,1)S(1)}, u32[]{:S(2)}, u32[]{:S(2)}) collective-permute-start(bf16[384,1024]{1,0:T(8,128)(2,1)S(1)} %get-tuple-element.57), channel_id=1, source_target_pairs={{0,32},{1,5},{4,36},{5,9},{8,40},{9,13},{12,44},{13,1},{32,64},{33... | collective-permute-start | bytes 2359304 | tf_op jit(solution)/shard_map/ppermute | solution.py:634
  169.4 12.0 %collective-permute-start.23 = (bf16[384,1024]{1,0:T(8,128)(2,1)S(1)}, bf16[384,1024]{1,0:T(8,128)(2,1)S(1)}, u32[]{:S(2)}, u32[]{:S(2)}) collective-permute-start(bf16[384,1024]{1,0:T(8,128)(2,1)S(1)} %get-tuple-element.58), channel_id=1, source_target_pairs={{0,96},{1,13},{4,100},{5,1},{8,104},{9,5},{12,108},{13,9},{32,0},{... | collective-permute-start | bytes 2359304 | tf_op jit(solution)/shard_map/ppermute | solution.py:634
  175.4 6.9 %copy-start.8 = (bf16[128,6144]{1,0:T(8,128)(2,1)}, bf16[128,6144]{1,0:T(8,128)(2,1)S(1)}, u32[]{:S(2)}) copy-start(bf16[128,6144]{1,0:T(8,128)(2,1)S(1)} %collective-permute-done.25.refs_5_) | copy-start | bytes 4718596
  183.5 10.2 %collective-permute-start.26 = (bf16[192,1024]{1,0:T(8,128)(2,1)S(1)}, bf16[192,1024]{1,0:T(8,128)(2,1)S(1)}, u32[]{:S(2)}, u32[]{:S(2)}) collective-permute-start(bf16[192,1024]{1,0:T(8,128)(2,1)S(1)} %get-tuple-element.60), channel_id=1, source_target_pairs={{0,16},{16,0},{1,17},{17,1},{2,18},{18,2},{3,19},{19,3},{4,20},{20... | collective-permute-start | bytes 1179656 | tf_op jit(solution)/shard_map/ppermute | solution.py:710
  (10 other events, 25.4 us)

commit v3 on v2

--- a/solution.py
+++ b/solution.py
@@ -687,9 +687,9 @@
     near_0, away_0 = near_rows, away_rows
     *texts, near_rows, away_rows, grads = step(1, own, far, texts, [pieces[0]])
     share_0 = core_sum(near_0, later(away_0, [pieces[0]]))
-    grads = later(grads, last_lefts[1:])
+    grads = later(grads, [last_lefts[1], last_lefts[3]])
     last_rights = spread(grads, [grads] * RING)
-    (so_far,) = weight_grad(where, lefts, rights, after=[grads, share_0])
+    (so_far,) = weight_grad(where, lefts, rights, after=[grads, share_0, last_lefts[2]])
     share_1 = core_sum(near_rows, later(away_rows, [grads]))
 
     from_second = lax.ppermute(share_0, "xl", [(1, 0)])

time: 197 us -> 197 us (level)
    ppermute x16, waiting for transfers between devices: 31.6 us -> 36.7 us  [rotate(): return lax.ppermute(array, ('z', 'y', 'c'), hop(first, distance))]
    ppermute x1, waiting for transfers between devices: 4.35 us -> 0.31 us  [local(): from_second = lax.ppermute(share_0, 'xl', [(1, 0)])]
    unnamed x62 -> x64, local copies, waits for them, and re-layouts: 4.94 us -> 4.98 us
  transfers between devices with their start and end apart: 27 -> 27, of which waited for: 15 -> 14; matrix products, arithmetic and copies ran while one was open for 0% -> 0% of each run, Pallas kernels for 28% -> 28%
where the time goes in v3:
time: 197 us
  waiting for transfers between devices  78.6 us (40%)
  Pallas kernels  69.9 us (35%)
  starting transfers between devices  40.8 us (21%)
  local copies, waits for them, and re-layouts  5.65 us (3%)
    pallas_call x20, Pallas kernels, call(): pl.pallas_call(with_waits, grid_spec=pltpu.PrefetchScalarGridSpec(num_sca...  69.9 us
    ppermute x16, waiting for transfers between devices, rotate(): return lax.ppermute(array, ('z', 'y', 'c'), hop(first, distance))  36.7 us
    ppermute x2, waiting for transfers between devices, local(): other.append(lax.ppermute(mine[image], 'xl', SWAP))  35.9 us
    ppermute x16, starting transfers between devices, rotate(): return lax.ppermute(array, ('z', 'y', 'c'), hop(first, distance))  27.5 us
    ppermute x2, waiting for transfers between devices, local(): far = lax.ppermute(own, 'c', SWAP)  5.14 us
    unnamed x64, local copies, waits for them, and re-layouts  4.98 us
  transfers between devices with their start and end apart: 27, of which 14 were waited for; matrix products, arithmetic and copies ran while one was open for 0% of the time, Pallas kernels for 28%

profile of v3, /device:TPU:0, one launch (start us, length us, event | category | flops | bytes accessed | tf_op | source)
XLA Modules:
  0.0 197.0 jit_solution(2595286138181434950)
XLA Ops:
  0.6 0.7 stack.23.refs_0_
  1.3 2.9 %shard_map.128.refs_3_ = bf16[128,6144]{1,0:T(8,128)(2,1)} custom-call(s32[5]{0:T(128)} %stack.23.refs_0_, bf16[1,512,6144]{2,1,0:T(8,128)(2,1)} %refs_1_.9, bf16[128,6144]{1,0:T(8,128)(2,1)} %refs_3_.3), custom_call_target="tpu_custom_call" | custom-call | tf_op jit(solution)/shard_map/pallas_call | solution.py:39
  4.3 3.0 %shard_map.129 = bf16[128,6144]{1,0:T(8,128)(2,1)} custom-call(s32[5]{0:T(128)} %stack.23.refs_0_, bf16[1,512,6144]{2,1,0:T(8,128)(2,1)} %refs_1_.9, bf16[128,6144]{1,0:T(8,128)(2,1)} %refs_3_.3, bf16[128,6144]{1,0:T(8,128)(2,1)} %shard_map.128.refs_3_), custom_call_target="tpu_custom_call" | custom-call | tf_op jit(solution)/shard_map/pallas_call | solution.py:39
  7.9 2.8 %copy-done = bf16[1,512,6144]{2,1,0:T(8,128)(2,1)S(1)} copy-done((bf16[1,512,6144]{2,1,0:T(8,128)(2,1)S(1)}, bf16[1,512,6144]{2,1,0:T(8,128)(2,1)}, u32[]{:S(2)}) %copy-start) | copy-done | bytes 6291480
  10.7 1.3 shard_map.131.refs_0_.refs_2_
  12.0 1.7 collective-permute-start.3
  13.7 1.3 shard_map.130.refs_3_.refs_0_.refs_6_
  15.0 33.6 %collective-permute-done.3.refs_1_.refs_3_ = bf16[128,6144]{1,0:T(8,128)(2,1)S(1)} collective-permute-done((bf16[128,6144]{1,0:T(8,128)(2,1)S(1)}, bf16[128,6144]{1,0:T(8,128)(2,1)S(1)}, u32[]{:S(2)}, u32[]{:S(2)}) %collective-permute-start.3) | collective-permute-done | bytes 1572896 | tf_op jit(solution)/shard_map/ppermute | solution.py:662
  48.5 1.4 shard_map.132.refs_1_.refs_2_
  50.1 1.7 collective-permute-start.1
  51.7 1.7 collective-permute-done.4.refs_2_.refs_3_
  53.5 5.3 %shard_map.133 = (bf16[2,128,1536]{2,1,0:T(8,128)(2,1)S(1)}, bf16[2,128,1536]{2,1,0:T(8,128)(2,1)S(1)}, bf16[2,128,1536]{2,1,0:T(8,128)(2,1)S(1)}, bf16[2,128,1536]{2,1,0:T(8,128)(2,1)S(1)}) custom-call(s32[5]{0:T(128)S(1)} %copy-done.24, bf16[128,6144]{1,0:T(8,128)(2,1)S(1)} %shard_map.132.refs_1_.refs_2_, ...), custom_call_target="tpu_custom_call" | custom-call | bytes 6291456 | tf_op jit(solution)/shard_map/pallas_call | solution.py:39
  58.7 1.7 collective-permute-start.6
  60.5 1.6 collective-permute-start.7
  62.0 2.1 %collective-permute-start.5 = (bf16[2,128,1536]{2,1,0:T(8,128)(2,1)S(1)}, bf16[2,128,1536]{2,1,0:T(8,128)(2,1)S(1)}, u32[]{:S(2)}, u32[]{:S(2)}) collective-permute-start(bf16[2,128,1536]{2,1,0:T(8,128)(2,1)S(1)} %get-tuple-element.36), channel_id=1, source_target_pairs={{0,8},{1,65},{4,12},{5,69},{8,0},{9,73},{12,4},{13,77},{32,40},{33... | collective-permute-start | bytes 2359304 | tf_op jit(solution)/shard_map/ppermute | solution.py:634
  64.1 13.2 %shard_map.134 = (f32[2,512,512]{2,1,0:T(8,128)}, f32[2,512,512]{2,1,0:T(8,128)}, bf16[128,6144]{1,0:T(8,128)(2,1)S(1)}, bf16[128,6144]{1,0:T(8,128)(2,1)S(1)}, bf16[256,1024]{1,0:T(8,128)(2,1)S(1)}) custom-call(s32[2]{0:T(128)S(1)} %bitcast.10, s32[2]{0:T(128)S(1)} %copy-done.30, bf16[128,6144]{1,0:T(8,128)(2,1)S(1)} %shard_map.132.refs_1_.refs_2_, ...), custom_call_target="tpu_custom_call" | custom-call | flops 7247757312 | bytes 22020096 | tf_op jit(solution)/shard_map/pallas_call | solution.py:39
  77.4 6.3 %collective-permute-start.10 = (bf16[256,1024]{1,0:T(8,128)(2,1)S(1)}, bf16[256,1024]{1,0:T(8,128)(2,1)S(1)}, u32[]{:S(2)}, u32[]{:S(2)}) collective-permute-start(bf16[256,1024]{1,0:T(8,128)(2,1)S(1)} %shard_map.135.refs_5_), channel_id=1, source_target_pairs={{0,12},{1,97},{4,0},{5,101},{8,4},{9,105},{12,8},{13,109},{32,44},... | collective-permute-start | bytes 1572872 | tf_op jit(solution)/shard_map/ppermute | solution.py:634
  83.7 0.9 collective-permute-start.8
  84.5 2.3 %collective-permute-done.1.refs_1_.refs_7_ = bf16[128,6144]{1,0:T(8,128)(2,1)S(1)} collective-permute-done((bf16[128,6144]{1,0:T(8,128)(2,1)S(1)}, bf16[128,6144]{1,0:T(8,128)(2,1)S(1)}, u32[]{:S(2)}, u32[]{:S(2)}) %collective-permute-start.1) | collective-permute-done | bytes 1572896 | tf_op jit(solution)/shard_map/ppermute | solution.py:662
  86.9 9.1 %collective-permute-done.10.refs_7_.refs_8_ = bf16[256,1024]{1,0:T(8,128)(2,1)S(1)} collective-permute-done((bf16[256,1024]{1,0:T(8,128)(2,1)S(1)}, bf16[256,1024]{1,0:T(8,128)(2,1)S(1)}, u32[]{:S(2)}, u32[]{:S(2)}) %collective-permute-start.10) | collective-permute-done | bytes 524320 | tf_op jit(solution)/shard_map/ppermute | solution.py:634
  96.0 3.7 %collective-permute-done.8.refs_5_.refs_6_ = bf16[256,1024]{1,0:T(8,128)(2,1)S(1)} collective-permute-done((bf16[256,1024]{1,0:T(8,128)(2,1)S(1)}, bf16[256,1024]{1,0:T(8,128)(2,1)S(1)}, u32[]{:S(2)}, u32[]{:S(2)}) %collective-permute-start.8) | collective-permute-done | bytes 524320 | tf_op jit(solution)/shard_map/ppermute | solution.py:634
  99.7 1.3 shard_map.136.refs_1_.refs_2_
  101.2 3.4 %collective-permute-done.11.refs_2_.refs_3_ = bf16[128,6144]{1,0:T(8,128)(2,1)S(1)} collective-permute-done((bf16[128,6144]{1,0:T(8,128)(2,1)S(1)}, bf16[128,6144]{1,0:T(8,128)(2,1)S(1)}, u32[]{:S(2)}, u32[]{:S(2)}) %collective-permute-start.11) | collective-permute-done | bytes 1572896 | tf_op jit(solution)/shard_map/ppermute | solution.py:684
  104.6 5.4 %shard_map.137 = (bf16[2,128,1536]{2,1,0:T(8,128)(2,1)S(1)}, bf16[2,128,1536]{2,1,0:T(8,128)(2,1)S(1)}, bf16[2,128,1536]{2,1,0:T(8,128)(2,1)}, bf16[2,128,1536]{2,1,0:T(8,128)(2,1)S(1)}) custom-call(s32[5]{0:T(128)S(1)} %copy-done.24, bf16[128,6144]{1,0:T(8,128)(2,1)S(1)} %shard_map.136.refs_1_.refs_2_, ...), custom_call_target="tpu_custom_call" | custom-call | bytes 6291456 | tf_op jit(solution)/shard_map/pallas_call | solution.py:39
  110.4 3.1 %collective-permute-start.14 = (bf16[2,128,1536]{2,1,0:T(8,128)(2,1)S(1)}, bf16[2,128,1536]{2,1,0:T(8,128)(2,1)S(1)}, u32[]{:S(2)}, u32[]{:S(2)}) collective-permute-start(bf16[2,128,1536]{2,1,0:T(8,128)(2,1)S(1)} %get-tuple-element.47), channel_id=1, source_target_pairs={{0,12},{1,97},{4,0},{5,101},{8,4},{9,105},{12,8},{13,109},{32,44},... | collective-permute-start | bytes 2359304 | tf_op jit(solution)/shard_map/ppermute | solution.py:634
  113.6 13.2 %shard_map.138 = (f32[2,512,512]{2,1,0:T(8,128)}, f32[2,512,512]{2,1,0:T(8,128)}, bf16[128,6144]{1,0:T(8,128)(2,1)S(1)}, bf16[128,6144]{1,0:T(8,128)(2,1)S(1)}, bf16[256,1024]{1,0:T(8,128)(2,1)S(1)}) custom-call(s32[2]{0:T(128)S(1)} %bitcast.11, s32[2]{0:T(128)S(1)} %copy-done.30, ...), custom_call_target="tpu_custom_call", output_to_operand_aliasing={{0}: (8, {}), {1}: (9, {})} | custom-call | flops 7247757312 | bytes 22020096 | tf_op jit(solution)/shard_map/pallas_call | solution.py:39
  126.8 1.1 collective-permute-start.19
  128.2 1.2 collective-permute-start.17
  129.4 2.3 %collective-permute-start.16 = (bf16[256,1024]{1,0:T(8,128)(2,1)S(1)}, bf16[256,1024]{1,0:T(8,128)(2,1)S(1)}, u32[]{:S(2)}, u32[]{:S(2)}) collective-permute-start(bf16[256,1024]{1,0:T(8,128)(2,1)S(1)} %shard_map.139.refs_9_.refs_1_.refs_5_), channel_id=1, source_target_pairs={{0,8},{1,65},{4,12},{5,69},{8,0},{9,73},{12,4},{13,77},{32,40},{33... | collective-permute-start | bytes 1572872 | tf_op jit(solution)/shard_map/ppermute | solution.py:634
  131.7 1.1 collective-permute-start.15
  133.2 1.3 collective-permute-start.25
  135.0 6.7 %collective-permute-done.13.refs_11_.refs_3_ = bf16[2,128,1536]{2,1,0:T(8,128)(2,1)S(1)} collective-permute-done((bf16[2,128,1536]{2,1,0:T(8,128)(2,1)}, bf16[2,128,1536]{2,1,0:T(8,128)(2,1)S(1)}, u32[]{:S(2)}, u32[]{:S(2)}) %collective-permute-start.13) | collective-permute-done | bytes 786464 | tf_op jit(solution)/shard_map/ppermute | solution.py:634
  141.7 3.7 %collective-permute-start.24 = (bf16[128,6144]{1,0:T(8,128)(2,1)S(1)}, bf16[128,6144]{1,0:T(8,128)(2,1)S(1)}, u32[]{:S(2)}, u32[]{:S(2)}) collective-permute-start(bf16[128,6144]{1,0:T(8,128)(2,1)S(1)} %add_convert_fusion.refs_11_.refs_8_), channel_id=1, source_target_pairs={{0,2},{1,3},{4,6},{5,7},{8,10},{9,11},{12,14},{13,15},{16,18},{17,... | collective-permute-start | bytes 4718600 | tf_op jit(solution)/shard_map/ppermute | solution.py:696
  145.4 6.0 %shard_map.141.refs_9_ = bf16[4,384,1024]{2,1,0:T(8,128)(2,1)S(1)} custom-call(s32[5]{0:T(128)S(1)} %copy-done.24, bf16[2,128,1536]{2,1,0:T(8,128)(2,1)S(1)} %copy-done.21, bf16[2,128,1536]{2,1,0:T(8,128)(2,1)S(1)} %collective-permute-done.6.refs_1_.refs_2_, bf16[2,128,1536]{2,1,0:T(8,128)(2,1)S(1)} %collective-permute-done.5.refs_4_.refs_3_, ...), custom_call_target="tpu_custom_call" | custom-call | tf_op jit(solution)/shard_map/pallas_call | solution.py:39
  151.5 1.4 collective-permute-done.15.refs_6_
  152.8 6.3 %shard_map.143 = (bf16[384,1024]{1,0:T(8,128)(2,1)S(1)}, bf16[384,1024]{1,0:T(8,128)(2,1)S(1)}, bf16[192,1024]{1,0:T(8,128)(2,1)S(1)}, bf16[192,1024]{1,0:T(8,128)(2,1)S(1)}, bf16[384,1024]{1,0:T(8,128)(2,1)S(1)}) custom-call(s32[5]{0:T(128)S(1)} %copy-done.24, bf16[2,128,1536]{2,1,0:T(8,128)(2,1)S(1)} %copy-done.11, ...), custom_call_target="tpu_custom_call" | custom-call | tf_op jit(solution)/shard_map/pallas_call | solution.py:39
  159.2 1.2 collective-permute-start.20
  160.4 2.2 %collective-permute-start.21 = (bf16[192,1024]{1,0:T(8,128)(2,1)S(1)}, bf16[192,1024]{1,0:T(8,128)(2,1)S(1)}, u32[]{:S(2)}, u32[]{:S(2)}) collective-permute-start(bf16[192,1024]{1,0:T(8,128)(2,1)S(1)} %get-tuple-element.56), channel_id=1, source_target_pairs={{0,96},{1,13},{4,100},{5,1},{8,104},{9,5},{12,108},{13,9},{32,0},{... | collective-permute-start | bytes 1179656 | tf_op jit(solution)/shard_map/ppermute | solution.py:634
  162.6 5.7 %collective-permute-done.20.refs_1_ = bf16[192,1024]{1,0:T(8,128)(2,1)S(1)} collective-permute-done((bf16[192,1024]{1,0:T(8,128)(2,1)S(1)}, bf16[192,1024]{1,0:T(8,128)(2,1)S(1)}, u32[]{:S(2)}, u32[]{:S(2)}) %collective-permute-start.20) | collective-permute-done | bytes 393248 | tf_op jit(solution)/shard_map/ppermute | solution.py:634
  168.4 1.9 collective-permute-start.22
  170.3 1.6 collective-permute-start.23
  172.2 9.6 %collective-permute-done.22.refs_2_ = bf16[384,1024]{1,0:T(8,128)(2,1)S(1)} collective-permute-done((bf16[384,1024]{1,0:T(8,128)(2,1)S(1)}, bf16[384,1024]{1,0:T(8,128)(2,1)S(1)}, u32[]{:S(2)}, u32[]{:S(2)}) %collective-permute-start.22) | collective-permute-done | bytes 786464 | tf_op jit(solution)/shard_map/ppermute | solution.py:634
  182.3 0.8 shard_map.145
  183.6 0.9 copy-done.22
  184.5 3.0 %collective-permute-start.26 = (bf16[192,1024]{1,0:T(8,128)(2,1)S(1)}, bf16[192,1024]{1,0:T(8,128)(2,1)S(1)}, u32[]{:S(2)}, u32[]{:S(2)}) collective-permute-start(bf16[192,1024]{1,0:T(8,128)(2,1)S(1)} %get-tuple-element.60), channel_id=1, source_target_pairs={{0,16},{16,0},{1,17},{17,1},{2,18},{18,2},{3,19},{19,3},{4,20},{20... | collective-permute-start | bytes 1179656 | tf_op jit(solution)/shard_map/ppermute | solution.py:710
  187.5 6.1 %shard_map.146.refs_2_ = f32[128,6144]{1,0:T(8,128)} custom-call(s32[5]{0:T(128)} %stack.23.refs_0_, f32[1,6144]{1,0:T(1,128)} %bitcast.7, bf16[128,6144]{1,0:T(8,128)(2,1)} %copy-done.4, bf16[128,6144]{1,0:T(8,128)(2,1)} %copy-done.7, bf16[128,6144]{1,0:T(8,128)(2,1)} %copy-done.2, bf16[128,6144]{1,0:T(8,128)(2,1)} %copy-done.8, ...), custom_call_target="tpu_custom_call" | custom-call | bytes 9437184 | tf_op jit(solution)/shard_map/pallas_call | solution.py:39
  194.1 0.8 copy-done.31
  194.8 2.1 %shard_map.147 = (f32[192,512]{1,0:T(8,128)}, f32[192,512]{1,0:T(8,128)}) custom-call(f32[192,1024]{1,0:T(8,128)} %copy-done.22, bf16[192,1024]{1,0:T(8,128)(2,1)} %copy-done.31, f32[128,6144]{1,0:T(8,128)} %shard_map.146.refs_2_), custom_call_target="tpu_custom_call" | custom-call | bytes 1966080 | tf_op jit(solution)/shard_map/pallas_call | solution.py:39
  (93 shorter events, 4.3 us)
Async XLA Ops:
  4.2 3.7 %copy-start.3 = (bf16[128,6144]{1,0:T(8,128)(2,1)S(1)}, bf16[128,6144]{1,0:T(8,128)(2,1)}, u32[]{:S(2)}) copy-start(bf16[128,6144]{1,0:T(8,128)(2,1)} %refs_3_.3) | copy-start | bytes 4718596
  4.2 3.7 %collective-permute-start.2 = (bf16[128,6144]{1,0:T(8,128)(2,1)}, bf16[128,6144]{1,0:T(8,128)(2,1)S(1)}, u32[]{:S(2)}, u32[]{:S(2)}) collective-permute-start(bf16[128,6144]{1,0:T(8,128)(2,1)} %shard_map.128.refs_3_), channel_id=1, source_target_pairs={{0,1},{1,0},{2,3},{3,2},{4,5},{5,4},{6,7},{7,6},{8,9},{9,8},{10,11... | collective-permute-start | bytes 4718600 | tf_op jit(solution)/shard_map/ppermute | solution.py:660
  7.3 6.4 %collective-permute-start = (bf16[128,6144]{1,0:T(8,128)(2,1)}, bf16[128,6144]{1,0:T(8,128)(2,1)S(1)}, u32[]{:S(2)}, u32[]{:S(2)}) collective-permute-start(bf16[128,6144]{1,0:T(8,128)(2,1)} %shard_map.129), channel_id=1, source_target_pairs={{0,1},{1,0},{2,3},{3,2},{4,5},{5,4},{6,7},{7,6},{8,9},{9,8},{10,11... | collective-permute-start | bytes 4718600 | tf_op jit(solution)/shard_map/ppermute | solution.py:660
  12.0 36.5 %copy-start.4 = (bf16[128,6144]{1,0:T(8,128)(2,1)}, bf16[128,6144]{1,0:T(8,128)(2,1)S(1)}, u32[]{:S(2)}) copy-start(bf16[128,6144]{1,0:T(8,128)(2,1)S(1)} %shard_map.131.refs_0_.refs_2_) | copy-start | bytes 4718596
  12.0 36.5 %copy-start.23 = (f32[6144]{0:T(1024)S(1)}, f32[6144]{0:T(1024)}, u32[]{:S(2)}) copy-start(f32[6144]{0:T(1024)} %param.11) | copy-start | bytes 73732
  12.0 36.5 %collective-permute-start.3 = (bf16[128,6144]{1,0:T(8,128)(2,1)S(1)}, bf16[128,6144]{1,0:T(8,128)(2,1)S(1)}, u32[]{:S(2)}, u32[]{:S(2)}) collective-permute-start(bf16[128,6144]{1,0:T(8,128)(2,1)S(1)} %shard_map.131.refs_0_.refs_2_), channel_id=1, source_target_pairs={{0,2},{2,0},{1,3},{3,1},{4,6},{6,4},{5,7},{7,5},{8,10},{10,8},{9,1... | collective-permute-start | bytes 4718600 | tf_op jit(solution)/shard_map/ppermute | solution.py:662
  15.0 84.7 %copy-start.1 = (bf16[128,6144]{1,0:T(8,128)(2,1)}, bf16[128,6144]{1,0:T(8,128)(2,1)S(1)}, u32[]{:S(2)}) copy-start(bf16[128,6144]{1,0:T(8,128)(2,1)S(1)} %shard_map.130.refs_3_.refs_0_.refs_6_) | copy-start | bytes 4718596
  49.9 14.2 %copy-start.25 = (bf16[2,512,512]{2,1,0:T(8,128)(2,1)S(1)}, bf16[2,512,512]{2,1,0:T(8,128)(2,1)}, u32[]{:S(2)}) copy-start(bf16[2,512,512]{2,1,0:T(8,128)(2,1)} %refs_6_.3) | copy-start | bytes 3145732
  49.9 14.2 %copy-start.27 = (bf16[2,512,512]{2,1,0:T(8,128)(2,1)S(1)}, bf16[2,512,512]{2,1,0:T(8,128)(2,1)}, u32[]{:S(2)}) copy-start(bf16[2,512,512]{2,1,0:T(8,128)(2,1)} %refs_7_.3) | copy-start | bytes 3145732
  49.9 14.2 %copy-start.29 = (s32[1,2]{1,0:T(1,128)S(1)}, s32[1,2]{1,0:T(1,128)}, u32[]{:S(2)}) copy-start(s32[1,2]{1,0:T(1,128)} %param.17) | copy-start | bytes 28
  50.0 14.2 %copy-start.30 = (s32[2]{0:T(128)S(1)}, s32[2]{0:T(128)}, u32[]{:S(2)}) copy-start(s32[2]{0:T(128)} %refs_1_.11) | copy-start | bytes 28
  50.0 3.5 %collective-permute-start.4 = (bf16[128,6144]{1,0:T(8,128)(2,1)S(1)}, bf16[128,6144]{1,0:T(8,128)(2,1)S(1)}, u32[]{:S(2)}, u32[]{:S(2)}) collective-permute-start(bf16[128,6144]{1,0:T(8,128)(2,1)S(1)} %shard_map.132.refs_1_.refs_2_), channel_id=1, source_target_pairs={{0,1},{1,0},{2,3},{3,2},{4,5},{5,4},{6,7},{7,6},{8,9},{9,8},{10,11... | collective-permute-start | bytes 4718600 | tf_op jit(solution)/shard_map/ppermute | solution.py:676
  50.1 36.8 %collective-permute-start.1 = (bf16[128,6144]{1,0:T(8,128)(2,1)S(1)}, bf16[128,6144]{1,0:T(8,128)(2,1)S(1)}, u32[]{:S(2)}, u32[]{:S(2)}) collective-permute-start(bf16[128,6144]{1,0:T(8,128)(2,1)S(1)} %shard_map.130.refs_3_.refs_0_.refs_6_), channel_id=1, source_target_pairs={{0,2},{2,0},{1,3},{3,1},{4,6},{6,4},{5,7},{7,5},{8,10},{10,8},{9,1... | collective-permute-start | bytes 4718600 | tf_op jit(solution)/shard_map/ppermute | solution.py:662
  58.7 18.6 %copy-start.20 = (bf16[2,128,1536]{2,1,0:T(8,128)(2,1)}, bf16[2,128,1536]{2,1,0:T(8,128)(2,1)S(1)}, u32[]{:S(2)}) copy-start(bf16[2,128,1536]{2,1,0:T(8,128)(2,1)S(1)} %get-tuple-element.34.refs_8_.refs_1_) | copy-start | bytes 2359300
  58.7 18.6 %collective-permute-start.6 = (bf16[2,128,1536]{2,1,0:T(8,128)(2,1)S(1)}, bf16[2,128,1536]{2,1,0:T(8,128)(2,1)S(1)}, u32[]{:S(2)}, u32[]{:S(2)}) collective-permute-start(bf16[2,128,1536]{2,1,0:T(8,128)(2,1)S(1)} %get-tuple-element.38), channel_id=1, source_target_pairs={{0,4},{1,33},{4,8},{5,37},{8,12},{9,41},{12,0},{13,45},{32,36},{33... | collective-permute-start | bytes 2359304 | tf_op jit(solution)/shard_map/ppermute | solution.py:634
  60.5 16.9 %collective-permute-start.7 = (bf16[2,128,1536]{2,1,0:T(8,128)(2,1)S(1)}, bf16[2,128,1536]{2,1,0:T(8,128)(2,1)S(1)}, u32[]{:S(2)}, u32[]{:S(2)}) collective-permute-start(bf16[2,128,1536]{2,1,0:T(8,128)(2,1)S(1)} %get-tuple-element.39), channel_id=1, source_target_pairs={{0,12},{1,97},{4,0},{5,101},{8,4},{9,105},{12,8},{13,109},{32,44},... | collective-permute-start | bytes 2359304 | tf_op jit(solution)/shard_map/ppermute | solution.py:634
  62.0 24.8 %collective-permute-start.5 = (bf16[2,128,1536]{2,1,0:T(8,128)(2,1)S(1)}, bf16[2,128,1536]{2,1,0:T(8,128)(2,1)S(1)}, u32[]{:S(2)}, u32[]{:S(2)}) collective-permute-start(bf16[2,128,1536]{2,1,0:T(8,128)(2,1)S(1)} %get-tuple-element.36), channel_id=1, source_target_pairs={{0,8},{1,65},{4,12},{5,69},{8,0},{9,73},{12,4},{13,77},{32,40},{33... | collective-permute-start | bytes 2359304 | tf_op jit(solution)/shard_map/ppermute | solution.py:634
  77.4 23.6 %copy-start.16 = (bf16[256,1024]{1,0:T(8,128)(2,1)}, bf16[256,1024]{1,0:T(8,128)(2,1)S(1)}, u32[]{:S(2)}) copy-start(bf16[256,1024]{1,0:T(8,128)(2,1)S(1)} %shard_map.135.refs_5_) | copy-start | bytes 1572868
  77.4 18.6 %collective-permute-start.10 = (bf16[256,1024]{1,0:T(8,128)(2,1)S(1)}, bf16[256,1024]{1,0:T(8,128)(2,1)S(1)}, u32[]{:S(2)}, u32[]{:S(2)}) collective-permute-start(bf16[256,1024]{1,0:T(8,128)(2,1)S(1)} %shard_map.135.refs_5_), channel_id=1, source_target_pairs={{0,12},{1,97},{4,0},{5,101},{8,4},{9,105},{12,8},{13,109},{32,44},... | collective-permute-start | bytes 1572872 | tf_op jit(solution)/shard_map/ppermute | solution.py:634
  83.7 12.3 %collective-permute-start.9 = (bf16[256,1024]{1,0:T(8,128)(2,1)S(1)}, bf16[256,1024]{1,0:T(8,128)(2,1)S(1)}, u32[]{:S(2)}, u32[]{:S(2)}) collective-permute-start(bf16[256,1024]{1,0:T(8,128)(2,1)S(1)} %shard_map.135.refs_5_), channel_id=1, source_target_pairs={{0,8},{1,65},{4,12},{5,69},{8,0},{9,73},{12,4},{13,77},{32,40},{33... | collective-permute-start | bytes 1572872 | tf_op jit(solution)/shard_map/ppermute | solution.py:634
  83.7 16.0 %collective-permute-start.8 = (bf16[256,1024]{1,0:T(8,128)(2,1)S(1)}, bf16[256,1024]{1,0:T(8,128)(2,1)S(1)}, u32[]{:S(2)}, u32[]{:S(2)}) collective-permute-start(bf16[256,1024]{1,0:T(8,128)(2,1)S(1)} %shard_map.135.refs_5_), channel_id=1, source_target_pairs={{0,4},{1,33},{4,8},{5,37},{8,12},{9,41},{12,0},{13,45},{32,36},{33... | collective-permute-start | bytes 1572872 | tf_op jit(solution)/shard_map/ppermute | solution.py:634
  86.9 14.2 %copy-start.6 = (bf16[128,6144]{1,0:T(8,128)(2,1)}, bf16[128,6144]{1,0:T(8,128)(2,1)S(1)}, u32[]{:S(2)}) copy-start(bf16[128,6144]{1,0:T(8,128)(2,1)S(1)} %collective-permute-done.1.refs_1_.refs_7_) | copy-start | bytes 4718596
  96.0 5.1 %copy-start.12 = (bf16[256,1024]{1,0:T(8,128)(2,1)}, bf16[256,1024]{1,0:T(8,128)(2,1)S(1)}, u32[]{:S(2)}) copy-start(bf16[256,1024]{1,0:T(8,128)(2,1)S(1)} %collective-permute-done.9.refs_6_.refs_7_) | copy-start | bytes 1572868
  101.1 3.5 %collective-permute-start.11 = (bf16[128,6144]{1,0:T(8,128)(2,1)S(1)}, bf16[128,6144]{1,0:T(8,128)(2,1)S(1)}, u32[]{:S(2)}, u32[]{:S(2)}) collective-permute-start(bf16[128,6144]{1,0:T(8,128)(2,1)S(1)} %shard_map.136.refs_1_.refs_2_), channel_id=1, source_target_pairs={{0,1},{1,0},{2,3},{3,2},{4,5},{5,4},{6,7},{7,6},{8,9},{9,8},{10,11... | collective-permute-start | bytes 4718600 | tf_op jit(solution)/shard_map/ppermute | solution.py:684
  104.6 5.5 %copy-start.18 = (bf16[128,6144]{1,0:T(8,128)(2,1)}, bf16[128,6144]{1,0:T(8,128)(2,1)S(1)}, u32[]{:S(2)}) copy-start(bf16[128,6144]{1,0:T(8,128)(2,1)S(1)} %collective-permute-done.11.refs_2_.refs_3_) | copy-start | bytes 4718596
  110.1 21.6 %collective-permute-start.18 = (bf16[128,6144]{1,0:T(8,128)(2,1)S(1)}, bf16[128,6144]{1,0:T(8,128)(2,1)S(1)}, u32[]{:S(2)}, u32[]{:S(2)}) collective-permute-start(bf16[128,6144]{1,0:T(8,128)(2,1)S(1)} %shard_map.140), channel_id=1, source_target_pairs={{0,1},{1,0},{2,3},{3,2},{4,5},{5,4},{6,7},{7,6},{8,9},{9,8},{10,11... | collective-permute-start | bytes 4718600 | tf_op jit(solution)/shard_map/ppermute | solution.py:668
  110.3 16.5 %collective-permute-start.12 = (bf16[2,128,1536]{2,1,0:T(8,128)(2,1)S(1)}, bf16[2,128,1536]{2,1,0:T(8,128)(2,1)S(1)}, u32[]{:S(2)}, u32[]{:S(2)}) collective-permute-start(bf16[2,128,1536]{2,1,0:T(8,128)(2,1)S(1)} %get-tuple-element.45), channel_id=1, source_target_pairs={{0,4},{1,33},{4,8},{5,37},{8,12},{9,41},{12,0},{13,45},{32,36},{33... | collective-permute-start | bytes 2359304 | tf_op jit(solution)/shard_map/ppermute | solution.py:634
  110.4 16.4 %collective-permute-start.14 = (bf16[2,128,1536]{2,1,0:T(8,128)(2,1)S(1)}, bf16[2,128,1536]{2,1,0:T(8,128)(2,1)S(1)}, u32[]{:S(2)}, u32[]{:S(2)}) collective-permute-start(bf16[2,128,1536]{2,1,0:T(8,128)(2,1)S(1)} %get-tuple-element.47), channel_id=1, source_target_pairs={{0,12},{1,97},{4,0},{5,101},{8,4},{9,105},{12,8},{13,109},{32,44},... | collective-permute-start | bytes 2359304 | tf_op jit(solution)/shard_map/ppermute | solution.py:634
  126.8 6.4 %collective-permute-start.19 = (bf16[128,6144]{1,0:T(8,128)(2,1)S(1)}, bf16[128,6144]{1,0:T(8,128)(2,1)S(1)}, u32[]{:S(2)}, u32[]{:S(2)}) collective-permute-start(bf16[128,6144]{1,0:T(8,128)(2,1)S(1)} %shard_map.142), channel_id=1, source_target_pairs={{0,1},{1,0},{2,3},{3,2},{4,5},{5,4},{6,7},{7,6},{8,9},{9,8},{10,11... | collective-permute-start | bytes 4718600 | tf_op jit(solution)/shard_map/ppermute | solution.py:668
  127.9 13.8 %collective-permute-start.13 = (bf16[2,128,1536]{2,1,0:T(8,128)(2,1)}, bf16[2,128,1536]{2,1,0:T(8,128)(2,1)S(1)}, u32[]{:S(2)}, u32[]{:S(2)}) collective-permute-start(bf16[2,128,1536]{2,1,0:T(8,128)(2,1)} %get-tuple-element.46), channel_id=1, source_target_pairs={{0,8},{1,65},{4,12},{5,69},{8,0},{9,73},{12,4},{13,77},{32,40},{33... | collective-permute-start | bytes 2359304 | tf_op jit(solution)/shard_map/ppermute | solution.py:634
  128.2 23.3 %collective-permute-start.17 = (bf16[256,1024]{1,0:T(8,128)(2,1)S(1)}, bf16[256,1024]{1,0:T(8,128)(2,1)S(1)}, u32[]{:S(2)}, u32[]{:S(2)}) collective-permute-start(bf16[256,1024]{1,0:T(8,128)(2,1)S(1)} %shard_map.139.refs_9_.refs_1_.refs_5_), channel_id=1, source_target_pairs={{0,12},{1,97},{4,0},{5,101},{8,4},{9,105},{12,8},{13,109},{32,44},... | collective-permute-start | bytes 1572872 | tf_op jit(solution)/shard_map/ppermute | solution.py:634
  129.4 22.1 %collective-permute-start.16 = (bf16[256,1024]{1,0:T(8,128)(2,1)S(1)}, bf16[256,1024]{1,0:T(8,128)(2,1)S(1)}, u32[]{:S(2)}, u32[]{:S(2)}) collective-permute-start(bf16[256,1024]{1,0:T(8,128)(2,1)S(1)} %shard_map.139.refs_9_.refs_1_.refs_5_), channel_id=1, source_target_pairs={{0,8},{1,65},{4,12},{5,69},{8,0},{9,73},{12,4},{13,77},{32,40},{33... | collective-permute-start | bytes 1572872 | tf_op jit(solution)/shard_map/ppermute | solution.py:634
  131.7 21.1 %collective-permute-start.15 = (bf16[256,1024]{1,0:T(8,128)(2,1)S(1)}, bf16[256,1024]{1,0:T(8,128)(2,1)S(1)}, u32[]{:S(2)}, u32[]{:S(2)}) collective-permute-start(bf16[256,1024]{1,0:T(8,128)(2,1)S(1)} %shard_map.139.refs_9_.refs_1_.refs_5_), channel_id=1, source_target_pairs={{0,4},{1,33},{4,8},{5,37},{8,12},{9,41},{12,0},{13,45},{32,36},{33... | collective-permute-start | bytes 1572872 | tf_op jit(solution)/shard_map/ppermute | solution.py:634
  133.2 19.6 %copy-start.2 = (bf16[128,6144]{1,0:T(8,128)(2,1)}, bf16[128,6144]{1,0:T(8,128)(2,1)S(1)}, u32[]{:S(2)}) copy-start(bf16[128,6144]{1,0:T(8,128)(2,1)S(1)} %add_convert_fusion.1.refs_10_.refs_4_) | copy-start | bytes 4718596
  133.2 39.0 %collective-permute-start.25 = (bf16[128,6144]{1,0:T(8,128)(2,1)S(1)}, bf16[128,6144]{1,0:T(8,128)(2,1)S(1)}, u32[]{:S(2)}, u32[]{:S(2)}) collective-permute-start(bf16[128,6144]{1,0:T(8,128)(2,1)S(1)} %add_convert_fusion.1.refs_10_.refs_4_), channel_id=1, source_target_pairs={{2,0},{3,1},{6,4},{7,5},{10,8},{11,9},{14,12},{15,13},{18,16},{19,... | collective-permute-start | bytes 4718600 | tf_op jit(solution)/shard_map/ppermute | solution.py:695
  134.5 10.9 %copy-start.13 = (bf16[256,1024]{1,0:T(8,128)(2,1)S(1)}, bf16[256,1024]{1,0:T(8,128)(2,1)}, u32[]{:S(2)}) copy-start(bf16[256,1024]{1,0:T(8,128)(2,1)} %copy-done.12) | copy-start | bytes 1572868
  134.5 10.9 %copy-start.15 = (bf16[256,1024]{1,0:T(8,128)(2,1)S(1)}, bf16[256,1024]{1,0:T(8,128)(2,1)}, u32[]{:S(2)}) copy-start(bf16[256,1024]{1,0:T(8,128)(2,1)} %copy-done.14) | copy-start | bytes 1572868
  134.6 10.9 %copy-start.17 = (bf16[256,1024]{1,0:T(8,128)(2,1)S(1)}, bf16[256,1024]{1,0:T(8,128)(2,1)}, u32[]{:S(2)}) copy-start(bf16[256,1024]{1,0:T(8,128)(2,1)} %copy-done.16) | copy-start | bytes 1572868
  134.6 10.9 %copy-start.21 = (bf16[2,128,1536]{2,1,0:T(8,128)(2,1)S(1)}, bf16[2,128,1536]{2,1,0:T(8,128)(2,1)}, u32[]{:S(2)}) copy-start(bf16[2,128,1536]{2,1,0:T(8,128)(2,1)} %copy-done.20) | copy-start | bytes 2359300
  134.9 17.9 %copy-start.5 = (bf16[128,6144]{1,0:T(8,128)(2,1)}, bf16[128,6144]{1,0:T(8,128)(2,1)S(1)}, u32[]{:S(2)}) copy-start(bf16[128,6144]{1,0:T(8,128)(2,1)S(1)} %add_convert_fusion.refs_11_.refs_8_) | copy-start | bytes 4718596
  135.0 17.9 %copy-start.11 = (bf16[2,128,1536]{2,1,0:T(8,128)(2,1)S(1)}, bf16[2,128,1536]{2,1,0:T(8,128)(2,1)}, u32[]{:S(2)}) copy-start(bf16[2,128,1536]{2,1,0:T(8,128)(2,1)} %copy-done.10) | copy-start | bytes 2359300
  141.7 40.6 %collective-permute-start.24 = (bf16[128,6144]{1,0:T(8,128)(2,1)S(1)}, bf16[128,6144]{1,0:T(8,128)(2,1)S(1)}, u32[]{:S(2)}, u32[]{:S(2)}) collective-permute-start(bf16[128,6144]{1,0:T(8,128)(2,1)S(1)} %add_convert_fusion.refs_11_.refs_8_), channel_id=1, source_target_pairs={{0,2},{1,3},{4,6},{5,7},{8,10},{9,11},{12,14},{13,15},{16,18},{17,... | collective-permute-start | bytes 4718600 | tf_op jit(solution)/shard_map/ppermute | solution.py:696
  159.2 9.1 %collective-permute-start.20 = (bf16[192,1024]{1,0:T(8,128)(2,1)S(1)}, bf16[192,1024]{1,0:T(8,128)(2,1)S(1)}, u32[]{:S(2)}, u32[]{:S(2)}) collective-permute-start(bf16[192,1024]{1,0:T(8,128)(2,1)S(1)} %get-tuple-element.54), channel_id=1, source_target_pairs={{0,32},{1,5},{4,36},{5,9},{8,40},{9,13},{12,44},{13,1},{32,64},{33... | collective-permute-start | bytes 1179656 | tf_op jit(solution)/shard_map/ppermute | solution.py:634
  160.4 7.9 %collective-permute-start.21 = (bf16[192,1024]{1,0:T(8,128)(2,1)S(1)}, bf16[192,1024]{1,0:T(8,128)(2,1)S(1)}, u32[]{:S(2)}, u32[]{:S(2)}) collective-permute-start(bf16[192,1024]{1,0:T(8,128)(2,1)S(1)} %get-tuple-element.56), channel_id=1, source_target_pairs={{0,96},{1,13},{4,100},{5,1},{8,104},{9,5},{12,108},{13,9},{32,0},{... | collective-permute-start | bytes 1179656 | tf_op jit(solution)/shard_map/ppermute | solution.py:634
  168.4 13.3 %collective-permute-start.22 = (bf16[384,1024]{1,0:T(8,128)(2,1)S(1)}, bf16[384,1024]{1,0:T(8,128)(2,1)S(1)}, u32[]{:S(2)}, u32[]{:S(2)}) collective-permute-start(bf16[384,1024]{1,0:T(8,128)(2,1)S(1)} %get-tuple-element.57), channel_id=1, source_target_pairs={{0,32},{1,5},{4,36},{5,9},{8,40},{9,13},{12,44},{13,1},{32,64},{33... | collective-permute-start | bytes 2359304 | tf_op jit(solution)/shard_map/ppermute | solution.py:634
  170.3 12.0 %collective-permute-start.23 = (bf16[384,1024]{1,0:T(8,128)(2,1)S(1)}, bf16[384,1024]{1,0:T(8,128)(2,1)S(1)}, u32[]{:S(2)}, u32[]{:S(2)}) collective-permute-start(bf16[384,1024]{1,0:T(8,128)(2,1)S(1)} %get-tuple-element.58), channel_id=1, source_target_pairs={{0,96},{1,13},{4,100},{5,1},{8,104},{9,5},{12,108},{13,9},{32,0},{... | collective-permute-start | bytes 2359304 | tf_op jit(solution)/shard_map/ppermute | solution.py:634
  172.2 10.9 %copy-start.8 = (bf16[128,6144]{1,0:T(8,128)(2,1)}, bf16[128,6144]{1,0:T(8,128)(2,1)S(1)}, u32[]{:S(2)}) copy-start(bf16[128,6144]{1,0:T(8,128)(2,1)S(1)} %collective-permute-done.25.refs_5_) | copy-start | bytes 4718596
  184.5 9.6 %collective-permute-start.26 = (bf16[192,1024]{1,0:T(8,128)(2,1)S(1)}, bf16[192,1024]{1,0:T(8,128)(2,1)S(1)}, u32[]{:S(2)}, u32[]{:S(2)}) collective-permute-start(bf16[192,1024]{1,0:T(8,128)(2,1)S(1)} %get-tuple-element.60), channel_id=1, source_target_pairs={{0,16},{16,0},{1,17},{17,1},{2,18},{18,2},{3,19},{19,3},{4,20},{20... | collective-permute-start | bytes 1179656 | tf_op jit(solution)/shard_map/ppermute | solution.py:710
  (11 other events, 26.2 us)
